TPU v7x, 512 devices: a whole 4x8x8 slice. The times are simulated.
512 devices in a mesh: bucket: 16 (over x_lo, y), edge: 32 (over x_hi, z, core).
Axes of the slice: x: 4 (x_hi: 2, x_lo: 2; x = x_hi * 2 + x_lo), y: 8, z: 8, core: 2. Of those that a mesh axis runs over, the one named last changes fastest.
Arguments:
- entity_block: float32 [4096, 400], P('bucket'), may hold values from -1.25 to 1.25
- block_state: float32 [4096], P('bucket'), may hold values from 50 to 5000
- hot_entities: float32 [512, 400], replicated, may hold values from -1.25 to 1.25
- hot_state: float32 [512], replicated, may hold values from 0.05 to 1
- relations: float32 [8192, 400], P('edge'), may hold values from -6 to 6
- relation_state: float32 [8192], P('edge'), may hold values from 4 to 400
- source_ids: int32 [16, 20480], P('bucket', 'edge'), may hold values from 0 to 767
- target_ids: int32 [16, 20480], P('bucket', 'edge'), may hold values from 0 to 767
- relation_ids: int32 [16, 20480], P('bucket', 'edge'), may hold values from 0 to 255
- negative_ids: int32 [16, 32, 1000], P('bucket', 'edge'), may hold values from 0 to 255
Outputs:
- new_block: float32 [4096, 400], P('bucket')
- new_block_state: float32 [4096], P('bucket')
- new_hot: float32 [512, 400], replicated
- new_hot_state: float32 [512], replicated
- new_relations: float32 [8192, 400], P('edge')
- new_relation_state: float32 [8192], P('edge')
Inputs may be any that keep to these rules, and one draw needn't show every extreme that they name: `source_ids`: ids below 256 name cold rows of a partition block, the others hot row id - 256. `target_ids`: ids below 256 name cold rows of the partner's block, the others hot row id - 256. `negative_ids`: rows of the partner's block.
All inputs are finite; a program needn't handle non-finite values.
Results may differ from a plain program's by a relative error of at most 0.0081.
Values may be sent and summed in bfloat16 or wider, within the bound.
No kernel may reach another device: no remote copies, remote signals or barrier semaphores. Data moves between devices by JAX's collectives and lax.ppermute only.
A program may use at most 64 MiB of HBM per device.

v0:
```python
import jax
import jax.numpy as jnp
from jax import lax
from jax.sharding import PartitionSpec as P

STEP = 0.3
EPS = 1e-06


def swapped(shard, axis, apart):
    return lax.ppermute(shard, axis, [(i, i ^ 1 << apart) for i in range(lax.axis_size(axis))])


def adagrad(weights, state_rows, grads):
    new_state = state_rows + jnp.mean(grads * grads, axis=-1)
    return (weights - STEP * grads / (jnp.sqrt(new_state)[:, None] + EPS), new_state)


def device_grads(
    own_table, partner_table, hot_table, kind_table, sources, targets, kinds, negatives
):
    rows = own_table.shape[0]
    hot_rows = hot_table.shape[0]
    width = own_table.shape[1]
    src_rows = jnp.concatenate([own_table, hot_table], axis=0)[sources]
    dst_rows = jnp.concatenate([partner_table, hot_table], axis=0)[targets]
    rel_rows = kind_table[kinds]
    queries = (src_rows.astype(jnp.float32) * rel_rows.astype(jnp.float32)).astype(jnp.bfloat16)
    positive = jnp.sum(queries.astype(jnp.float32) * dst_rows.astype(jnp.float32), axis=-1)
    pos_grad = -jax.nn.sigmoid(-positive)
    groups = negatives.shape[0]
    blocked = queries.reshape(groups, -1, width)
    neg_rows = partner_table[negatives]
    scores = jnp.einsum("cqd,cnd->cqn", blocked, neg_rows, preferred_element_type=jnp.float32)
    neg_grad = jax.nn.sigmoid(scores).astype(jnp.bfloat16)
    query_grad = pos_grad[:, None] * dst_rows.astype(jnp.float32) + jnp.einsum(
        "cqn,cnd->cqd", neg_grad, neg_rows, preferred_element_type=jnp.float32
    ).reshape(-1, width)
    row_grad = jnp.einsum("cqn,cqd->cnd", neg_grad, blocked, preferred_element_type=jnp.float32)
    src_grad = query_grad * rel_rows.astype(jnp.float32)
    kind_grad = query_grad * src_rows.astype(jnp.float32)
    dst_grad = pos_grad[:, None] * queries.astype(jnp.float32)
    src_sum = jax.ops.segment_sum(src_grad, sources, rows + hot_rows)
    dst_sum = jax.ops.segment_sum(dst_grad, targets, rows + hot_rows)
    neg_sum = jax.ops.segment_sum(row_grad.reshape(-1, width), negatives.reshape(-1), rows)
    kind_sum = jax.ops.segment_sum(kind_grad, kinds, kind_table.shape[0])
    return (src_sum[:rows], dst_sum[:rows] + neg_sum, src_sum[rows:] + dst_sum[rows:], kind_sum)


def local(
    entity_block,
    block_state,
    hot_entities,
    hot_state,
    relations,
    relation_state,
    source_ids,
    target_ids,
    relation_ids,
    negative_ids,
):
    own_table = entity_block.astype(jnp.bfloat16)
    swap_bit = lax.axis_size("bucket").bit_length() - 2
    partner_table = swapped(own_table, "bucket", swap_bit)
    own_grad, partner_grad, hot_grad, kind_grad = device_grads(
        own_table,
        partner_table,
        hot_entities.astype(jnp.bfloat16),
        relations.astype(jnp.bfloat16),
        source_ids[0],
        target_ids[0],
        relation_ids[0],
        negative_ids[0],
    )
    returned = swapped(partner_grad, "bucket", swap_bit)
    block_grad = own_grad + returned
    block_total = lax.psum(block_grad, "edge")
    new_block, new_block_state = adagrad(entity_block, block_state, block_total)
    hot_total = lax.psum(hot_grad, ("bucket", "edge"))
    new_hot, new_hot_state = adagrad(hot_entities, hot_state, hot_total)
    kind_total = lax.psum(kind_grad.astype(jnp.bfloat16), "bucket").astype(jnp.float32)
    new_relations, new_relation_state = adagrad(relations, relation_state, kind_total)
    return (new_block, new_block_state, new_hot, new_hot_state, new_relations, new_relation_state)


def solution(mesh):
    placed = (
        P("bucket", None),
        P("bucket"),
        P(),
        P(),
        P("edge", None),
        P("edge"),
        P("bucket", "edge"),
        P("bucket", "edge"),
        P("bucket", "edge"),
        P("bucket", "edge", None),
    )
    return jax.shard_map(
        local,
        mesh=mesh,
        in_specs=placed,
        out_specs=(P("bucket", None), P("bucket"), P(), P(), P("edge", None), P("edge")),
        check_vma=False,
    )
```

profile of v0, /device:TPU:1, one launch (start us, length us, event | category | flops | bytes accessed | tf_op | source)
XLA Modules:
  0.0 759.1 jit_solution(16987422687463379233)
XLA Ops:
  9.5 3.9 collective-permute-start
  16.0 2.8 gather_fusion.1
  20.4 3.3 gather_fusion
  25.1 3.3 gather_fusion.2
  30.7 5.1 gather_fusion.3
  35.8 2.5 divide_convert_fusion
  39.9 2.2 convert_multiply_fusion.5
  42.2 2.3 fusion.15
  44.5 1.5 copy.49
  46.0 8.0 %scatter_custom_fusion.3 = f32[256,400]{1,0:T(8,128)} fusion(s32[640]{0:T(1024)S(1)} %reduce.5, f32[640,400]{1,0:T(8,128)} %copy.49, f32[]{:T(128)} %constant.8.clone.1), kind=kCustom, calls=%fused_computation.35 | custom fusion | flops 256000 | bytes 410112 | tf_op jit(solution)/shard_map/scatter-add | solution.py:46
  54.0 1.9 convert_element_type.56
  56.1 1.5 copy.44
  57.6 1.5 copy.45
  59.1 7.6 %scatter_custom_fusion.1 = f32[768,400]{1,0:T(8,128)S(1)} fusion(s32[640]{0:T(1024)S(1)} %reduce.4, f32[640,400]{1,0:T(8,128)} %copy.45, f32[]{:T(128)} %constant.8.clone.1), kind=kCustom, calls=%fused_computation.23 | custom fusion | flops 256000 | bytes 1229312 | tf_op jit(solution)/shard_map/scatter-add | solution.py:44
  66.8 7.9 %scatter_fusion = f32[256,400]{1,0:T(8,128)S(1)} fusion(f32[256,400]{1,0:T(8,128)S(1)} %slice.25, s32[1000]{0:T(1024)S(1)} %bitcast.16, f32[1000,400]{1,0:T(8,128)} %fusion.15), kind=kCustom, calls=%fused_computation.6 | custom fusion | flops 400000 | bytes 4804000 | tf_op jit(solution)/shard_map/scatter-add | solution.py:45
  74.7 1.9 collective-permute-start.1
  76.6 7.6 %scatter_custom_fusion = f32[768,400]{1,0:T(8,128)S(1)} fusion(s32[640]{0:T(1024)S(1)} %reduce, f32[640,400]{1,0:T(8,128)} %copy.44, f32[]{:T(128)} %constant.8.clone.1), kind=kCustom, calls=%fused_computation.25 | custom fusion | flops 256000 | bytes 1229312 | tf_op jit(solution)/shard_map/scatter-add | solution.py:43
  84.2 2.4 slice_add_fusion
  86.7 104.6 %all-reduce.8.cloned.1.call-done = bf16[256,400]{1,0:T(8,128)(2,1)} async-done(((bf16[256,400]{1,0:T(8,128)(2,1)}), bf16[256,400]{1,0:T(8,128)(2,1)}) %all-reduce.8.cloned.1.call-update) | async-done | bytes 204816 | tf_op jit(solution)/shard_map/psum | solution.py:81
  193.0 2.0 fusion.7
  195.0 2.0 copy.53
  197.0 279.6 %all-reduce.6.cloned.1.call-done = f32[512,400]{1,0:T(8,128)} async-done(((f32[512,400]{1,0:T(8,128)}), f32[512,400]{1,0:T(8,128)}) %all-reduce.6.cloned.1.call-update) | async-done | bytes 819216 | tf_op jit(solution)/shard_map/psum | solution.py:79
  477.9 1.9 slice_add_fusion.1
  483.1 264.7 %all-reduce.4.cloned.1.call-done = f32[256,400]{1,0:T(8,128)} async-done(((f32[256,400]{1,0:T(8,128)}), f32[256,400]{1,0:T(8,128)}) %all-reduce.4.cloned.1.call-update) | async-done | bytes 409616 | tf_op jit(solution)/shard_map/psum | solution.py:77
  (80 shorter events, 21.2 us)
Async XLA Ops:
  8.0 5.4 copy-start.8
  8.0 6.5 copy-start.13
  8.0 6.5 copy-start.12
  8.0 6.5 copy-start.14
  8.0 6.6 copy-start.10
  8.1 183.3 %all-reduce.8.cloned.1.call-start = ((), (), s32[]{:S(2)}) async-start(), calls=%async_computation.2 | async-start | bytes 524288 | tf_op jit(solution)/shard_map/psum | solution.py:81
  9.4 5.2 copy-start.1
  9.4 5.5 copy-start.9
  9.5 9.7 %collective-permute-start = (bf16[256,400]{1,0:T(8,128)(2,1)S(1)}, bf16[256,400]{1,0:T(8,128)(2,1)S(1)}, u32[]{:S(2)}, u32[]{:S(2)}) collective-permute-start(bf16[256,400]{1,0:T(8,128)(2,1)S(1)} %convert_element_type.47), channel_id=1, source_target_pairs={{0,256},{32,288},{64,320},{96,352},{128,384},{160,416},{192,448},{... | collective-permute-start | bytes 614408 | tf_op jit(solution)/shard_map/ppermute | solution.py:11
  16.0 3.1 copy-start.11
  35.8 2.5 copy-start.7
  38.3 1.6 copy-start.4
  42.2 2.3 copy-start.6
  44.5 11.6 %copy-start.5 = (f32[640,400]{0,1:T(8,128)S(1)}, f32[640,400]{0,1:T(8,128)}, u32[]{:S(2)}) copy-start(f32[640,400]{0,1:T(8,128)} %get-tuple-element.27) | copy-start | bytes 3072004
  54.0 3.6 copy-start.3
  55.9 420.7 %all-reduce.6.cloned.1.call-start = ((), (), s32[]{:S(2)}) async-start(), calls=%async_computation.1 | async-start | bytes 2097152 | tf_op jit(solution)/shard_map/psum | solution.py:79
  66.7 7.9 %copy-start = (f32[768,400]{1,0:T(8,128)}, f32[768,400]{1,0:T(8,128)S(1)}, u32[]{:S(2)}) copy-start(f32[768,400]{1,0:T(8,128)S(1)} %scatter_custom_fusion.1) | copy-start | bytes 3686404
  74.7 403.3 %collective-permute-start.1 = (f32[256,400]{1,0:T(8,128)S(1)}, f32[256,400]{1,0:T(8,128)}, u32[]{:S(2)}, u32[]{:S(2)}) collective-permute-start(f32[256,400]{1,0:T(8,128)S(1)} %scatter_fusion), channel_id=1, source_target_pairs={{0,256},{32,288},{64,320},{96,352},{128,384},{160,416},{192,448},{... | collective-permute-start | bytes 1228808 | tf_op jit(solution)/shard_map/ppermute | solution.py:11
  84.2 108.2 %copy-start.16 = (f32[256]{0:T(256)S(1)}, f32[256]{0:T(256)}, u32[]{:S(2)}) copy-start(f32[256]{0:T(256)} %param.15) | copy-start | bytes 3076
  86.7 661.2 %all-reduce.4.cloned.1.call-start = ((), (), s32[]{:S(2)}) async-start(), calls=%async_computation | async-start | bytes 1048576 | tf_op jit(solution)/shard_map/psum | solution.py:77
  197.0 282.9 %copy-start.15 = (f32[512]{0:T(512)S(1)}, f32[512]{0:T(512)}, u32[]{:S(2)}) copy-start(f32[512]{0:T(512)} %param.13) | copy-start | bytes 6148
  481.9 267.1 %copy-start.17 = (f32[256]{0:T(256)S(1)}, f32[256]{0:T(256)}, u32[]{:S(2)}) copy-start(f32[256]{0:T(256)} %param.11) | copy-start | bytes 3076
  481.9 267.6 %copy-start.2 = (f32[256,400]{1,0:T(8,128)S(1)}, f32[256,400]{1,0:T(8,128)}, u32[]{:S(2)}) copy-start(f32[256,400]{1,0:T(8,128)} %copy-done.1) | copy-start | bytes 1228804
Sparse Core Ops, SparseCore 0:
  56.0 135.2 all-reduce.7
  196.4 280.0 all-reduce.5
Sparse Core Ops, SparseCore 1:
  480.0 267.8 all-reduce.3
where the time goes:
time: 760 us; the launch traced here: 759 us
  waiting for transfers between devices  649 us (85%)
  other arithmetic  51.7 us (7%)
  local copies, waits for them, and re-layouts  29.3 us (4%)
  between operations  15.9 us (2%)
    psum x1, waiting for transfers between devices, local(): hot_total = lax.psum(hot_grad, ('bucket', 'edge'))  280 us
    psum x1, waiting for transfers between devices, local(): block_total = lax.psum(block_grad, 'edge')  265 us
    psum x1, waiting for transfers between devices, local(): lax.psum(kind_grad.astype(jnp.bfloat16), 'bucket').astype(jnp.float32)  105 us
  transfers between devices with their start and end apart: 5, of which 3 were waited for; matrix products, arithmetic and copies ran while one was open for 6% of the time, Pallas kernels for 0%

commit v1 on v0

v1 whole, which is shorter than its diff:
```python
import jax
import jax.numpy as jnp
from jax import lax
from jax.experimental import pallas as pl
from jax.experimental.pallas import tpu as pltpu
from jax.sharding import PartitionSpec as P

STEP = 0.3
EPS = 1e-06
F32 = jnp.float32
BF16 = jnp.bfloat16
PEERS = 16
VMEM = pl.BlockSpec(memory_space=pltpu.VMEM)


def call(body, outs, args, flops=1 << 22):
    moved = sum(a.size * a.dtype.itemsize for a in args)
    return pl.pallas_call(
        body,
        out_shape=[jax.ShapeDtypeStruct(shape, dtype) for shape, dtype in outs],
        in_specs=[VMEM] * len(args),
        out_specs=[VMEM] * len(outs),
        compiler_params=pltpu.CompilerParams(vmem_limit_bytes=40 << 20),
        cost_estimate=pl.CostEstimate(flops=flops, bytes_accessed=moved, transcendentals=0),
    )(*args)


def one_hot(ids, rows):
    grid = lax.broadcasted_iota(jnp.int32, (rows, ids.shape[1]), 0)
    return jnp.where(grid == ids, 1.0, 0.0).astype(BF16)


def mm(a, b):
    return lax.dot_general(a, b, (((1,), (0,)), ((), ())), preferred_element_type=F32)


def mm_t(a, b):
    return lax.dot_general(a, b, (((1,), (1,)), ((), ())), preferred_element_type=F32)


def core_of():
    return lax.axis_index("edge") & 1


def gather_kernel(own, hot, rel, src_ids, dst_ids, rel_ids, src_out, rel_out, dst_out):
    rows = own.shape[1]
    hot_rows = hot.shape[1]
    hot_bf = hot[...].astype(BF16)
    src_hot = one_hot(src_ids[...] - rows, hot_rows)
    src_own = one_hot(src_ids[...], rows)
    src_out[...] = (mm(own[...], src_own) + mm(hot_bf, src_hot)).astype(BF16)
    rel_out[...] = mm(rel[...].astype(BF16), one_hot(rel_ids[...], rel.shape[1])).astype(BF16)
    dst_out[...] = mm(hot_bf, one_hot(dst_ids[...] - rows, hot_rows)).astype(BF16)


def grad_kernel(
    partner, src, rel, dst_hot, src_ids, dst_ids, rel_ids, neg_ids, keep, send, kind
):
    width, rows = partner.shape
    hot_rows = 2 * rows
    core = core_of()
    src_f = src[...].astype(F32)
    rel_f = rel[...].astype(F32)
    query = (src_f * rel_f).astype(BF16)
    query_f = query.astype(F32)
    dst_own = one_hot(dst_ids[...], rows)
    dst = mm(partner[...], dst_own) + dst_hot[...].astype(F32)
    positive = jnp.sum(query_f * dst, axis=0, keepdims=True)
    pos_grad = -1.0 / (1.0 + jnp.exp(positive))
    scores = mm(partner[...].T, query)
    sig = (1.0 / (1.0 + jnp.exp(-scores))).astype(BF16)
    named = one_hot(neg_ids[...], rows)
    count = mm_t(jnp.ones((8, neg_ids.shape[1]), BF16), named)[:1, :]
    scaled = partner[...].astype(F32) * count
    high = scaled.astype(BF16)
    low = (scaled - high.astype(F32)).astype(BF16)
    query_grad = pos_grad * dst + mm(high, sig) + mm(low, sig)
    row_grad = mm_t(query, sig) * count
    src_grad = (query_grad * rel_f).astype(BF16)
    kind_grad = (query_grad * src_f).astype(BF16)
    dst_grad = (pos_grad * query_f).astype(BF16)
    kind[:width, :] = mm_t(kind_grad, one_hot(rel_ids[...], kind.shape[1])).astype(BF16)
    kind[width:, :] = jnp.zeros((kind.shape[0] - width, kind.shape[1]), BF16)
    half = rows // 2
    src_at = src_ids[...]
    dst_at = dst_ids[...]
    own_flip = core * half
    hot_flip = core * rows
    own_src = mm_t(src_grad, one_hot(jnp.where(src_at < rows, src_at ^ own_flip, -1), rows))
    hot_sum = mm_t(
        src_grad, one_hot(jnp.where(src_at < rows, -1, (src_at - rows) ^ hot_flip), hot_rows)
    ) + mm_t(dst_grad, one_hot(jnp.where(dst_at < rows, -1, (dst_at - rows) ^ hot_flip), hot_rows))
    partner_dst = mm_t(dst_grad, one_hot(jnp.where(dst_at < rows, dst_at ^ own_flip, -1), rows))
    first = core == 0
    neg_keep = jnp.where(first, row_grad[:, :half], row_grad[:, half:])
    neg_send = jnp.where(first, row_grad[:, half:], row_grad[:, :half])
    keep[:, :half] = own_src[:, :half]
    keep[:, half : 2 * half] = partner_dst[:, :half] + neg_keep
    keep[:, 2 * half :] = hot_sum[:, :rows]
    send[:, :half] = own_src[:, half:].astype(BF16)
    send[:, half : 2 * half] = (partner_dst[:, half:] + neg_send).astype(BF16)
    send[:, 2 * half :] = hot_sum[:, rows:].astype(BF16)


def add_kernel(keep, got, out):
    width = keep.shape[0]
    out[:width, :] = (keep[...] + got[...].astype(F32)).astype(BF16)
    out[width:, :] = jnp.zeros((out.shape[0] - width, out.shape[1]), BF16)


def chunk_sum(ref, lanes):
    rows = ref.shape[0] // PEERS
    total = ref[:rows, lanes].astype(F32)
    for peer in range(1, PEERS):
        total = total + ref[peer * rows : (peer + 1) * rows, lanes].astype(F32)
    return total


def bucket_kernel(got, kind, out, own, partner):
    rows = got.shape[0] // PEERS
    lanes = kind.shape[1]
    half = lanes // 2
    own[...] = chunk_sum(got, slice(0, half))
    partner[...] = chunk_sum(got, slice(half, lanes))
    hot = chunk_sum(got, slice(lanes, 2 * lanes)).astype(BF16)
    out[:, :lanes] = kind[...]
    for peer in range(PEERS):
        out[peer * rows : (peer + 1) * rows, lanes:] = hot


def spread_kernel(got, own, partner, out, kind):
    rows = got.shape[0] // PEERS
    lanes = got.shape[1] // 2
    half = own.shape[1]
    kind_sum = chunk_sum(got, slice(0, lanes)).astype(BF16)
    hot_sum = chunk_sum(got, slice(lanes, 2 * lanes)).astype(BF16)
    own_sum = (own[...] + partner[...]).astype(BF16)
    for peer in range(PEERS):
        at = slice(peer * rows, (peer + 1) * rows)
        out[at, :half] = own_sum
        out[at, half:] = hot_sum
        kind[at, :] = kind_sum


def adagrad(weights, state, grads, new_weights, new_state, at):
    total = state[:, at] + jnp.sum(grads * grads, axis=0, keepdims=True) / grads.shape[0]
    new_state[:, at] = total
    new_weights[:, at] = weights[:, at] - grads * (STEP / (jnp.sqrt(total) + EPS))


def entity_kernel(mine, other, block, block_state, hot, hot_state, new_b, new_bs, new_h, new_hs):
    width, rows = block.shape
    half = rows // 2
    first = core_of() == 0
    for part in range(2):
        low = jnp.where(first, part == 0, part == 1)
        grads = jnp.where(low, mine[:width, :], other[:width, :]).astype(F32)
        adagrad(block, block_state, grads[:, :half], new_b, new_bs, slice(part * half, (part + 1) * half))
        adagrad(hot, hot_state, grads[:, half:], new_h, new_hs, slice(part * rows, (part + 1) * rows))


def relation_kernel(grads, weights, state, new_weights, new_state):
    width, rows = weights.shape
    adagrad(weights, state, grads[:width, :].astype(F32), new_weights, new_state, slice(0, rows))


def flipped(x, axis, bit):
    return lax.ppermute(x, axis, [(i, i ^ bit) for i in range(lax.axis_size(axis))])


def exchanged(x, axis, groups=None):
    return lax.all_to_all(x, axis, 0, 0, tiled=True, axis_index_groups=groups)


def local(
    entity_block,
    block_state,
    hot_entities,
    hot_state,
    relations,
    relation_state,
    source_ids,
    target_ids,
    relation_ids,
    negative_ids,
):
    rows, width = entity_block.shape
    hot_rows = hot_entities.shape[0]
    edges = source_ids.shape[1]
    padded = -(-width // 256) * 256
    slot = padded // PEERS
    half = rows // 2
    block_t, hot_t, rel_t = entity_block.T, hot_entities.T, relations.T
    negatives = negative_ids.reshape(1, -1)
    own_bf = block_t.astype(BF16)
    swap = lax.axis_size("bucket") // 2
    partner = flipped(own_bf, "bucket", swap)
    src, rel, dst_hot = call(
        gather_kernel,
        [((width, edges), BF16)] * 3,
        (own_bf, hot_t, rel_t, source_ids, target_ids, relation_ids),
        1 << 30,
    )
    keep, send, kind = call(
        grad_kernel,
        [((width, 2 * rows), F32), ((width, 2 * rows), BF16), ((padded, rows), BF16)],
        (partner, src, rel, dst_hot, source_ids, target_ids, relation_ids, negatives),
        1 << 31,
    )
    pairs = [[2 * i + core for i in range(PEERS)] for core in range(2)]
    (mixed,) = call(add_kernel, [((padded, 2 * rows), BF16)], (keep, flipped(send, "edge", 1)))
    mixed = exchanged(mixed, "edge", pairs)
    to_bucket, own_part, partner_part = call(
        bucket_kernel,
        [((padded, 2 * rows), BF16), ((slot, half), F32), ((slot, half), F32)],
        (mixed, kind),
    )
    returned = flipped(partner_part, "bucket", swap)
    from_bucket = exchanged(to_bucket, "bucket")
    entity_part, kind_part = call(
        spread_kernel,
        [((padded, half + rows), BF16), ((padded, rows), BF16)],
        (from_bucket, own_part, returned),
    )
    mine = exchanged(entity_part, "edge", pairs)
    mine, kind_part = lax.optimization_barrier((mine, kind_part))
    other = flipped(mine, "edge", 1)
    kind_grads = exchanged(kind_part, "bucket")
    new_block, new_block_state, new_hot, new_hot_state = call(
        entity_kernel,
        [((width, rows), F32), ((1, rows), F32), ((width, hot_rows), F32), ((1, hot_rows), F32)],
        (mine, other, block_t, block_state.reshape(1, -1), hot_t, hot_state.reshape(1, -1)),
    )
    new_relations, new_relation_state = call(
        relation_kernel,
        [((width, rows), F32), ((1, rows), F32)],
        (kind_grads, rel_t, relation_state.reshape(1, -1)),
    )
    return (
        new_block.T,
        new_block_state.reshape(-1),
        new_hot.T,
        new_hot_state.reshape(-1),
        new_relations.T,
        new_relation_state.reshape(-1),
    )


def solution(mesh):
    placed = (
        P("bucket", None),
        P("bucket"),
        P(),
        P(),
        P("edge", None),
        P("edge"),
        P("bucket", "edge"),
        P("bucket", "edge"),
        P("bucket", "edge"),
        P("bucket", "edge", None),
    )
    return jax.shard_map(
        local,
        mesh=mesh,
        in_specs=placed,
        out_specs=(P("bucket", None), P("bucket"), P(), P(), P("edge", None), P("edge")),
        check_vma=False,
    )
```

time: 760 us -> 106 us (0.14)
  the two profiles are of different devices: /device:TPU:1 before, /device:TPU:8 now
where the time goes in v1:
time: 106 us
  blocking collectives  50.4 us (48%)
  starting transfers between devices  23.5 us (22%)
  waiting for transfers between devices  19.4 us (18%)
  Pallas kernels  7.87 us (7%)
  local copies, waits for them, and re-layouts  2.54 us (2%)
  other arithmetic  1.07 us (1%)
    all_to_all x2, blocking collectives, exchanged(): return lax.all_to_all(x, axis, 0, 0, tiled=True, axis_index_groups=groups)  50.4 us
    all_to_all x2, starting transfers between devices, exchanged(): return lax.all_to_all(x, axis, 0, 0, tiled=True, axis_index_groups=groups)  12.9 us
    all_to_all x2, waiting for transfers between devices, exchanged(): return lax.all_to_all(x, axis, 0, 0, tiled=True, axis_index_groups=groups)  10.8 us
    ppermute x4, starting transfers between devices, flipped(): lax.ppermute(x, axis, [(i, i ^ bit) for i in range(lax.axis_size(axis))])  10.6 us
    ppermute x4, waiting for transfers between devices, flipped(): lax.ppermute(x, axis, [(i, i ^ bit) for i in range(lax.axis_size(axis))])  8.6 us
    pallas_call x7, Pallas kernels, call(): pl.pallas_call(body, out_shape=[jax.ShapeDtypeStruct(shape, dtype) for sh...  7.87 us
    unnamed x22, local copies, waits for them, and re-layouts  2.54 us
  transfers between devices with their start and end apart: 6, of which 6 were waited for; matrix products, arithmetic and copies ran while one was open for 0% of the time, Pallas kernels for 2%

profile of v1, /device:TPU:8, one launch (start us, length us, event | category | flops | bytes accessed | tf_op | source)
XLA Modules:
  0.0 105.5 jit_solution(18015823360930337680)
XLA Ops:
  0.7 1.1 %bitcast_convert_fusion.own = bf16[400,256]{1,0:T(8,128)(2,1)S(1)} fusion(f32[256,400]{0,1:T(8,128)} %param.10), kind=kLoop, calls=%fused_computation | loop fusion | flops 102400 | bytes 614400 | tf_op jit(solution)/shard_map/convert_element_type | solution.py:195
  1.7 3.4 %collective-permute-start = (bf16[400,256]{1,0:T(8,128)(2,1)S(1)}, bf16[400,256]{1,0:T(8,128)(2,1)S(1)}, u32[]{:S(2)}, u32[]{:S(2)}) collective-permute-start(bf16[400,256]{1,0:T(8,128)(2,1)S(1)} %bitcast_convert_fusion.own), channel_id=1, source_target_pairs={{0,256},{32,288},{64,320},{96,352},{128,384},{160,416},{192,448},{... | collective-permute-start | bytes 614408 | tf_op jit(solution)/shard_map/ppermute | solution.py:168
  5.2 1.1 %copy-done.1 = f32[512,400]{0,1:T(8,128)S(1)} copy-done((f32[512,400]{0,1:T(8,128)S(1)}, f32[512,400]{0,1:T(8,128)}, u32[]{:S(2)}) %copy-start.1) | copy-done | bytes 819224
  6.3 1.1 %shard_map.145 = (bf16[400,640]{1,0:T(8,128)(2,1)S(1)}, bf16[400,640]{1,0:T(8,128)(2,1)S(1)}, bf16[400,640]{1,0:T(8,128)(2,1)S(1)}) custom-call(bf16[400,256]{1,0:T(8,128)(2,1)S(1)} %bitcast_convert_fusion.own, f32[400,512]{1,0:T(8,128)S(1)} %bitcast.29, f32[400,256]{1,0:T(8,128)S(1)} %bitcast.31, s32[1,640]{1,0:T(1,128)S(1)} %copy-done.8, ...), custom_call_target="tpu_custom_call" | custom-call | flops 1073741824 | bytes 1441280 | tf_op jit(solution)/shard_map/pallas_call | solution.py:18
  7.5 2.9 %collective-permute-done.partner = bf16[400,256]{1,0:T(8,128)(2,1)S(1)} collective-permute-done((bf16[400,256]{1,0:T(8,128)(2,1)S(1)}, bf16[400,256]{1,0:T(8,128)(2,1)S(1)}, u32[]{:S(2)}, u32[]{:S(2)}) %collective-permute-start) | collective-permute-done | bytes 204832 | tf_op jit(solution)/shard_map/ppermute | solution.py:168
  10.5 2.8 %shard_map.146 = (f32[400,512]{1,0:T(8,128)S(1)}, bf16[400,512]{1,0:T(8,128)(2,1)S(1)}, bf16[512,256]{1,0:T(8,128)(2,1)S(1)}) custom-call(bf16[400,256]{1,0:T(8,128)(2,1)S(1)} %collective-permute-done.partner, bf16[400,640]{1,0:T(8,128)(2,1)S(1)} %get-tuple-element.25.src, bf16[400,640]{1,0:T(8,128)(2,1)S(1)} %get-tuple-element.26.rel, ...), custom_call_target="tpu_custom_call" | custom-call | flops 2147483648 | bytes 1752480 | tf_op jit(solution)/shard_map/pallas_call | solution.py:18
  13.3 1.9 %collective-permute-start.1 = (bf16[400,512]{1,0:T(8,128)(2,1)S(1)}, bf16[400,512]{1,0:T(8,128)(2,1)S(1)}, u32[]{:S(2)}, u32[]{:S(2)}) collective-permute-start(bf16[400,512]{1,0:T(8,128)(2,1)S(1)} %get-tuple-element.29), channel_id=1, source_target_pairs={{0,1},{1,0},{2,3},{3,2},{4,5},{5,4},{6,7},{7,6},{8,9},{9,8},{10,11... | collective-permute-start | bytes 1228808 | tf_op jit(solution)/shard_map/ppermute | solution.py:168
  15.2 1.7 %collective-permute-done.1.got = bf16[400,512]{1,0:T(8,128)(2,1)S(1)} collective-permute-done((bf16[400,512]{1,0:T(8,128)(2,1)S(1)}, bf16[400,512]{1,0:T(8,128)(2,1)S(1)}, u32[]{:S(2)}, u32[]{:S(2)}) %collective-permute-start.1) | collective-permute-done | bytes 409632 | tf_op jit(solution)/shard_map/ppermute | solution.py:168
  17.0 29.9 %all_to_all.45 = bf16[16,32,512]{2,1,0:T(8,128)(2,1)S(1)} all-to-all(bf16[16,32,512]{2,1,0:T(8,128)(2,1)S(1)} %bitcast.24), channel_id=1, replica_groups={{0,2,4,6,8,10,12,14,16,18,20,22,24,26,28,30},{1,3,5,7,9,11,13,15,17,19,..., dimensions={0} | all-to-all | bytes 1048576 | tf_op jit(solution)/shard_map/all_to_all | solution.py:172
  47.0 0.9 shard_map.148
  47.8 7.6 %all-to-all-start.1 = ((bf16[16,32,512]{2,1,0:T(8,128)(2,1)}), bf16[16,32,512]{2,1,0:T(8,128)(2,1)S(1)}, u32[]{:S(2)}, u32[]{:S(2)}) async-start(bf16[16,32,512]{2,1,0:T(8,128)(2,1)} %bitcast.6), calls=%async_computation.1 | async-start | bytes 1048576 | tf_op jit(solution)/shard_map/all_to_all | solution.py:172
  55.4 3.4 %collective-permute-start.2 = (f32[32,128]{1,0:T(8,128)S(1)}, f32[32,128]{1,0:T(8,128)S(1)}, u32[]{:S(2)}, u32[]{:S(2)}) collective-permute-start(f32[32,128]{1,0:T(8,128)S(1)} %get-tuple-element.33), channel_id=1, source_target_pairs={{0,256},{32,288},{64,320},{96,352},{128,384},{160,416},{192,448},{... | collective-permute-start | bytes 49160 | tf_op jit(solution)/shard_map/ppermute | solution.py:168
  58.8 2.2 %collective-permute-done.2.partner = f32[32,128]{1,0:T(8,128)S(1)} collective-permute-done((f32[32,128]{1,0:T(8,128)S(1)}, f32[32,128]{1,0:T(8,128)S(1)}, u32[]{:S(2)}, u32[]{:S(2)}) %collective-permute-start.2) | collective-permute-done | bytes 16416 | tf_op jit(solution)/shard_map/ppermute | solution.py:168
  61.0 7.4 %all-to-all-done.1 = bf16[16,32,512]{2,1,0:T(8,128)(2,1)S(1)} async-done(((bf16[16,32,512]{2,1,0:T(8,128)(2,1)}), bf16[16,32,512]{2,1,0:T(8,128)(2,1)S(1)}, u32[]{:S(2)}, u32[]{:S(2)}) %all-to-all-start.1) | async-done | bytes 524320 | tf_op jit(solution)/shard_map/all_to_all | solution.py:172
  68.4 0.8 shard_map.149
  69.2 20.5 %all_to_all.46 = bf16[16,32,384]{2,1,0:T(8,128)(2,1)S(1)} all-to-all(bf16[16,32,384]{2,1,0:T(8,128)(2,1)S(1)} %bitcast.33), channel_id=1, replica_groups={{0,2,4,6,8,10,12,14,16,18,20,22,24,26,28,30},{1,3,5,7,9,11,13,15,17,19,..., dimensions={0} | all-to-all | bytes 786432 | tf_op jit(solution)/shard_map/all_to_all | solution.py:172
  89.6 5.3 %all-to-all-start.3 = ((bf16[16,32,256]{2,1,0:T(8,128)(2,1)}), bf16[16,32,256]{2,1,0:T(8,128)(2,1)S(1)}, u32[]{:S(2)}, u32[]{:S(2)}) async-start(bf16[16,32,256]{2,1,0:T(8,128)(2,1)} %bitcast.16), calls=%async_computation.3 | async-start | bytes 524288 | tf_op jit(solution)/shard_map/all_to_all | solution.py:172
  94.9 1.9 %collective-permute-start.3 = (bf16[512,384]{1,0:T(8,128)(2,1)S(1)}, bf16[512,384]{1,0:T(8,128)(2,1)S(1)}, u32[]{:S(2)}, u32[]{:S(2)}) collective-permute-start(bf16[512,384]{1,0:T(8,128)(2,1)S(1)} %bitcast.26), channel_id=1, source_target_pairs={{0,1},{1,0},{2,3},{3,2},{4,5},{5,4},{6,7},{7,6},{8,9},{9,8},{10,11... | collective-permute-start | bytes 1179656 | tf_op jit(solution)/shard_map/ppermute | solution.py:168
  96.8 1.7 %collective-permute-done.3.other = bf16[512,384]{1,0:T(8,128)(2,1)S(1)} collective-permute-done((bf16[512,384]{1,0:T(8,128)(2,1)S(1)}, bf16[512,384]{1,0:T(8,128)(2,1)S(1)}, u32[]{:S(2)}, u32[]{:S(2)}) %collective-permute-start.3) | collective-permute-done | bytes 393248 | tf_op jit(solution)/shard_map/ppermute | solution.py:168
  98.5 0.7 copy-done.4
  99.2 1.3 %shard_map.150 = (f32[400,256]{1,0:T(8,128)}, f32[1,256]{1,0:T(1,128)}, f32[400,512]{1,0:T(8,128)}, f32[1,512]{1,0:T(1,128)}) custom-call(bf16[512,384]{1,0:T(8,128)(2,1)S(1)} %bitcast.27, bf16[512,384]{1,0:T(8,128)(2,1)S(1)} %collective-permute-done.3.other, f32[400,256]{1,0:T(8,128)S(1)} %bitcast.25, f32[1,256]{1,0:T(1,128)S(1)} %bitcast.35, ...), custom_call_target="tpu_custom_call" | custom-call | flops 4194304 | bytes 2018304 | tf_op jit(solution)/shard_map/pallas_call | solution.py:18
  100.5 3.5 %all-to-all-done.3 = bf16[16,32,256]{2,1,0:T(8,128)(2,1)S(1)} async-done(((bf16[16,32,256]{2,1,0:T(8,128)(2,1)}), bf16[16,32,256]{2,1,0:T(8,128)(2,1)S(1)}, u32[]{:S(2)}, u32[]{:S(2)}) %all-to-all-start.3) | async-done | bytes 262176 | tf_op jit(solution)/shard_map/all_to_all | solution.py:172
  104.0 0.7 copy-done.6
  104.6 0.9 shard_map.151
  (20 shorter events, 0.1 us)
Async XLA Ops:
  0.6 4.5 %copy-start.3 = (f32[256,400]{0,1:T(8,128)S(1)}, f32[256,400]{0,1:T(8,128)}, u32[]{:S(2)}) copy-start(f32[256,400]{0,1:T(8,128)} %param.14) | copy-start | bytes 1228804
  0.6 4.5 %copy-start.9 = (s32[1,640]{1,0:T(1,128)S(1)}, s32[1,640]{1,0:T(1,128)}, u32[]{:S(2)}) copy-start(s32[1,640]{1,0:T(1,128)} %dst_ids.3) | copy-start | bytes 7684
  0.7 4.5 %copy-start.10 = (s32[1,640]{1,0:T(1,128)S(1)}, s32[1,640]{1,0:T(1,128)}, u32[]{:S(2)}) copy-start(s32[1,640]{1,0:T(1,128)} %rel_ids.3) | copy-start | bytes 7684
  1.7 3.5 %copy-start.8 = (s32[1,640]{1,0:T(1,128)S(1)}, s32[1,640]{1,0:T(1,128)}, u32[]{:S(2)}) copy-start(s32[1,640]{1,0:T(1,128)} %src_ids.3) | copy-start | bytes 7684
  1.7 8.7 %collective-permute-start = (bf16[400,256]{1,0:T(8,128)(2,1)S(1)}, bf16[400,256]{1,0:T(8,128)(2,1)S(1)}, u32[]{:S(2)}, u32[]{:S(2)}) collective-permute-start(bf16[400,256]{1,0:T(8,128)(2,1)S(1)} %bitcast_convert_fusion.own), channel_id=1, source_target_pairs={{0,256},{32,288},{64,320},{96,352},{128,384},{160,416},{192,448},{... | collective-permute-start | bytes 614408 | tf_op jit(solution)/shard_map/ppermute | solution.py:168
  5.2 1.1 %copy-start.1 = (f32[512,400]{0,1:T(8,128)S(1)}, f32[512,400]{0,1:T(8,128)}, u32[]{:S(2)}) copy-start(f32[512,400]{0,1:T(8,128)} %param.12) | copy-start | bytes 2457604
  7.5 3.0 %copy-start.7 = (s32[1,1,1000]{2,1,0:T(1,128)S(1)}, s32[1,1,1000]{2,1,0:T(1,128)}, u32[]{:S(2)}) copy-start(s32[1,1,1000]{2,1,0:T(1,128)} %param.19) | copy-start | bytes 12004
  13.3 3.6 %collective-permute-start.1 = (bf16[400,512]{1,0:T(8,128)(2,1)S(1)}, bf16[400,512]{1,0:T(8,128)(2,1)S(1)}, u32[]{:S(2)}, u32[]{:S(2)}) collective-permute-start(bf16[400,512]{1,0:T(8,128)(2,1)S(1)} %get-tuple-element.29), channel_id=1, source_target_pairs={{0,1},{1,0},{2,3},{3,2},{4,5},{5,4},{6,7},{7,6},{8,9},{9,8},{10,11... | collective-permute-start | bytes 1228808 | tf_op jit(solution)/shard_map/ppermute | solution.py:168
  47.8 20.6 %all-to-all-start.1 = ((bf16[16,32,512]{2,1,0:T(8,128)(2,1)}), bf16[16,32,512]{2,1,0:T(8,128)(2,1)S(1)}, u32[]{:S(2)}, u32[]{:S(2)}) async-start(bf16[16,32,512]{2,1,0:T(8,128)(2,1)} %bitcast.6), calls=%async_computation.1 | async-start | bytes 1048576 | tf_op jit(solution)/shard_map/all_to_all | solution.py:172
  55.4 5.6 %collective-permute-start.2 = (f32[32,128]{1,0:T(8,128)S(1)}, f32[32,128]{1,0:T(8,128)S(1)}, u32[]{:S(2)}, u32[]{:S(2)}) collective-permute-start(f32[32,128]{1,0:T(8,128)S(1)} %get-tuple-element.33), channel_id=1, source_target_pairs={{0,256},{32,288},{64,320},{96,352},{128,384},{160,416},{192,448},{... | collective-permute-start | bytes 49160 | tf_op jit(solution)/shard_map/ppermute | solution.py:168
  68.4 30.1 %copy-start.2 = (f32[512,400]{0,1:T(8,128)S(1)}, f32[512,400]{0,1:T(8,128)}, u32[]{:S(2)}) copy-start(f32[512,400]{0,1:T(8,128)} %param.12) | copy-start | bytes 2457604
  89.6 8.9 %copy-start = (f32[256,400]{0,1:T(8,128)S(1)}, f32[256,400]{0,1:T(8,128)}, u32[]{:S(2)}) copy-start(f32[256,400]{0,1:T(8,128)} %param.10) | copy-start | bytes 1228804
  89.6 14.3 %all-to-all-start.3 = ((bf16[16,32,256]{2,1,0:T(8,128)(2,1)}), bf16[16,32,256]{2,1,0:T(8,128)(2,1)S(1)}, u32[]{:S(2)}, u32[]{:S(2)}) async-start(bf16[16,32,256]{2,1,0:T(8,128)(2,1)} %bitcast.16), calls=%async_computation.3 | async-start | bytes 524288 | tf_op jit(solution)/shard_map/all_to_all | solution.py:172
  94.9 3.6 %collective-permute-start.3 = (bf16[512,384]{1,0:T(8,128)(2,1)S(1)}, bf16[512,384]{1,0:T(8,128)(2,1)S(1)}, u32[]{:S(2)}, u32[]{:S(2)}) collective-permute-start(bf16[512,384]{1,0:T(8,128)(2,1)S(1)} %bitcast.26), channel_id=1, source_target_pairs={{0,1},{1,0},{2,3},{3,2},{4,5},{5,4},{6,7},{7,6},{8,9},{9,8},{10,11... | collective-permute-start | bytes 1179656 | tf_op jit(solution)/shard_map/ppermute | solution.py:168
  98.5 0.7 copy-start.4
  98.5 0.7 copy-start.5
  104.0 0.7 copy-start.6

commit v2 on v1

v2 whole, which is shorter than its diff:
```python
import jax
import jax.numpy as jnp
from jax import lax
from jax.experimental import pallas as pl
from jax.experimental.pallas import tpu as pltpu
from jax.sharding import PartitionSpec as P

STEP = 0.3
EPS = 1e-06
F32 = jnp.float32
BF16 = jnp.bfloat16
PEERS = 16
VMEM = pl.BlockSpec(memory_space=pltpu.VMEM)


def call(body, outs, args, flops=1 << 22):
    moved = sum(a.size * a.dtype.itemsize for a in args)
    return pl.pallas_call(
        body,
        out_shape=[jax.ShapeDtypeStruct(shape, dtype) for shape, dtype in outs],
        in_specs=[VMEM] * len(args),
        out_specs=[VMEM] * len(outs),
        compiler_params=pltpu.CompilerParams(vmem_limit_bytes=40 << 20),
        cost_estimate=pl.CostEstimate(flops=flops, bytes_accessed=moved, transcendentals=0),
    )(*args)


def one_hot(ids, rows):
    grid = lax.broadcasted_iota(jnp.int32, (rows, ids.shape[1]), 0)
    return jnp.where(grid == ids, 1.0, 0.0).astype(BF16)


def mm(a, b):
    return lax.dot_general(a, b, (((1,), (0,)), ((), ())), preferred_element_type=F32)


def mm_t(a, b):
    return lax.dot_general(a, b, (((1,), (1,)), ((), ())), preferred_element_type=F32)


def core_of():
    return lax.axis_index("edge") & 1


def pack_kernel(block, src_ids, dst_ids, rel_ids, neg_ids, table, ids):
    table[...] = block[...].astype(BF16)
    ids[...] = jnp.full(ids.shape, -1, jnp.int32)
    for row, part in enumerate((src_ids, dst_ids, rel_ids, neg_ids)):
        ids[row : row + 1, : part.shape[1]] = part[...]


def id_rows(ids, edges):
    return ids[0:1, :edges], ids[1:2, :edges], ids[2:3, :edges], ids[3:4, :]


def gather_kernel(own, hot, rel, ids, src_out, rel_out, dst_out, hot_bf, rel_bf):
    rows = own.shape[1]
    hot_rows = hot.shape[1]
    src_at, dst_at, rel_at, _ = id_rows(ids, src_out.shape[1])
    hot_bf[...] = hot[...].astype(BF16)
    rel_bf[...] = rel[...].astype(BF16)
    src_out[...] = (
        mm(own[...], one_hot(src_at, rows)) + mm(hot_bf[...], one_hot(src_at - rows, hot_rows))
    ).astype(BF16)
    rel_out[...] = mm(rel_bf[...], one_hot(rel_at, rel.shape[1])).astype(BF16)
    dst_out[...] = mm(hot_bf[...], one_hot(dst_at - rows, hot_rows)).astype(BF16)


def edge_grads(partner, src, rel, dst, neg_at):
    query = (src * rel).astype(BF16)
    query_f = query.astype(F32)
    positive = jnp.sum(query_f * dst, axis=0, keepdims=True)
    pos_grad = -1.0 / (1.0 + jnp.exp(positive))
    scores = mm(partner.T, query)
    sig = (1.0 / (1.0 + jnp.exp(-scores))).astype(BF16)
    named = one_hot(neg_at, partner.shape[1])
    count = mm_t(jnp.ones((8, neg_at.shape[1]), BF16), named)[:1, :]
    scaled = partner.astype(F32) * count
    high = scaled.astype(BF16)
    low = (scaled - high.astype(F32)).astype(BF16)
    query_grad = pos_grad * dst + mm(high, sig) + mm(low, sig)
    src_grad = (query_grad * rel).astype(BF16)
    kind_grad = (query_grad * src).astype(BF16)
    dst_grad = (pos_grad * query_f).astype(BF16)
    return query, sig, count, src_grad, kind_grad, dst_grad


def grad_kernel(own, partner, hot, rel, src, rel_rows, dst_hot, ids, far_ids, keep, send, kind):
    width, rows = own.shape
    hot_rows = hot.shape[1]
    half = rows // 2
    edges = src.shape[1]
    core = core_of()
    side = lax.axis_index("bucket") // (lax.axis_size("bucket") // 2)
    own_flip = core * half

    def hot_at(at):
        local_at = at - rows - side * (hot_rows // 2)
        inside = (local_at >= 0) & (local_at < hot_rows // 2)
        return jnp.where(inside, local_at ^ own_flip, -1)

    def cold_at(at):
        return jnp.where(at < rows, at ^ own_flip, -1)

    src_at, dst_at, rel_at, neg_at = id_rows(ids, edges)
    dst = mm(partner[...], one_hot(dst_at, rows)) + dst_hot[...].astype(F32)
    _, _, _, src_grad, kind_grad, dst_grad = edge_grads(
        partner[...], src[...].astype(F32), rel_rows[...].astype(F32), dst, neg_at
    )
    block_sum = mm_t(src_grad, one_hot(cold_at(src_at), rows))
    hot_sum = mm_t(src_grad, one_hot(hot_at(src_at), rows))
    hot_sum += mm_t(dst_grad, one_hot(hot_at(dst_at), rows))
    kind_sum = mm_t(kind_grad, one_hot(rel_at - side * half, half))

    src_at, dst_at, rel_at, neg_at = id_rows(far_ids, edges)
    far_src = mm(partner[...], one_hot(src_at, rows)) + mm(hot[...], one_hot(src_at - rows, hot_rows))
    far_dst = mm(own[...], one_hot(dst_at, rows)) + mm(hot[...], one_hot(dst_at - rows, hot_rows))
    far_rel = mm(rel[...], one_hot(rel_at, rel.shape[1]))
    query, sig, count, src_grad, kind_grad, dst_grad = edge_grads(
        own[...], far_src, far_rel, far_dst, neg_at
    )
    row_grad = mm_t(query, sig) * count
    block_sum += mm_t(dst_grad, one_hot(cold_at(dst_at), rows))
    hot_sum += mm_t(src_grad, one_hot(hot_at(src_at), rows))
    hot_sum += mm_t(dst_grad, one_hot(hot_at(dst_at), rows))
    kind_sum += mm_t(kind_grad, one_hot(rel_at - side * half, half))

    first = core == 0
    neg_keep = jnp.where(first, row_grad[:, :half], row_grad[:, half:])
    neg_send = jnp.where(first, row_grad[:, half:], row_grad[:, :half])
    keep[:, :half] = block_sum[:, :half] + neg_keep
    keep[:, half:] = hot_sum[:, :half]
    send[:, :half] = (block_sum[:, half:] + neg_send).astype(BF16)
    send[:, half:] = hot_sum[:, half:].astype(BF16)
    kind[:width, :] = kind_sum.astype(BF16)
    kind[width:, :] = jnp.zeros((kind.shape[0] - width, kind.shape[1]), BF16)


def add_kernel(keep, got, out):
    width = keep.shape[0]
    out[:width, :] = (keep[...] + got[...].astype(F32)).astype(BF16)
    out[width:, :] = jnp.zeros((out.shape[0] - width, out.shape[1]), BF16)


def chunk_sum(ref, lanes, peers):
    rows = ref.shape[0] // PEERS
    total = 0.0
    for peer in peers:
        total = total + ref[peer * rows : (peer + 1) * rows, lanes].astype(F32)
    return total


def bucket_kernel(got, kind, out, own):
    rows = got.shape[0] // PEERS
    half = kind.shape[1]
    everyone = range(PEERS)
    own[...] = chunk_sum(got, slice(0, half), everyone)
    hot = chunk_sum(got, slice(half, 2 * half), everyone).astype(BF16)
    out[:, :half] = kind[...]
    for peer in everyone:
        out[peer * rows : (peer + 1) * rows, half:] = hot


def spread_kernel(got, own, out, kind):
    rows = got.shape[0] // PEERS
    half = own.shape[1]
    own_sum = own[...].astype(BF16)
    parts = []
    for side in range(2):
        peers = range(side * PEERS // 2, (side + 1) * PEERS // 2)
        parts.append(chunk_sum(got, slice(0, 2 * half), peers).astype(BF16))
    for peer in range(PEERS):
        at = slice(peer * rows, (peer + 1) * rows)
        out[at, :half] = own_sum
        for side, part in enumerate(parts):
            out[at, (side + 1) * half : (side + 2) * half] = part[:, half:]
            kind[at, side * half : (side + 1) * half] = part[:, :half]


def adagrad(weights, state, grads, new_weights, new_state, at):
    total = state[:, at] + jnp.sum(grads * grads, axis=0, keepdims=True) / grads.shape[0]
    new_state[:, at] = total
    new_weights[:, at] = weights[:, at] - grads * (STEP / (jnp.sqrt(total) + EPS))


def entity_kernel(mine, other, block, block_state, hot, hot_state, new_b, new_bs, new_h, new_hs):
    width, rows = block.shape
    half = rows // 2
    first = core_of() == 0
    for core in range(2):
        from_mine = first if core == 0 else jnp.logical_not(first)
        grads = jnp.where(from_mine, mine[:width, :], other[:width, :]).astype(F32)
        at = slice(core * half, (core + 1) * half)
        adagrad(block, block_state, grads[:, :half], new_b, new_bs, at)
        for side in range(2):
            at = slice(side * rows + core * half, side * rows + (core + 1) * half)
            part = grads[:, (side + 1) * half : (side + 2) * half]
            adagrad(hot, hot_state, part, new_h, new_hs, at)


def relation_kernel(grads, weights, state, new_weights, new_state):
    width, rows = weights.shape
    adagrad(weights, state, grads[:width, :].astype(F32), new_weights, new_state, slice(0, rows))


def flipped(x, axis, bit):
    return lax.ppermute(x, axis, [(i, i ^ bit) for i in range(lax.axis_size(axis))])


def exchanged(x, axis, groups=None):
    return lax.all_to_all(x, axis, 0, 0, tiled=True, axis_index_groups=groups)


def local(
    entity_block,
    block_state,
    hot_entities,
    hot_state,
    relations,
    relation_state,
    source_ids,
    target_ids,
    relation_ids,
    negative_ids,
):
    rows, width = entity_block.shape
    hot_rows = hot_entities.shape[0]
    edges = source_ids.shape[1]
    padded = -(-width // 256) * 256
    slot = padded // PEERS
    half = rows // 2
    block_t, hot_t, rel_t = entity_block.T, hot_entities.T, relations.T
    own_bf, ids = call(
        pack_kernel,
        [((width, rows), BF16), ((8, 1024), jnp.int32)],
        (block_t, source_ids, target_ids, relation_ids, negative_ids.reshape(1, -1)),
    )
    swap = lax.axis_size("bucket") // 2
    partner = flipped(own_bf, "bucket", swap)
    far_ids = flipped(ids, "bucket", swap)
    src, rel_rows, dst_hot, hot_bf, rel_bf = call(
        gather_kernel,
        [((width, edges), BF16)] * 3 + [((width, hot_rows), BF16), ((width, rows), BF16)],
        (own_bf, hot_t, rel_t, ids),
        1 << 30,
    )
    keep, send, kind = call(
        grad_kernel,
        [((width, rows), F32), ((width, rows), BF16), ((padded, half), BF16)],
        (own_bf, partner, hot_bf, rel_bf, src, rel_rows, dst_hot, ids, far_ids),
        1 << 31,
    )
    pairs = [[2 * i + core for i in range(PEERS)] for core in range(2)]
    (mixed,) = call(add_kernel, [((padded, rows), BF16)], (keep, flipped(send, "edge", 1)))
    mixed = exchanged(mixed, "edge", pairs)
    to_bucket, own_part = call(
        bucket_kernel, [((padded, rows), BF16), ((slot, half), F32)], (mixed, kind)
    )
    from_bucket = exchanged(to_bucket, "bucket")
    entity_part, kind_part = call(
        spread_kernel, [((padded, 3 * half), BF16), ((padded, rows), BF16)], (from_bucket, own_part)
    )
    mine = exchanged(entity_part, "edge", pairs)
    mine, kind_part = lax.optimization_barrier((mine, kind_part))
    other = flipped(mine, "edge", 1)
    kind_grads = exchanged(kind_part, "bucket")
    new_block, new_block_state, new_hot, new_hot_state = call(
        entity_kernel,
        [((width, rows), F32), ((1, rows), F32), ((width, hot_rows), F32), ((1, hot_rows), F32)],
        (mine, other, block_t, block_state.reshape(1, -1), hot_t, hot_state.reshape(1, -1)),
    )
    new_relations, new_relation_state = call(
        relation_kernel,
        [((width, rows), F32), ((1, rows), F32)],
        (kind_grads, rel_t, relation_state.reshape(1, -1)),
    )
    return (
        new_block.T,
        new_block_state.reshape(-1),
        new_hot.T,
        new_hot_state.reshape(-1),
        new_relations.T,
        new_relation_state.reshape(-1),
    )


def solution(mesh):
    placed = (
        P("bucket", None),
        P("bucket"),
        P(),
        P(),
        P("edge", None),
        P("edge"),
        P("bucket", "edge"),
        P("bucket", "edge"),
        P("bucket", "edge"),
        P("bucket", "edge", None),
    )
    return jax.shard_map(
        local,
        mesh=mesh,
        in_specs=placed,
        out_specs=(P("bucket", None), P("bucket"), P(), P(), P("edge", None), P("edge")),
        check_vma=False,
    )
```

time: 106 us -> 99.2 us (0.936)
  waiting for transfers between devices: 19.4 us -> 7.73 us
  blocking collectives: 50.4 us -> 59.8 us
  starting transfers between devices: 23.5 us -> 14.5 us
  local copies, waits for them, and re-layouts: 2.54 us -> 6.23 us
  Pallas kernels: 7.87 us -> 9.63 us
  other arithmetic: 1.07 us -> 0 us
    all_to_all x2 -> x3, blocking collectives: 50.4 us -> 59.8 us  [exchanged(): return lax.all_to_all(x, axis, 0, 0, tiled=True, axis_index_groups=groups)]
    all_to_all x2 -> x1, starting transfers between devices: 12.9 us -> 4.64 us  [exchanged(): return lax.all_to_all(x, axis, 0, 0, tiled=True, axis_index_groups=groups)]
    all_to_all x2 -> x1, waiting for transfers between devices: 10.8 us -> 3.42 us  [exchanged(): return lax.all_to_all(x, axis, 0, 0, tiled=True, axis_index_groups=groups)]
    ppermute x4, waiting for transfers between devices: 8.6 us -> 4.31 us  [flipped(): lax.ppermute(x, axis, [(i, i ^ bit) for i in range(lax.axis_size(axis))])]
    unnamed x22 -> x24, local copies, waits for them, and re-layouts: 2.54 us -> 6.23 us
    pallas_call x7 -> x8, Pallas kernels: 7.87 us -> 9.63 us  [call(): pl.pallas_call(body, out_shape=[jax.ShapeDtypeStruct(shape, dtype) for sh...]
    convert_element_type x1 -> x0, other arithmetic: 1.07 us -> none  [local(): own_bf = block_t.astype(BF16)]
  transfers between devices with their start and end apart: 6 -> 5, of which waited for: 6 -> 4; matrix products, arithmetic and copies ran while one was open for 0% -> 0% of each run, Pallas kernels for 2% -> 3%
where the time goes in v2:
time: 99.2 us; the launch traced here: 98.6 us
  blocking collectives  59.8 us (60%)
  starting transfers between devices  14.5 us (15%)
  Pallas kernels  9.63 us (10%)
  waiting for transfers between devices  7.73 us (8%)
  local copies, waits for them, and re-layouts  6.23 us (6%)
    all_to_all x3, blocking collectives, exchanged(): return lax.all_to_all(x, axis, 0, 0, tiled=True, axis_index_groups=groups)  59.8 us
    ppermute x4, starting transfers between devices, flipped(): lax.ppermute(x, axis, [(i, i ^ bit) for i in range(lax.axis_size(axis))])  9.82 us
    pallas_call x8, Pallas kernels, call(): pl.pallas_call(body, out_shape=[jax.ShapeDtypeStruct(shape, dtype) for sh...  9.63 us
    unnamed x24, local copies, waits for them, and re-layouts  6.23 us
    all_to_all x1, starting transfers between devices, exchanged(): return lax.all_to_all(x, axis, 0, 0, tiled=True, axis_index_groups=groups)  4.64 us
    ppermute x4, waiting for transfers between devices, flipped(): lax.ppermute(x, axis, [(i, i ^ bit) for i in range(lax.axis_size(axis))])  4.31 us
    all_to_all x1, waiting for transfers between devices, exchanged(): return lax.all_to_all(x, axis, 0, 0, tiled=True, axis_index_groups=groups)  3.42 us
  transfers between devices with their start and end apart: 5, of which 4 were waited for; matrix products, arithmetic and copies ran while one was open for 0% of the time, Pallas kernels for 3%

profile of v2, /device:TPU:8, one launch (start us, length us, event | category | flops | bytes accessed | tf_op | source)
XLA Modules:
  0.0 98.6 jit_solution(4057832786181915305)
XLA Ops:
  0.6 0.7 copy-done.6
  1.3 1.0 %copy-done = f32[256,400]{0,1:T(8,128)S(1)} copy-done((f32[256,400]{0,1:T(8,128)S(1)}, f32[256,400]{0,1:T(8,128)}, u32[]{:S(2)}) %copy-start) | copy-done | bytes 409624
  2.3 0.7 copy-done.5
  3.0 0.7 copy-done.7
  3.7 0.7 copy-done.8
  4.4 3.5 %collective-permute-start = (bf16[400,256]{1,0:T(8,128)(2,1)S(1)}, bf16[400,256]{1,0:T(8,128)(2,1)S(1)}, u32[]{:S(2)}, u32[]{:S(2)}) collective-permute-start(bf16[400,256]{1,0:T(8,128)(2,1)S(1)} %get-tuple-element.28.own), channel_id=1, source_target_pairs={{0,256},{32,288},{64,320},{96,352},{128,384},{160,416},{192,448},{... | collective-permute-start | bytes 614408 | tf_op jit(solution)/shard_map/ppermute | solution.py:207
  7.9 2.4 %collective-permute-start.1 = (s32[8,1024]{1,0:T(8,128)S(1)}, s32[8,1024]{1,0:T(8,128)S(1)}, u32[]{:S(2)}, u32[]{:S(2)}) collective-permute-start(s32[8,1024]{1,0:T(8,128)S(1)} %get-tuple-element.29.ids), channel_id=1, source_target_pairs={{0,256},{32,288},{64,320},{96,352},{128,384},{160,416},{192,448},{... | collective-permute-start | bytes 98312 | tf_op jit(solution)/shard_map/ppermute | solution.py:207
  10.4 1.1 %copy-done.2 = f32[512,400]{0,1:T(8,128)S(1)} copy-done((f32[512,400]{0,1:T(8,128)S(1)}, f32[512,400]{0,1:T(8,128)}, u32[]{:S(2)}) %copy-start.2) | copy-done | bytes 819224
  11.6 1.2 %shard_map.146 = (bf16[400,640]{1,0:T(8,128)(2,1)S(1)}, bf16[400,640]{1,0:T(8,128)(2,1)S(1)}, bf16[400,640]{1,0:T(8,128)(2,1)S(1)}, bf16[400,512]{1,0:T(8,128)(2,1)S(1)}, bf16[400,256]{1,0:T(8,128)(2,1)S(1)}) custom-call(bf16[400,256]{1,0:T(8,128)(2,1)S(1)} %get-tuple-element.28.own, f32[400,512]{1,0:T(8,128)S(1)} %bitcast.29, f32[400,256]{1,0:T(8,128)S(1)} %bitcast.31, ...), custom_call_target="tpu_custom_call" | custom-call | flops 1073741824 | bytes 1466368 | tf_op jit(solution)/shard_map/pallas_call | solution.py:18
  12.7 1.2 %collective-permute-done.1.far_ids = s32[8,1024]{1,0:T(8,128)S(1)} collective-permute-done((s32[8,1024]{1,0:T(8,128)S(1)}, s32[8,1024]{1,0:T(8,128)S(1)}, u32[]{:S(2)}, u32[]{:S(2)}) %collective-permute-start.1) | collective-permute-done | bytes 32800 | tf_op jit(solution)/shard_map/ppermute | solution.py:207
  14.0 5.3 %shard_map.147 = (f32[400,256]{1,0:T(8,128)S(1)}, bf16[400,256]{1,0:T(8,128)(2,1)S(1)}, bf16[512,128]{1,0:T(8,128)(2,1)S(1)}) custom-call(bf16[400,256]{1,0:T(8,128)(2,1)S(1)} %get-tuple-element.28.own, bf16[400,256]{1,0:T(8,128)(2,1)S(1)} %collective-permute-done.partner, bf16[400,512]{1,0:T(8,128)(2,1)S(1)} %get-tuple-element.30.hot, ...), custom_call_target="tpu_custom_call" | custom-call | flops 2147483648 | bytes 2625536 | tf_op jit(solution)/shard_map/pallas_call | solution.py:18
  19.3 1.9 %collective-permute-start.2 = (bf16[400,256]{1,0:T(8,128)(2,1)S(1)}, bf16[400,256]{1,0:T(8,128)(2,1)S(1)}, u32[]{:S(2)}, u32[]{:S(2)}) collective-permute-start(bf16[400,256]{1,0:T(8,128)(2,1)S(1)} %get-tuple-element.36), channel_id=1, source_target_pairs={{0,1},{1,0},{2,3},{3,2},{4,5},{5,4},{6,7},{7,6},{8,9},{9,8},{10,11... | collective-permute-start | bytes 614408 | tf_op jit(solution)/shard_map/ppermute | solution.py:207
  21.2 1.4 %collective-permute-done.2.got = bf16[400,256]{1,0:T(8,128)(2,1)S(1)} collective-permute-done((bf16[400,256]{1,0:T(8,128)(2,1)S(1)}, bf16[400,256]{1,0:T(8,128)(2,1)S(1)}, u32[]{:S(2)}, u32[]{:S(2)}) %collective-permute-start.2) | collective-permute-done | bytes 204832 | tf_op jit(solution)/shard_map/ppermute | solution.py:207
  22.7 24.6 %all_to_all.45 = bf16[16,32,256]{2,1,0:T(8,128)(2,1)S(1)} all-to-all(bf16[16,32,256]{2,1,0:T(8,128)(2,1)S(1)} %bitcast.28), channel_id=1, replica_groups={{0,2,4,6,8,10,12,14,16,18,20,22,24,26,28,30},{1,3,5,7,9,11,13,15,17,19,..., dimensions={0} | all-to-all | bytes 524288 | tf_op jit(solution)/shard_map/all_to_all | solution.py:211
  47.4 16.4 %all_to_all.46 = bf16[16,32,256]{2,1,0:T(8,128)(2,1)S(1)} all-to-all(bf16[16,32,256]{2,1,0:T(8,128)(2,1)S(1)} %bitcast.34), channel_id=1, replica_groups=mesh['bucket'=16,'edge'=32] {'bucket'}, dimensions={0} | all-to-all | bytes 524288 | tf_op jit(solution)/shard_map/all_to_all | solution.py:211
  63.8 0.8 shard_map.150
  64.6 18.7 %all_to_all.47 = bf16[16,32,384]{2,1,0:T(8,128)(2,1)S(1)} all-to-all(bf16[16,32,384]{2,1,0:T(8,128)(2,1)S(1)} %bitcast.33), channel_id=1, replica_groups={{0,2,4,6,8,10,12,14,16,18,20,22,24,26,28,30},{1,3,5,7,9,11,13,15,17,19,..., dimensions={0} | all-to-all | bytes 786432 | tf_op jit(solution)/shard_map/all_to_all | solution.py:211
  83.3 4.6 %all-to-all-start.3 = ((bf16[16,32,256]{2,1,0:T(8,128)(2,1)}), bf16[16,32,256]{2,1,0:T(8,128)(2,1)S(1)}, u32[]{:S(2)}, u32[]{:S(2)}) async-start(bf16[16,32,256]{2,1,0:T(8,128)(2,1)} %bitcast.16), calls=%async_computation.3 | async-start | bytes 524288 | tf_op jit(solution)/shard_map/all_to_all | solution.py:211
  88.0 1.9 %collective-permute-start.3 = (bf16[512,384]{1,0:T(8,128)(2,1)S(1)}, bf16[512,384]{1,0:T(8,128)(2,1)S(1)}, u32[]{:S(2)}, u32[]{:S(2)}) collective-permute-start(bf16[512,384]{1,0:T(8,128)(2,1)S(1)} %bitcast.23), channel_id=1, source_target_pairs={{0,1},{1,0},{2,3},{3,2},{4,5},{5,4},{6,7},{7,6},{8,9},{9,8},{10,11... | collective-permute-start | bytes 1179656 | tf_op jit(solution)/shard_map/ppermute | solution.py:207
  89.9 1.7 %collective-permute-done.3.other = bf16[512,384]{1,0:T(8,128)(2,1)S(1)} collective-permute-done((bf16[512,384]{1,0:T(8,128)(2,1)S(1)}, bf16[512,384]{1,0:T(8,128)(2,1)S(1)}, u32[]{:S(2)}, u32[]{:S(2)}) %collective-permute-start.3) | collective-permute-done | bytes 393248 | tf_op jit(solution)/shard_map/ppermute | solution.py:207
  92.3 1.3 %shard_map.151 = (f32[400,256]{1,0:T(8,128)}, f32[1,256]{1,0:T(1,128)}, f32[400,512]{1,0:T(8,128)}, f32[1,512]{1,0:T(1,128)}) custom-call(bf16[512,384]{1,0:T(8,128)(2,1)S(1)} %bitcast.24, bf16[512,384]{1,0:T(8,128)(2,1)S(1)} %collective-permute-done.3.other, f32[400,256]{1,0:T(8,128)S(1)} %bitcast.22, f32[1,256]{1,0:T(1,128)S(1)} %bitcast.37, ...), custom_call_target="tpu_custom_call" | custom-call | flops 4194304 | bytes 2018304 | tf_op jit(solution)/shard_map/pallas_call | solution.py:18
  93.6 3.4 %all-to-all-done.3 = bf16[16,32,256]{2,1,0:T(8,128)(2,1)S(1)} async-done(((bf16[16,32,256]{2,1,0:T(8,128)(2,1)}), bf16[16,32,256]{2,1,0:T(8,128)(2,1)S(1)}, u32[]{:S(2)}, u32[]{:S(2)}) %all-to-all-start.3) | async-done | bytes 262176 | tf_op jit(solution)/shard_map/all_to_all | solution.py:211
  97.0 0.7 copy-done.11
  97.7 0.9 shard_map.152
  (21 shorter events, 0.8 us)
Async XLA Ops:
  0.6 0.7 copy-start.6
  1.3 1.0 %copy-start = (f32[256,400]{0,1:T(8,128)S(1)}, f32[256,400]{0,1:T(8,128)}, u32[]{:S(2)}) copy-start(f32[256,400]{0,1:T(8,128)} %param.10) | copy-start | bytes 1228804
  2.3 0.7 copy-start.5
  3.0 0.7 copy-start.7
  3.7 0.7 copy-start.8
  4.4 6.0 %copy-start.4 = (f32[256,400]{0,1:T(8,128)S(1)}, f32[256,400]{0,1:T(8,128)}, u32[]{:S(2)}) copy-start(f32[256,400]{0,1:T(8,128)} %param.14) | copy-start | bytes 1228804
  4.4 9.5 %collective-permute-start = (bf16[400,256]{1,0:T(8,128)(2,1)S(1)}, bf16[400,256]{1,0:T(8,128)(2,1)S(1)}, u32[]{:S(2)}, u32[]{:S(2)}) collective-permute-start(bf16[400,256]{1,0:T(8,128)(2,1)S(1)} %get-tuple-element.28.own), channel_id=1, source_target_pairs={{0,256},{32,288},{64,320},{96,352},{128,384},{160,416},{192,448},{... | collective-permute-start | bytes 614408 | tf_op jit(solution)/shard_map/ppermute | solution.py:207
  7.9 6.0 %collective-permute-start.1 = (s32[8,1024]{1,0:T(8,128)S(1)}, s32[8,1024]{1,0:T(8,128)S(1)}, u32[]{:S(2)}, u32[]{:S(2)}) collective-permute-start(s32[8,1024]{1,0:T(8,128)S(1)} %get-tuple-element.29.ids), channel_id=1, source_target_pairs={{0,256},{32,288},{64,320},{96,352},{128,384},{160,416},{192,448},{... | collective-permute-start | bytes 98312 | tf_op jit(solution)/shard_map/ppermute | solution.py:207
  10.4 1.1 %copy-start.2 = (f32[512,400]{0,1:T(8,128)S(1)}, f32[512,400]{0,1:T(8,128)}, u32[]{:S(2)}) copy-start(f32[512,400]{0,1:T(8,128)} %param.12) | copy-start | bytes 2457604
  19.3 3.3 %collective-permute-start.2 = (bf16[400,256]{1,0:T(8,128)(2,1)S(1)}, bf16[400,256]{1,0:T(8,128)(2,1)S(1)}, u32[]{:S(2)}, u32[]{:S(2)}) collective-permute-start(bf16[400,256]{1,0:T(8,128)(2,1)S(1)} %get-tuple-element.36), channel_id=1, source_target_pairs={{0,1},{1,0},{2,3},{3,2},{4,5},{5,4},{6,7},{7,6},{8,9},{9,8},{10,11... | collective-permute-start | bytes 614408 | tf_op jit(solution)/shard_map/ppermute | solution.py:207
  63.8 27.8 %copy-start.3 = (f32[512,400]{0,1:T(8,128)S(1)}, f32[512,400]{0,1:T(8,128)}, u32[]{:S(2)}) copy-start(f32[512,400]{0,1:T(8,128)} %param.12) | copy-start | bytes 2457604
  83.3 8.3 %copy-start.1 = (f32[256,400]{0,1:T(8,128)S(1)}, f32[256,400]{0,1:T(8,128)}, u32[]{:S(2)}) copy-start(f32[256,400]{0,1:T(8,128)} %param.10) | copy-start | bytes 1228804
  83.3 13.7 %all-to-all-start.3 = ((bf16[16,32,256]{2,1,0:T(8,128)(2,1)}), bf16[16,32,256]{2,1,0:T(8,128)(2,1)S(1)}, u32[]{:S(2)}, u32[]{:S(2)}) async-start(bf16[16,32,256]{2,1,0:T(8,128)(2,1)} %bitcast.16), calls=%async_computation.3 | async-start | bytes 524288 | tf_op jit(solution)/shard_map/all_to_all | solution.py:211
  88.0 3.6 %copy-start.9 = (f32[512]{0:T(512)S(1)}, f32[512]{0:T(512)}, u32[]{:S(2)}) copy-start(f32[512]{0:T(512)} %param.13) | copy-start | bytes 6148
  88.0 3.6 %collective-permute-start.3 = (bf16[512,384]{1,0:T(8,128)(2,1)S(1)}, bf16[512,384]{1,0:T(8,128)(2,1)S(1)}, u32[]{:S(2)}, u32[]{:S(2)}) collective-permute-start(bf16[512,384]{1,0:T(8,128)(2,1)S(1)} %bitcast.23), channel_id=1, source_target_pairs={{0,1},{1,0},{2,3},{3,2},{4,5},{5,4},{6,7},{7,6},{8,9},{9,8},{10,11... | collective-permute-start | bytes 1179656 | tf_op jit(solution)/shard_map/ppermute | solution.py:207
  91.6 0.7 copy-start.10
  97.0 0.7 copy-start.11

commit v3 on v2

v3 whole, which is shorter than its diff:
```python
import functools

import jax
import jax.numpy as jnp
from jax import lax
from jax.experimental import pallas as pl
from jax.experimental.pallas import tpu as pltpu
from jax.sharding import PartitionSpec as P

STEP = 0.3
EPS = 1e-06
F32 = jnp.float32
BF16 = jnp.bfloat16
PEERS = 16
WORD = 256
VMEM = pl.BlockSpec(memory_space=pltpu.VMEM)


def call(body, outs, args, flops=1 << 22, specs=None, scratch=()):
    moved = sum(a.size * a.dtype.itemsize for a in args)
    return pl.pallas_call(
        body,
        out_shape=[jax.ShapeDtypeStruct(shape, dtype) for shape, dtype in outs],
        in_specs=specs or [VMEM] * len(args),
        out_specs=[VMEM] * len(outs),
        scratch_shapes=scratch,
        compiler_params=pltpu.CompilerParams(vmem_limit_bytes=32 << 20),
        cost_estimate=pl.CostEstimate(flops=flops, bytes_accessed=moved, transcendentals=0),
    )(*args)


def one_hot(ids, rows):
    grid = lax.broadcasted_iota(jnp.int32, (rows, ids.shape[1]), 0)
    return jnp.where(grid == ids, 1.0, 0.0).astype(BF16)


def mm(a, b):
    return lax.dot_general(a, b, (((1,), (0,)), ((), ())), preferred_element_type=F32)


def mm_t(a, b):
    return lax.dot_general(a, b, (((1,), (1,)), ((), ())), preferred_element_type=F32)


def core_of():
    return lax.axis_index("edge") & 1


def pieces(length):
    return [(at, min(WORD, length - at)) for at in range(0, length, WORD)]


def id_plan(edges, negatives):
    plan, row = [], 0
    for which, length, digits in ((0, edges, 2), (1, edges, 2), (2, edges, 1), (3, negatives, 1)):
        for digit in range(digits):
            plan.append((which, digit, row, length))
            row += len(pieces(length))
    return plan, -(-row // 32) * 32


def pack_kernel(block, src_ids, dst_ids, rel_ids, neg_ids, table, in_block, *scratch):
    held, sems, rows_f = scratch[:4], scratch[4], scratch[5]
    sources = (src_ids, dst_ids, rel_ids, neg_ids)
    copies = [pltpu.make_async_copy(block, in_block, sems.at[4])]
    for at, (source, target) in enumerate(zip(sources, held)):
        copies.append(pltpu.make_async_copy(source, target, sems.at[at]))
    for copy in copies:
        copy.start()
    for copy in copies[1:]:
        copy.wait()
    width = block.shape[0]
    plan, _ = id_plan(src_ids.shape[1], neg_ids.shape[1])
    rows_f[...] = jnp.full(rows_f.shape, -1.0, F32)
    for which, digit, row, length in plan:
        ids = held[which][...]
        ids = ids >> 8 if digit else ids & 255
        for step, (at, size) in enumerate(pieces(length)):
            rows_f[row + step : row + step + 1, :size] = ids[:, at : at + size].astype(F32)
    table[width:, :] = rows_f[...].astype(BF16)
    copies[0].wait()
    table[:width, :] = in_block[...].astype(BF16)


def unpack(table, width, edges, negatives):
    plan, _ = id_plan(edges, negatives)
    rows_f = table[width:, :].astype(F32)
    out = [None] * 4
    for which, digit, row, length in plan:
        parts = [
            rows_f[row + step : row + step + 1, : -(-size // 128) * 128]
            for step, (_, size) in enumerate(pieces(length))
        ]
        ids = jnp.concatenate(parts, axis=1).astype(jnp.int32)
        out[which] = out[which] + ids * 256 if digit else ids
    return out


def gather_kernel(negatives, own, hot, rel, src_out, rel_out, dst_out, hot_bf, rel_bf):
    width, rows = hot.shape[0], own.shape[1]
    hot_rows = hot.shape[1]
    src_at, dst_at, rel_at, _ = unpack(own, width, src_out.shape[1], negatives)
    hot_bf[...] = hot[...].astype(BF16)
    rel_bf[...] = rel[...].astype(BF16)
    src_out[...] = (
        mm(own[:width, :], one_hot(src_at, rows))
        + mm(hot_bf[...], one_hot(src_at - rows, hot_rows))
    ).astype(BF16)
    rel_out[...] = mm(rel_bf[...], one_hot(rel_at, rel.shape[1])).astype(BF16)
    dst_out[...] = mm(hot_bf[...], one_hot(dst_at - rows, hot_rows)).astype(BF16)


def edge_grads(partner, src, rel, dst, neg_at):
    query = (src * rel).astype(BF16)
    query_f = query.astype(F32)
    positive = jnp.sum(query_f * dst, axis=0, keepdims=True)
    pos_grad = -1.0 / (1.0 + jnp.exp(positive))
    scores = mm(partner.T, query)
    sig = (1.0 / (1.0 + jnp.exp(-scores))).astype(BF16)
    named = one_hot(neg_at, partner.shape[1])
    count = mm_t(jnp.ones((8, neg_at.shape[1]), BF16), named)[:1, :]
    scaled = partner.astype(F32) * count
    high = scaled.astype(BF16)
    low = (scaled - high.astype(F32)).astype(BF16)
    query_grad = pos_grad * dst + mm(high, sig) + mm(low, sig)
    src_grad = (query_grad * rel).astype(BF16)
    kind_grad = (query_grad * src).astype(BF16)
    dst_grad = (pos_grad * query_f).astype(BF16)
    return query, sig, count, src_grad, kind_grad, dst_grad


def grad_kernel(negatives, own, partner, hot, rel, src, rel_rows, dst_hot, keep, send):
    width, edges = src.shape
    rows, hot_rows = own.shape[1], hot.shape[1]
    half = rows // 2
    side = lax.axis_index("bucket") // (lax.axis_size("bucket") // 2)
    own_table, partner_table = own[:width, :], partner[:width, :]

    def hot_hits(at):
        at = at - rows - side * rows
        return one_hot(at, rows)

    src_at, dst_at, rel_at, neg_at = unpack(own, width, edges, negatives)
    dst = mm(partner_table, one_hot(dst_at, rows)) + dst_hot[...].astype(F32)
    _, _, _, src_grad, kind_grad, dst_grad = edge_grads(
        partner_table, src[...].astype(F32), rel_rows[...].astype(F32), dst, neg_at
    )
    block_sum = mm_t(src_grad, one_hot(src_at, rows))
    hot_sum = mm_t(src_grad, hot_hits(src_at))
    hot_sum += mm_t(dst_grad, hot_hits(dst_at))
    kind_sum = mm_t(kind_grad, one_hot(rel_at - side * half, half))

    src_at, dst_at, rel_at, neg_at = unpack(partner, width, edges, negatives)
    far_src = mm(partner_table, one_hot(src_at, rows)) + mm(
        hot[...], one_hot(src_at - rows, hot_rows)
    )
    far_dst = mm(own_table, one_hot(dst_at, rows)) + mm(hot[...], one_hot(dst_at - rows, hot_rows))
    far_rel = mm(rel[...], one_hot(rel_at, rel.shape[1]))
    query, sig, count, src_grad, kind_grad, dst_grad = edge_grads(
        own_table, far_src, far_rel, far_dst, neg_at
    )
    block_sum += mm_t(query, sig) * count
    block_sum += mm_t(dst_grad, one_hot(dst_at, rows))
    hot_sum += mm_t(src_grad, hot_hits(src_at))
    hot_sum += mm_t(dst_grad, hot_hits(dst_at))
    kind_sum += mm_t(kind_grad, one_hot(rel_at - side * half, half))

    @pl.when(core_of() == 0)
    def _():
        keep[:, :rows] = block_sum
        keep[:, rows:] = hot_sum
        send[:, :half] = kind_sum.astype(BF16)
        send[:, half:] = jnp.zeros((width, send.shape[1] - half), BF16)

    @pl.when(core_of() == 1)
    def _():
        keep[:, :half] = kind_sum
        keep[:, half:] = jnp.zeros((width, keep.shape[1] - half), F32)
        send[:, :rows] = block_sum.astype(BF16)
        send[:, rows:] = hot_sum.astype(BF16)


def merge_kernel(keep, got, out):
    width, lanes = keep.shape
    half = lanes // 4
    out[width:, :] = jnp.zeros((out.shape[0] - width, lanes), BF16)

    @pl.when(core_of() == 0)
    def _():
        out[:width, :] = (keep[...] + got[...].astype(F32)).astype(BF16)

    @pl.when(core_of() == 1)
    def _():
        out[:width, :half] = got[:, :half]
        out[:width, half : 2 * half] = keep[:, :half].astype(BF16)
        out[:width, 2 * half :] = jnp.zeros((width, 2 * half), BF16)


def chunk_sum(ref, lanes, peers):
    rows = ref.shape[0] // PEERS
    total = 0.0
    for peer in peers:
        total = total + ref[peer * rows : (peer + 1) * rows, lanes].astype(F32)
    return total


SIDES = (range(PEERS // 2), range(PEERS // 2, PEERS))


def first_kernel(got, out, held):
    rows = got.shape[0] // PEERS
    lanes = out.shape[1]
    half = lanes // 2

    @pl.when(core_of() == 0)
    def _():
        held[:, :lanes] = chunk_sum(got, slice(0, lanes), range(PEERS)).astype(BF16)
        held[:, lanes:] = jnp.zeros((rows, lanes), BF16)
        hot = chunk_sum(got, slice(lanes, 2 * lanes), range(PEERS)).astype(BF16)
        for peer in range(PEERS):
            out[peer * rows : (peer + 1) * rows, :] = hot

    @pl.when(core_of() == 1)
    def _():
        for side, peers in enumerate(SIDES):
            part = chunk_sum(got, slice(0, lanes), peers).astype(BF16)
            for core in range(2):
                at = core * lanes + side * half
                held[:, at : at + half] = part[:, core * half : (core + 1) * half]
        out[...] = jnp.zeros(out.shape, BF16)


def second_kernel(got, held, out):
    rows = got.shape[0] // PEERS
    lanes = got.shape[1]

    @pl.when(core_of() == 0)
    def _():
        parts = [held[:, :lanes]]
        parts += [chunk_sum(got, slice(0, lanes), peers).astype(BF16) for peers in SIDES]
        for peer in range(PEERS):
            for at, part in enumerate(parts):
                out[peer * rows : (peer + 1) * rows, at * lanes : (at + 1) * lanes] = part

    @pl.when(core_of() == 1)
    def _():
        for peer in range(PEERS):
            out[peer * rows : (peer + 1) * rows, : 2 * lanes] = held[...]
            out[peer * rows : (peer + 1) * rows, 2 * lanes :] = jnp.zeros((rows, lanes), BF16)


def adagrad(weights, state, grads, new_weights, new_state, at):
    total = state[:, at] + jnp.sum(grads * grads, axis=0, keepdims=True) / grads.shape[0]
    new_state[:, at] = total
    new_weights[:, at] = weights[:, at] - grads * (STEP / (jnp.sqrt(total) + EPS))


def update_kernel(
    mine, other, block, block_s, hot, hot_s, rel, rel_s, new_b, new_bs, new_h, new_hs, new_r, new_rs
):
    width, rows = block.shape
    first = core_of() == 0
    for part in range(3):
        at = slice(part * rows, (part + 1) * rows)
        grads = jnp.where(first, mine[:width, at], other[:width, at]).astype(F32)
        if part == 0:
            adagrad(block, block_s, grads, new_b, new_bs, slice(0, rows))
        else:
            adagrad(hot, hot_s, grads, new_h, new_hs, slice((part - 1) * rows, part * rows))
    grads = jnp.where(first, other[:width, :rows], mine[:width, rows : 2 * rows]).astype(F32)
    adagrad(rel, rel_s, grads, new_r, new_rs, slice(0, rows))


def flipped(x, axis, bit):
    return lax.ppermute(x, axis, [(i, i ^ bit) for i in range(lax.axis_size(axis))])


def exchanged(x, groups):
    return lax.all_to_all(x, ("bucket", "edge"), 0, 0, tiled=True, axis_index_groups=groups)


def edge_groups(core):
    n = lax.axis_size("edge")
    return [[b * n + e for e in range(core, n, 2)] for b in range(lax.axis_size("bucket"))]


def bucket_groups(core):
    n = lax.axis_size("edge")
    return [[b * n + e for b in range(lax.axis_size("bucket"))] for e in range(core, n, 2)]


def local(
    entity_block,
    block_state,
    hot_entities,
    hot_state,
    relations,
    relation_state,
    source_ids,
    target_ids,
    relation_ids,
    negative_ids,
):
    rows, width = entity_block.shape
    hot_rows = hot_entities.shape[0]
    edges = source_ids.shape[1]
    padded = -(-width // 256) * 256
    slot = padded // PEERS
    block_t, hot_t, rel_t = entity_block.T, hot_entities.T, relations.T
    negatives = negative_ids.shape[-1]
    ids = (source_ids, target_ids, relation_ids, negative_ids.reshape(1, -1))
    _, id_height = id_plan(edges, negatives)
    (own,) = call(
        pack_kernel,
        [((width + id_height, rows), BF16)],
        (block_t, *ids),
        specs=[pl.BlockSpec(memory_space=pl.ANY)] * 5,
        scratch=[pltpu.VMEM((width, rows), F32)]
        + [pltpu.VMEM(part.shape, jnp.int32) for part in ids]
        + [pltpu.SemaphoreType.DMA((5,)), pltpu.VMEM((id_height, rows), F32)],
    )
    partner = flipped(own, "bucket", lax.axis_size("bucket") // 2)
    src, rel_rows, dst_hot, hot_bf, rel_bf = call(
        functools.partial(gather_kernel, negatives),
        [((width, edges), BF16)] * 3 + [((width, hot_rows), BF16), ((width, rows), BF16)],
        (own, hot_t, rel_t),
        1 << 30,
    )
    keep, send = call(
        functools.partial(grad_kernel, negatives),
        [((width, 2 * rows), F32), ((width, 2 * rows), BF16)],
        (own, partner, hot_bf, rel_bf, src, rel_rows, dst_hot),
        1 << 31,
    )
    both = edge_groups(0) + bucket_groups(1)
    (mixed,) = call(
        merge_kernel, [((padded, 2 * rows), BF16)], (keep, flipped(send, "edge", 1))
    )
    mixed = exchanged(mixed, both)
    hot_part, held = call(
        first_kernel, [((padded, rows), BF16), ((slot, 2 * rows), BF16)], (mixed,)
    )
    hot_part = exchanged(hot_part, bucket_groups(0) + edge_groups(1))
    (totals,) = call(second_kernel, [((padded, 3 * rows), BF16)], (hot_part, held))
    mine = exchanged(totals, both)
    other = flipped(mine, "edge", 1)
    shapes = [(width, rows), (1, rows), (width, hot_rows), (1, hot_rows), (width, rows), (1, rows)]
    new_block, new_block_state, new_hot, new_hot_state, new_relations, new_relation_state = call(
        update_kernel,
        [(shape, F32) for shape in shapes],
        (
            mine,
            other,
            block_t,
            block_state.reshape(1, -1),
            hot_t,
            hot_state.reshape(1, -1),
            rel_t,
            relation_state.reshape(1, -1),
        ),
    )
    return (
        new_block.T,
        new_block_state.reshape(-1),
        new_hot.T,
        new_hot_state.reshape(-1),
        new_relations.T,
        new_relation_state.reshape(-1),
    )


def solution(mesh):
    placed = (
        P("bucket", None),
        P("bucket"),
        P(),
        P(),
        P("edge", None),
        P("edge"),
        P("bucket", "edge"),
        P("bucket", "edge"),
        P("bucket", "edge"),
        P("bucket", "edge", None),
    )
    return jax.shard_map(
        local,
        mesh=mesh,
        in_specs=placed,
        out_specs=(P("bucket", None), P("bucket"), P(), P(), P("edge", None), P("edge")),
        check_vma=False,
    )
```

time: 99.2 us -> 93.5 us (0.943)
  the two profiles are of different devices: /device:TPU:8 before, /device:TPU:1 now
where the time goes in v3:
time: 93.5 us; the launch traced here: 93 us
  blocking collectives  53.6 us (57%)
  starting transfers between devices  20.4 us (22%)
  Pallas kernels  8.52 us (9%)
  local copies, waits for them, and re-layouts  5.57 us (6%)
  waiting for transfers between devices  4.17 us (4%)
    all_to_all x3, blocking collectives, exchanged(): lax.all_to_all(x, ('bucket', 'edge'), 0, 0, tiled=True, axis_index_groups...  53.6 us
    ppermute x3, starting transfers between devices, flipped(): lax.ppermute(x, axis, [(i, i ^ bit) for i in range(lax.axis_size(axis))])  20.4 us
    pallas_call x7, Pallas kernels, call(): pl.pallas_call(body, out_shape=[jax.ShapeDtypeStruct(shape, dtype) for sh...  8.52 us
    unnamed x24, local copies, waits for them, and re-layouts  5.57 us
    ppermute x3, waiting for transfers between devices, flipped(): lax.ppermute(x, axis, [(i, i ^ bit) for i in range(lax.axis_size(axis))])  4.17 us
  transfers between devices with their start and end apart: 3, of which 3 were waited for; matrix products, arithmetic and copies ran while one was open for 0% of the time, Pallas kernels for 1%

profile of v3, /device:TPU:1, one launch (start us, length us, event | category | flops | bytes accessed | tf_op | source)
XLA Modules:
  0.0 93.0 jit_solution(10276464787018656323)
XLA Ops:
  0.6 0.7 copy-done.6
  1.3 1.0 %copy-done = f32[256,400]{0,1:T(8,128)S(1)} copy-done((f32[256,400]{0,1:T(8,128)S(1)}, f32[256,400]{0,1:T(8,128)}, u32[]{:S(2)}) %copy-start) | copy-done | bytes 409624
  2.3 0.7 copy-done.5
  3.0 0.7 copy-done.7
  3.7 0.7 copy-done.8
  4.4 0.3 shard_map.145.own
  4.7 3.9 %collective-permute-start = (bf16[432,256]{1,0:T(8,128)(2,1)S(1)}, bf16[432,256]{1,0:T(8,128)(2,1)S(1)}, u32[]{:S(2)}, u32[]{:S(2)}) collective-permute-start(bf16[432,256]{1,0:T(8,128)(2,1)S(1)} %shard_map.145.own), channel_id=1, source_target_pairs={{0,256},{32,288},{64,320},{96,352},{128,384},{160,416},{192,448},{... | collective-permute-start | bytes 663560 | tf_op jit(solution)/shard_map/ppermute | solution.py:275
  8.7 1.1 %copy-done.2 = f32[512,400]{0,1:T(8,128)S(1)} copy-done((f32[512,400]{0,1:T(8,128)S(1)}, f32[512,400]{0,1:T(8,128)}, u32[]{:S(2)}) %copy-start.2) | copy-done | bytes 819224
  9.8 1.2 %shard_map.146 = (bf16[400,640]{1,0:T(8,128)(2,1)S(1)}, bf16[400,640]{1,0:T(8,128)(2,1)S(1)}, bf16[400,640]{1,0:T(8,128)(2,1)S(1)}, bf16[400,512]{1,0:T(8,128)(2,1)S(1)}, bf16[400,256]{1,0:T(8,128)(2,1)S(1)}) custom-call(bf16[432,256]{1,0:T(8,128)(2,1)S(1)} %shard_map.145.own, f32[400,512]{1,0:T(8,128)S(1)} %bitcast.27, f32[400,256]{1,0:T(8,128)S(1)} %bitcast.29), custom_call_target="tpu_custom_call" | custom-call | flops 1073741824 | bytes 1449984 | tf_op jit(solution)/shard_map/pallas_call | solution.py:21
  11.0 0.9 collective-permute-done.partner
  11.9 5.4 %shard_map.147 = (f32[400,512]{1,0:T(8,128)S(1)}, bf16[400,512]{1,0:T(8,128)(2,1)S(1)}) custom-call(bf16[432,256]{1,0:T(8,128)(2,1)S(1)} %shard_map.145.own, bf16[432,256]{1,0:T(8,128)(2,1)S(1)} %collective-permute-done.partner, bf16[400,512]{1,0:T(8,128)(2,1)S(1)} %get-tuple-element.21.hot, bf16[400,256]{1,0:T(8,128)(2,1)S(1)} %get-tuple-element.22.rel, ...), custom_call_target="tpu_custom_call" | custom-call | flops 2147483648 | bytes 2592768 | tf_op jit(solution)/shard_map/pallas_call | solution.py:21
  17.4 9.3 %collective-permute-start.1 = (bf16[400,512]{1,0:T(8,128)(2,1)S(1)}, bf16[400,512]{1,0:T(8,128)(2,1)S(1)}, u32[]{:S(2)}, u32[]{:S(2)}) collective-permute-start(bf16[400,512]{1,0:T(8,128)(2,1)S(1)} %get-tuple-element.27), channel_id=1, source_target_pairs={{0,1},{1,0},{2,3},{3,2},{4,5},{5,4},{6,7},{7,6},{8,9},{9,8},{10,11... | collective-permute-start | bytes 1228808 | tf_op jit(solution)/shard_map/ppermute | solution.py:275
  26.7 1.4 %collective-permute-done.1.got = bf16[400,512]{1,0:T(8,128)(2,1)S(1)} collective-permute-done((bf16[400,512]{1,0:T(8,128)(2,1)S(1)}, bf16[400,512]{1,0:T(8,128)(2,1)S(1)}, u32[]{:S(2)}, u32[]{:S(2)}) %collective-permute-start.1) | collective-permute-done | bytes 409632 | tf_op jit(solution)/shard_map/ppermute | solution.py:275
  28.1 0.1 shard_map.148
  28.2 14.1 %all_to_all.33 = bf16[16,32,512]{2,1,0:T(8,128)(2,1)S(1)} all-to-all(bf16[16,32,512]{2,1,0:T(8,128)(2,1)S(1)} %bitcast.23), channel_id=1, replica_groups={{0,2,4,6,8,10,12,14,16,18,20,22,24,26,28,30},{32,34,36,38,40,42,44,46,4..., dimensions={0} | all-to-all | bytes 1048576 | tf_op jit(solution)/shard_map/all_to_all | solution.py:279
  42.3 21.1 %all_to_all.34 = bf16[16,32,256]{2,1,0:T(8,128)(2,1)S(1)} all-to-all(bf16[16,32,256]{2,1,0:T(8,128)(2,1)S(1)} %bitcast.31), channel_id=1, replica_groups={{0,32,64,96,128,160,192,224,256,288,320,352,384,416,448,480},{2,34,66,9..., dimensions={0} | all-to-all | bytes 524288 | tf_op jit(solution)/shard_map/all_to_all | solution.py:279
  63.4 0.1 shard_map.150
  63.5 0.0 copy-start.11
  63.5 18.4 %all_to_all.35 = bf16[16,32,768]{2,1,0:T(8,128)(2,1)S(1)} all-to-all(bf16[16,32,768]{2,1,0:T(8,128)(2,1)S(1)} %bitcast.19), channel_id=1, replica_groups={{0,2,4,6,8,10,12,14,16,18,20,22,24,26,28,30},{32,34,36,38,40,42,44,46,4..., dimensions={0} | all-to-all | bytes 1572864 | tf_op jit(solution)/shard_map/all_to_all | solution.py:279
  81.9 7.1 %collective-permute-start.2 = (bf16[512,768]{1,0:T(8,128)(2,1)S(1)}, bf16[512,768]{1,0:T(8,128)(2,1)S(1)}, u32[]{:S(2)}, u32[]{:S(2)}) collective-permute-start(bf16[512,768]{1,0:T(8,128)(2,1)S(1)} %bitcast.20), channel_id=1, source_target_pairs={{0,1},{1,0},{2,3},{3,2},{4,5},{5,4},{6,7},{7,6},{8,9},{9,8},{10,11... | collective-permute-start | bytes 2359304 | tf_op jit(solution)/shard_map/ppermute | solution.py:275
  89.0 1.9 %collective-permute-done.2.other = bf16[512,768]{1,0:T(8,128)(2,1)S(1)} collective-permute-done((bf16[512,768]{1,0:T(8,128)(2,1)S(1)}, bf16[512,768]{1,0:T(8,128)(2,1)S(1)}, u32[]{:S(2)}, u32[]{:S(2)}) %collective-permute-start.2) | collective-permute-done | bytes 786464 | tf_op jit(solution)/shard_map/ppermute | solution.py:275
  90.9 0.7 copy-done.9
  91.6 0.0 copy-done.10
  91.6 1.4 %shard_map.151 = (f32[400,256]{1,0:T(8,128)}, f32[1,256]{1,0:T(1,128)}, f32[400,512]{1,0:T(8,128)}, f32[1,512]{1,0:T(1,128)}, f32[400,256]{1,0:T(8,128)}, /*index=5*/f32[1,256]{1,0:T(1,128)}) custom-call(bf16[512,768]{1,0:T(8,128)(2,1)S(1)} %bitcast.21, bf16[512,768]{1,0:T(8,128)(2,1)S(1)} %collective-permute-done.2.other, f32[400,256]{1,0:T(8,128)S(1)} %bitcast.25, ...), custom_call_target="tpu_custom_call" | custom-call | flops 4194304 | bytes 3215360 | tf_op jit(solution)/shard_map/pallas_call | solution.py:21
  (16 shorter events, 0.1 us)
Async XLA Ops:
  0.6 0.7 copy-start.6
  1.3 1.0 %copy-start = (f32[256,400]{0,1:T(8,128)S(1)}, f32[256,400]{0,1:T(8,128)}, u32[]{:S(2)}) copy-start(f32[256,400]{0,1:T(8,128)} %param.10) | copy-start | bytes 1228804
  2.3 0.7 copy-start.5
  3.0 0.7 copy-start.7
  3.7 0.7 copy-start.8
  4.4 4.3 %copy-start.4 = (f32[256,400]{0,1:T(8,128)S(1)}, f32[256,400]{0,1:T(8,128)}, u32[]{:S(2)}) copy-start(f32[256,400]{0,1:T(8,128)} %param.14) | copy-start | bytes 1228804
  4.7 7.3 %collective-permute-start = (bf16[432,256]{1,0:T(8,128)(2,1)S(1)}, bf16[432,256]{1,0:T(8,128)(2,1)S(1)}, u32[]{:S(2)}, u32[]{:S(2)}) collective-permute-start(bf16[432,256]{1,0:T(8,128)(2,1)S(1)} %shard_map.145.own), channel_id=1, source_target_pairs={{0,256},{32,288},{64,320},{96,352},{128,384},{160,416},{192,448},{... | collective-permute-start | bytes 663560 | tf_op jit(solution)/shard_map/ppermute | solution.py:275
  8.7 1.1 %copy-start.2 = (f32[512,400]{0,1:T(8,128)S(1)}, f32[512,400]{0,1:T(8,128)}, u32[]{:S(2)}) copy-start(f32[512,400]{0,1:T(8,128)} %param.12) | copy-start | bytes 2457604
  17.4 10.7 %collective-permute-start.1 = (bf16[400,512]{1,0:T(8,128)(2,1)S(1)}, bf16[400,512]{1,0:T(8,128)(2,1)S(1)}, u32[]{:S(2)}, u32[]{:S(2)}) collective-permute-start(bf16[400,512]{1,0:T(8,128)(2,1)S(1)} %get-tuple-element.27), channel_id=1, source_target_pairs={{0,1},{1,0},{2,3},{3,2},{4,5},{5,4},{6,7},{7,6},{8,9},{9,8},{10,11... | collective-permute-start | bytes 1228808 | tf_op jit(solution)/shard_map/ppermute | solution.py:275
  63.4 27.5 %copy-start.3 = (f32[512,400]{0,1:T(8,128)S(1)}, f32[512,400]{0,1:T(8,128)}, u32[]{:S(2)}) copy-start(f32[512,400]{0,1:T(8,128)} %param.12) | copy-start | bytes 2457604
  63.4 27.5 %copy-start.1 = (f32[256,400]{0,1:T(8,128)S(1)}, f32[256,400]{0,1:T(8,128)}, u32[]{:S(2)}) copy-start(f32[256,400]{0,1:T(8,128)} %param.10) | copy-start | bytes 1228804
  63.5 27.5 %copy-start.11 = (f32[256]{0:T(256)S(1)}, f32[256]{0:T(256)}, u32[]{:S(2)}) copy-start(f32[256]{0:T(256)} %param.15) | copy-start | bytes 3076
  81.9 9.0 %collective-permute-start.2 = (bf16[512,768]{1,0:T(8,128)(2,1)S(1)}, bf16[512,768]{1,0:T(8,128)(2,1)S(1)}, u32[]{:S(2)}, u32[]{:S(2)}) collective-permute-start(bf16[512,768]{1,0:T(8,128)(2,1)S(1)} %bitcast.20), channel_id=1, source_target_pairs={{0,1},{1,0},{2,3},{3,2},{4,5},{5,4},{6,7},{7,6},{8,9},{9,8},{10,11... | collective-permute-start | bytes 2359304 | tf_op jit(solution)/shard_map/ppermute | solution.py:275
  90.9 0.7 copy-start.9
  90.9 0.7 copy-start.10

commit v4 on v3

--- a/solution.py
+++ b/solution.py
@@ -14,17 +14,18 @@
 PEERS = 16
 WORD = 256
 VMEM = pl.BlockSpec(memory_space=pltpu.VMEM)
-
-
-def call(body, outs, args, flops=1 << 22, specs=None, scratch=()):
+HBM = pl.BlockSpec(memory_space=pltpu.HBM)
+
+
+def call(body, outs, args, flops=1 << 22, specs=None, out_specs=None, scratch=(), room=32):
     moved = sum(a.size * a.dtype.itemsize for a in args)
     return pl.pallas_call(
         body,
         out_shape=[jax.ShapeDtypeStruct(shape, dtype) for shape, dtype in outs],
         in_specs=specs or [VMEM] * len(args),
-        out_specs=[VMEM] * len(outs),
+        out_specs=out_specs or [VMEM] * len(outs),
         scratch_shapes=scratch,
-        compiler_params=pltpu.CompilerParams(vmem_limit_bytes=32 << 20),
+        compiler_params=pltpu.CompilerParams(vmem_limit_bytes=room << 20),
         cost_estimate=pl.CostEstimate(flops=flops, bytes_accessed=moved, transcendentals=0),
     )(*args)
 
@@ -96,8 +97,13 @@
     return out
 
 
-def gather_kernel(negatives, own, hot, rel, src_out, rel_out, dst_out, hot_bf, rel_bf):
+def gather_kernel(
+    negatives, own, hot, rel, block_s, hot_s, rel_s, src_out, rel_out, dst_out, hot_bf, rel_bf, states
+):
     width, rows = hot.shape[0], own.shape[1]
+    states[...] = jnp.zeros(states.shape, F32)
+    for at, state in enumerate((block_s, hot_s, rel_s)):
+        states[at : at + 1, : state.shape[1]] = state[...]
     hot_rows = hot.shape[1]
     src_at, dst_at, rel_at, _ = unpack(own, width, src_out.shape[1], negatives)
     hot_bf[...] = hot[...].astype(BF16)
@@ -137,33 +143,31 @@
     own_table, partner_table = own[:width, :], partner[:width, :]
 
     def hot_hits(at):
-        at = at - rows - side * rows
-        return one_hot(at, rows)
-
-    src_at, dst_at, rel_at, neg_at = unpack(own, width, edges, negatives)
-    dst = mm(partner_table, one_hot(dst_at, rows)) + dst_hot[...].astype(F32)
-    _, _, _, src_grad, kind_grad, dst_grad = edge_grads(
-        partner_table, src[...].astype(F32), rel_rows[...].astype(F32), dst, neg_at
-    )
-    block_sum = mm_t(src_grad, one_hot(src_at, rows))
-    hot_sum = mm_t(src_grad, hot_hits(src_at))
-    hot_sum += mm_t(dst_grad, hot_hits(dst_at))
-    kind_sum = mm_t(kind_grad, one_hot(rel_at - side * half, half))
-
-    src_at, dst_at, rel_at, neg_at = unpack(partner, width, edges, negatives)
-    far_src = mm(partner_table, one_hot(src_at, rows)) + mm(
-        hot[...], one_hot(src_at - rows, hot_rows)
-    )
-    far_dst = mm(own_table, one_hot(dst_at, rows)) + mm(hot[...], one_hot(dst_at - rows, hot_rows))
-    far_rel = mm(rel[...], one_hot(rel_at, rel.shape[1]))
-    query, sig, count, src_grad, kind_grad, dst_grad = edge_grads(
-        own_table, far_src, far_rel, far_dst, neg_at
-    )
-    block_sum += mm_t(query, sig) * count
-    block_sum += mm_t(dst_grad, one_hot(dst_at, rows))
-    hot_sum += mm_t(src_grad, hot_hits(src_at))
-    hot_sum += mm_t(dst_grad, hot_hits(dst_at))
-    kind_sum += mm_t(kind_grad, one_hot(rel_at - side * half, half))
+        return one_hot(at - rows - side * rows, rows)
+
+    near_src, near_dst, near_rel, near_neg = unpack(own, width, edges, negatives)
+    dst = mm(partner_table, one_hot(near_dst, rows)) + dst_hot[...].astype(F32)
+    _, _, _, near_src_grad, near_kind_grad, near_dst_grad = edge_grads(
+        partner_table, src[...].astype(F32), rel_rows[...].astype(F32), dst, near_neg
+    )
+    far_src, far_dst, far_rel, far_neg = unpack(partner, width, edges, negatives)
+    ends = jnp.concatenate([far_src, far_dst], axis=1)
+    from_hot = mm(hot[...], one_hot(ends - rows, hot_rows))
+    src_rows = mm(partner_table, one_hot(far_src, rows)) + from_hot[:, :edges]
+    dst_rows = mm(own_table, one_hot(far_dst, rows)) + from_hot[:, edges:]
+    kind_rows = mm(rel[...], one_hot(far_rel, rel.shape[1]))
+    query, sig, count, far_src_grad, far_kind_grad, far_dst_grad = edge_grads(
+        own_table, src_rows, kind_rows, dst_rows, far_neg
+    )
+    cold = jnp.concatenate([near_src_grad, far_dst_grad], axis=1)
+    cold_at = jnp.concatenate([near_src, far_dst], axis=1)
+    block_sum = mm_t(query, sig) * count + mm_t(cold, one_hot(cold_at, rows))
+    named = jnp.concatenate([near_dst_grad, cold, far_src_grad], axis=1)
+    named_at = jnp.concatenate([near_dst, cold_at, far_src], axis=1)
+    hot_sum = mm_t(named, hot_hits(named_at))
+    kind_grad = jnp.concatenate([near_kind_grad, far_kind_grad], axis=1)
+    kind_at = jnp.concatenate([near_rel, far_rel], axis=1)
+    kind_sum = mm_t(kind_grad, one_hot(kind_at - side * half, half))
 
     @pl.when(core_of() == 0)
     def _():
@@ -249,26 +253,31 @@
             out[peer * rows : (peer + 1) * rows, 2 * lanes :] = jnp.zeros((rows, lanes), BF16)
 
 
-def adagrad(weights, state, grads, new_weights, new_state, at):
-    total = state[:, at] + jnp.sum(grads * grads, axis=0, keepdims=True) / grads.shape[0]
-    new_state[:, at] = total
-    new_weights[:, at] = weights[:, at] - grads * (STEP / (jnp.sqrt(total) + EPS))
-
-
-def update_kernel(
-    mine, other, block, block_s, hot, hot_s, rel, rel_s, new_b, new_bs, new_h, new_hs, new_r, new_rs
-):
+def update_kernel(mine, other, states, block, hot, rel, *refs):
+    outs, state_outs, helds, state_held, sems = refs[:3], refs[3:6], refs[6:9], refs[9], refs[10]
     width, rows = block.shape
     first = core_of() == 0
-    for part in range(3):
-        at = slice(part * rows, (part + 1) * rows)
-        grads = jnp.where(first, mine[:width, at], other[:width, at]).astype(F32)
-        if part == 0:
-            adagrad(block, block_s, grads, new_b, new_bs, slice(0, rows))
-        else:
-            adagrad(hot, hot_s, grads, new_h, new_hs, slice((part - 1) * rows, part * rows))
-    grads = jnp.where(first, other[:width, :rows], mine[:width, rows : 2 * rows]).astype(F32)
-    adagrad(rel, rel_s, grads, new_r, new_rs, slice(0, rows))
+    copies = []
+    state_held[...] = states[...]
+    for table, weights in enumerate((block, hot, rel)):
+        for low in range(0, weights.shape[1], rows):
+            at = slice(low, low + rows)
+            if table < 2:
+                lanes = slice(table * rows + low, (table + 1) * rows + low)
+                grads = jnp.where(first, mine[:width, lanes], other[:width, lanes])
+            else:
+                grads = jnp.where(first, other[:width, :rows], mine[:width, rows : 2 * rows])
+            grads = grads.astype(F32)
+            total = states[table : table + 1, at] + jnp.sum(grads * grads, axis=0, keepdims=True) / width
+            state_held[table : table + 1, at] = total
+            helds[table][:, at] = weights[:, at] - grads * (STEP / (jnp.sqrt(total) + EPS))
+        state = state_held.at[table : table + 1, : weights.shape[1]]
+        copies.append(pltpu.make_async_copy(helds[table], outs[table], sems.at[2 * table]))
+        copies.append(pltpu.make_async_copy(state, state_outs[table], sems.at[2 * table + 1]))
+        copies[-2].start()
+        copies[-1].start()
+    for copy in copies:
+        copy.wait()
 
 
 def flipped(x, axis, bit):
@@ -314,16 +323,19 @@
         pack_kernel,
         [((width + id_height, rows), BF16)],
         (block_t, *ids),
-        specs=[pl.BlockSpec(memory_space=pl.ANY)] * 5,
+        specs=[HBM] * 5,
+        room=63,
         scratch=[pltpu.VMEM((width, rows), F32)]
         + [pltpu.VMEM(part.shape, jnp.int32) for part in ids]
         + [pltpu.SemaphoreType.DMA((5,)), pltpu.VMEM((id_height, rows), F32)],
     )
     partner = flipped(own, "bucket", lax.axis_size("bucket") // 2)
-    src, rel_rows, dst_hot, hot_bf, rel_bf = call(
+    state_rows = [state.reshape(1, -1) for state in (block_state, hot_state, relation_state)]
+    src, rel_rows, dst_hot, hot_bf, rel_bf, states = call(
         functools.partial(gather_kernel, negatives),
-        [((width, edges), BF16)] * 3 + [((width, hot_rows), BF16), ((width, rows), BF16)],
-        (own, hot_t, rel_t),
+        [((width, edges), BF16)] * 3
+        + [((width, hot_rows), BF16), ((width, rows), BF16), ((8, hot_rows), F32)],
+        (own, hot_t, rel_t, *state_rows),
         1 << 30,
     )
     keep, send = call(
@@ -344,28 +356,23 @@
     (totals,) = call(second_kernel, [((padded, 3 * rows), BF16)], (hot_part, held))
     mine = exchanged(totals, both)
     other = flipped(mine, "edge", 1)
-    shapes = [(width, rows), (1, rows), (width, hot_rows), (1, hot_rows), (width, rows), (1, rows)]
-    new_block, new_block_state, new_hot, new_hot_state, new_relations, new_relation_state = call(
+    tables = (block_t, hot_t, rel_t)
+    new_block, new_hot, new_relations, *new_states = call(
         update_kernel,
-        [(shape, F32) for shape in shapes],
-        (
-            mine,
-            other,
-            block_t,
-            block_state.reshape(1, -1),
-            hot_t,
-            hot_state.reshape(1, -1),
-            rel_t,
-            relation_state.reshape(1, -1),
-        ),
-    )
+        [(part.shape, F32) for part in (*tables, *state_rows)],
+        (mine, other, states, *tables),
+        out_specs=[HBM] * 6,
+        scratch=[pltpu.VMEM(part.shape, F32) for part in (*tables, states)]
+        + [pltpu.SemaphoreType.DMA((6,))],
+    )
+    new_block_state, new_hot_state, new_relation_state = [part.reshape(-1) for part in new_states]
     return (
         new_block.T,
-        new_block_state.reshape(-1),
+        new_block_state,
         new_hot.T,
-        new_hot_state.reshape(-1),
+        new_hot_state,
         new_relations.T,
-        new_relation_state.reshape(-1),
+        new_relation_state,
     )
 
 

time: 93.5 us -> 90.1 us (0.964)
  local copies, waits for them, and re-layouts: 5.57 us -> 2.78 us
    unnamed x24 -> x18, local copies, waits for them, and re-layouts: 5.57 us -> 2.78 us
  transfers between devices with their start and end apart: 3 -> 3, of which waited for: 3 -> 2; matrix products, arithmetic and copies ran while one was open for 0% -> 0% of each run, Pallas kernels for 1% -> 1%
where the time goes in v4:
time: 90.1 us; the launch traced here: 89.7 us
  blocking collectives  53.6 us (59%)
  starting transfers between devices  19.9 us (22%)
  Pallas kernels  9.36 us (10%)
  waiting for transfers between devices  3.24 us (4%)
  local copies, waits for them, and re-layouts  2.78 us (3%)
    all_to_all x3, blocking collectives, exchanged(): lax.all_to_all(x, ('bucket', 'edge'), 0, 0, tiled=True, axis_index_groups...  53.6 us
    ppermute x3, starting transfers between devices, flipped(): lax.ppermute(x, axis, [(i, i ^ bit) for i in range(lax.axis_size(axis))])  19.9 us
    pallas_call x7, Pallas kernels, call(): pl.pallas_call(body, out_shape=[jax.ShapeDtypeStruct(shape, dtype) for sh...  9.36 us
    ppermute x3, waiting for transfers between devices, flipped(): lax.ppermute(x, axis, [(i, i ^ bit) for i in range(lax.axis_size(axis))])  3.24 us
    unnamed x18, local copies, waits for them, and re-layouts  2.78 us
  transfers between devices with their start and end apart: 3, of which 2 were waited for; matrix products, arithmetic and copies ran while one was open for 0% of the time, Pallas kernels for 1%

profile of v4, /device:TPU:1, one launch (start us, length us, event | category | flops | bytes accessed | tf_op | source)
XLA Modules:
  0.0 89.7 jit_solution(4615613213343028184)
XLA Ops:
  0.6 1.8 %shard_map.145.own = bf16[432,256]{1,0:T(8,128)(2,1)} custom-call(f32[400,256]{1,0:T(8,128)} %bitcast.24, s32[1,640]{1,0:T(1,128)} %src_ids.1, s32[1,640]{1,0:T(1,128)} %dst_ids.1, s32[1,640]{1,0:T(1,128)} %rel_ids.1, s32[1,1000]{1,0:T(1,128)} %bitcast.35), custom_call_target="tpu_custom_call" | custom-call | flops 4194304 | bytes 421280 | tf_op jit(solution)/shard_map/pallas_call | solution.py:22
  2.5 3.9 %collective-permute-start = (bf16[432,256]{1,0:T(8,128)(2,1)}, bf16[432,256]{1,0:T(8,128)(2,1)S(1)}, u32[]{:S(2)}, u32[]{:S(2)}) collective-permute-start(bf16[432,256]{1,0:T(8,128)(2,1)} %shard_map.145.own), channel_id=1, source_target_pairs={{0,256},{32,288},{64,320},{96,352},{128,384},{160,416},{192,448},{... | collective-permute-start | bytes 663560 | tf_op jit(solution)/shard_map/ppermute | solution.py:284
  6.4 0.0 copy-start.8
  6.4 0.0 copy-start.6
  6.4 0.0 copy-start.7
  6.5 0.6 copy-done.8
  7.1 0.0 copy-done.6
  7.1 0.0 copy-done.7
  7.1 1.1 %copy-done.1 = f32[512,400]{0,1:T(8,128)S(1)} copy-done((f32[512,400]{0,1:T(8,128)S(1)}, f32[512,400]{0,1:T(8,128)}, u32[]{:S(2)}) %copy-start.1) | copy-done | bytes 819224
  8.3 0.9 %copy-done.4 = bf16[432,256]{1,0:T(8,128)(2,1)S(1)} copy-done((bf16[432,256]{1,0:T(8,128)(2,1)S(1)}, bf16[432,256]{1,0:T(8,128)(2,1)}, u32[]{:S(2)}) %copy-start.4) | copy-done | bytes 221208
  9.2 1.2 %shard_map.146 = (bf16[400,640]{1,0:T(8,128)(2,1)S(1)}, bf16[400,640]{1,0:T(8,128)(2,1)S(1)}, bf16[400,640]{1,0:T(8,128)(2,1)S(1)}, bf16[400,512]{1,0:T(8,128)(2...) custom-call(bf16[432,256]{1,0:T(8,128)(2,1)S(1)} %copy-done.4, f32[400,512]{1,0:T(8,128)S(1)} %bitcast.27, ...), custom_call_target="tpu_custom_call" | custom-call | flops 1073741824 | bytes 1454080 | tf_op jit(solution)/shard_map/pallas_call | solution.py:22
  10.4 4.8 %shard_map.147 = (f32[400,512]{1,0:T(8,128)S(1)}, bf16[400,512]{1,0:T(8,128)(2,1)S(1)}) custom-call(bf16[432,256]{1,0:T(8,128)(2,1)S(1)} %copy-done.5, bf16[432,256]{1,0:T(8,128)(2,1)S(1)} %collective-permute-done.partner, bf16[400,512]{1,0:T(8,128)(2,1)S(1)} %get-tuple-element.22.hot, bf16[400,256]{1,0:T(8,128)(2,1)S(1)} %get-tuple-element.23.rel, ...), custom_call_target="tpu_custom_call" | custom-call | flops 2147483648 | bytes 2592768 | tf_op jit(solution)/shard_map/pallas_call | solution.py:22
  15.2 8.9 %collective-permute-start.1 = (bf16[400,512]{1,0:T(8,128)(2,1)S(1)}, bf16[400,512]{1,0:T(8,128)(2,1)S(1)}, u32[]{:S(2)}, u32[]{:S(2)}) collective-permute-start(bf16[400,512]{1,0:T(8,128)(2,1)S(1)} %get-tuple-element.28), channel_id=1, source_target_pairs={{0,1},{1,0},{2,3},{3,2},{4,5},{5,4},{6,7},{7,6},{8,9},{9,8},{10,11... | collective-permute-start | bytes 1228808 | tf_op jit(solution)/shard_map/ppermute | solution.py:284
  24.1 1.4 %collective-permute-done.1.got = bf16[400,512]{1,0:T(8,128)(2,1)S(1)} collective-permute-done((bf16[400,512]{1,0:T(8,128)(2,1)S(1)}, bf16[400,512]{1,0:T(8,128)(2,1)S(1)}, u32[]{:S(2)}, u32[]{:S(2)}) %collective-permute-start.1) | collective-permute-done | bytes 409632 | tf_op jit(solution)/shard_map/ppermute | solution.py:284
  25.5 0.1 shard_map.148
  25.5 14.1 %all_to_all.33 = bf16[16,32,512]{2,1,0:T(8,128)(2,1)S(1)} all-to-all(bf16[16,32,512]{2,1,0:T(8,128)(2,1)S(1)} %bitcast.23), channel_id=1, replica_groups={{0,2,4,6,8,10,12,14,16,18,20,22,24,26,28,30},{32,34,36,38,40,42,44,46,4..., dimensions={0} | all-to-all | bytes 1048576 | tf_op jit(solution)/shard_map/all_to_all | solution.py:288
  39.7 21.1 %all_to_all.34 = bf16[16,32,256]{2,1,0:T(8,128)(2,1)S(1)} all-to-all(bf16[16,32,256]{2,1,0:T(8,128)(2,1)S(1)} %bitcast.31), channel_id=1, replica_groups={{0,32,64,96,128,160,192,224,256,288,320,352,384,416,448,480},{2,34,66,9..., dimensions={0} | all-to-all | bytes 524288 | tf_op jit(solution)/shard_map/all_to_all | solution.py:288
  60.7 0.1 shard_map.150
  60.8 0.0 copy-start.2
  60.8 0.0 copy-start
  60.8 18.4 %all_to_all.35 = bf16[16,32,768]{2,1,0:T(8,128)(2,1)S(1)} all-to-all(bf16[16,32,768]{2,1,0:T(8,128)(2,1)S(1)} %bitcast.19), channel_id=1, replica_groups={{0,2,4,6,8,10,12,14,16,18,20,22,24,26,28,30},{32,34,36,38,40,42,44,46,4..., dimensions={0} | all-to-all | bytes 1572864 | tf_op jit(solution)/shard_map/all_to_all | solution.py:288
  79.2 7.1 %collective-permute-start.2 = (bf16[512,768]{1,0:T(8,128)(2,1)S(1)}, bf16[512,768]{1,0:T(8,128)(2,1)S(1)}, u32[]{:S(2)}, u32[]{:S(2)}) collective-permute-start(bf16[512,768]{1,0:T(8,128)(2,1)S(1)} %bitcast.20), channel_id=1, source_target_pairs={{0,1},{1,0},{2,3},{3,2},{4,5},{5,4},{6,7},{7,6},{8,9},{9,8},{10,11... | collective-permute-start | bytes 2359304 | tf_op jit(solution)/shard_map/ppermute | solution.py:284
  86.3 1.9 %collective-permute-done.2.other = bf16[512,768]{1,0:T(8,128)(2,1)S(1)} collective-permute-done((bf16[512,768]{1,0:T(8,128)(2,1)S(1)}, bf16[512,768]{1,0:T(8,128)(2,1)S(1)}, u32[]{:S(2)}, u32[]{:S(2)}) %collective-permute-start.2) | collective-permute-done | bytes 786464 | tf_op jit(solution)/shard_map/ppermute | solution.py:284
  88.2 1.4 %shard_map.151 = (f32[400,256]{1,0:T(8,128)}, f32[400,512]{1,0:T(8,128)}, f32[400,256]{1,0:T(8,128)}, f32[1,256]{1,0:T(1,128)}, f32[1,512]{1,0:T(1,128)}, /*index=5*/f32[1,256]{1,0:T(1,128)}) custom-call(bf16[512,768]{1,0:T(8,128)(2,1)S(1)} %bitcast.21, bf16[512,768]{1,0:T(8,128)(2,1)S(1)} %collective-permute-done.2.other, ...), custom_call_target="tpu_custom_call" | custom-call | flops 4194304 | bytes 3227648 | tf_op jit(solution)/shard_map/pallas_call | solution.py:22
  (10 shorter events, 0.1 us)
Async XLA Ops:
  0.6 5.8 %copy-start.3 = (f32[256,400]{0,1:T(8,128)S(1)}, f32[256,400]{0,1:T(8,128)}, u32[]{:S(2)}) copy-start(f32[256,400]{0,1:T(8,128)} %param.14) | copy-start | bytes 1228804
  2.5 8.0 %collective-permute-start = (bf16[432,256]{1,0:T(8,128)(2,1)}, bf16[432,256]{1,0:T(8,128)(2,1)S(1)}, u32[]{:S(2)}, u32[]{:S(2)}) collective-permute-start(bf16[432,256]{1,0:T(8,128)(2,1)} %shard_map.145.own), channel_id=1, source_target_pairs={{0,256},{32,288},{64,320},{96,352},{128,384},{160,416},{192,448},{... | collective-permute-start | bytes 663560 | tf_op jit(solution)/shard_map/ppermute | solution.py:284
  6.4 0.7 copy-start.8
  6.4 0.7 copy-start.6
  6.4 0.7 copy-start.7
  7.1 1.1 %copy-start.1 = (f32[512,400]{0,1:T(8,128)S(1)}, f32[512,400]{0,1:T(8,128)}, u32[]{:S(2)}) copy-start(f32[512,400]{0,1:T(8,128)} %param.12) | copy-start | bytes 2457604
  8.3 0.9 %copy-start.4 = (bf16[432,256]{1,0:T(8,128)(2,1)S(1)}, bf16[432,256]{1,0:T(8,128)(2,1)}, u32[]{:S(2)}) copy-start(bf16[432,256]{1,0:T(8,128)(2,1)} %shard_map.145.own) | copy-start | bytes 663556
  9.2 1.2 %copy-start.5 = (bf16[432,256]{1,0:T(8,128)(2,1)S(1)}, bf16[432,256]{1,0:T(8,128)(2,1)}, u32[]{:S(2)}) copy-start(bf16[432,256]{1,0:T(8,128)(2,1)} %shard_map.145.own) | copy-start | bytes 663556
  15.2 10.2 %collective-permute-start.1 = (bf16[400,512]{1,0:T(8,128)(2,1)S(1)}, bf16[400,512]{1,0:T(8,128)(2,1)S(1)}, u32[]{:S(2)}, u32[]{:S(2)}) collective-permute-start(bf16[400,512]{1,0:T(8,128)(2,1)S(1)} %get-tuple-element.28), channel_id=1, source_target_pairs={{0,1},{1,0},{2,3},{3,2},{4,5},{5,4},{6,7},{7,6},{8,9},{9,8},{10,11... | collective-permute-start | bytes 1228808 | tf_op jit(solution)/shard_map/ppermute | solution.py:284
  60.8 27.4 %copy-start.2 = (f32[512,400]{0,1:T(8,128)S(1)}, f32[512,400]{0,1:T(8,128)}, u32[]{:S(2)}) copy-start(f32[512,400]{0,1:T(8,128)} %param.12) | copy-start | bytes 2457604
  60.8 27.4 %copy-start = (f32[256,400]{0,1:T(8,128)S(1)}, f32[256,400]{0,1:T(8,128)}, u32[]{:S(2)}) copy-start(f32[256,400]{0,1:T(8,128)} %param.10) | copy-start | bytes 1228804
  79.2 9.0 %collective-permute-start.2 = (bf16[512,768]{1,0:T(8,128)(2,1)S(1)}, bf16[512,768]{1,0:T(8,128)(2,1)S(1)}, u32[]{:S(2)}, u32[]{:S(2)}) collective-permute-start(bf16[512,768]{1,0:T(8,128)(2,1)S(1)} %bitcast.20), channel_id=1, source_target_pairs={{0,1},{1,0},{2,3},{3,2},{4,5},{5,4},{6,7},{7,6},{8,9},{9,8},{10,11... | collective-permute-start | bytes 2359304 | tf_op jit(solution)/shard_map/ppermute | solution.py:284

commit v5 on v4

--- a/solution.py
+++ b/solution.py
@@ -174,103 +174,171 @@
         keep[:, :rows] = block_sum
         keep[:, rows:] = hot_sum
         send[:, :half] = kind_sum.astype(BF16)
-        send[:, half:] = jnp.zeros((width, send.shape[1] - half), BF16)
+        send[:, half:rows] = jnp.zeros((width, half), BF16)
+        send[:, rows:] = hot_sum.astype(BF16)
 
     @pl.when(core_of() == 1)
     def _():
         keep[:, :half] = kind_sum
-        keep[:, half:] = jnp.zeros((width, keep.shape[1] - half), F32)
+        keep[:, half:rows] = jnp.zeros((width, half), F32)
+        keep[:, rows:] = hot_sum
         send[:, :rows] = block_sum.astype(BF16)
         send[:, rows:] = hot_sum.astype(BF16)
 
 
-def merge_kernel(keep, got, out):
-    width, lanes = keep.shape
-    half = lanes // 4
-    out[width:, :] = jnp.zeros((out.shape[0] - width, lanes), BF16)
+SIDES = (range(PEERS // 2), range(PEERS // 2, PEERS))
+LANES = 128
+
+
+def cuts(width):
+    whole = width // PEERS
+    last = width // (4 * PEERS)
+    return whole, whole - last, last
+
+
+def slot_rows(width):
+    whole, near, last = cuts(width)
+    sizes = (
+        (2 * whole + 2 * near, 2 * whole + 2 * last),
+        (2 * near, 4 * last),
+        (2 * whole + 4 * near, 4 * whole + 4 * last),
+    )
+    return [-(-max(pair) // 8) * 8 for pair in sizes]
+
+
+def merge_kernel(keep, got, out, sums, packed):
+    width = keep.shape[0]
+    whole, near, last = cuts(width)
+    split = PEERS * near
+    hot = slice(2 * LANES, 4 * LANES)
+
+    def put(block, value):
+        sums[block] = value
+
+    def blank(end):
+        if end < packed.shape[1]:
+            packed[:, end:, :] = jnp.zeros((PEERS, packed.shape[1] - end, LANES), F32)
+
+    for block in range(2):
+        at = slice(hot.start + block * LANES, hot.start + (block + 1) * LANES)
+        put(2 + block, keep[:, at] + got[:, at].astype(F32))
 
     @pl.when(core_of() == 0)
     def _():
-        out[:width, :] = (keep[...] + got[...].astype(F32)).astype(BF16)
+        for block in range(2):
+            at = slice(block * LANES, (block + 1) * LANES)
+            put(block, keep[:, at] + got[:, at].astype(F32))
+            for peer in range(PEERS):
+                low = 2 * whole + block * near
+                packed[peer, low : low + near, :] = sums[2 + block, peer * near : (peer + 1) * near, :]
+        blank(2 * whole + 2 * near)
 
     @pl.when(core_of() == 1)
     def _():
-        out[:width, :half] = got[:, :half]
-        out[:width, half : 2 * half] = keep[:, :half].astype(BF16)
-        out[:width, 2 * half :] = jnp.zeros((width, 2 * half), BF16)
-
-
-def chunk_sum(ref, lanes, peers):
-    rows = ref.shape[0] // PEERS
-    total = 0.0
-    for peer in peers:
-        total = total + ref[peer * rows : (peer + 1) * rows, lanes].astype(F32)
+        put(0, got[:, :LANES].astype(F32))
+        put(1, keep[:, :LANES])
+        for block in range(2):
+            for peer in range(PEERS):
+                low, start = 2 * whole + block * last, split + peer * last
+                packed[peer, low : low + last, :] = sums[2 + block, start : start + last, :]
+        blank(2 * whole + 2 * last)
+
+    for block in range(2):
+        for peer in range(PEERS):
+            low = block * whole
+            packed[peer, low : low + whole, :] = sums[block, peer * whole : (peer + 1) * whole, :]
+    out[...] = packed[...].astype(BF16)
+
+
+def peer_sum(ref, peers):
+    total = ref[peers[0]].astype(F32)
+    for peer in peers[1:]:
+        total = total + ref[peer].astype(F32)
     return total
 
 
-SIDES = (range(PEERS // 2), range(PEERS // 2, PEERS))
-
-
-def first_kernel(got, out, held):
-    rows = got.shape[0] // PEERS
-    lanes = out.shape[1]
-    half = lanes // 2
+def first_kernel(width, got, out, held, total, row):
+    whole, near, last = cuts(width)
+    held[...] = jnp.zeros(held.shape, F32)
+    row[...] = jnp.zeros(row.shape, F32)
 
     @pl.when(core_of() == 0)
     def _():
-        held[:, :lanes] = chunk_sum(got, slice(0, lanes), range(PEERS)).astype(BF16)
-        held[:, lanes:] = jnp.zeros((rows, lanes), BF16)
-        hot = chunk_sum(got, slice(lanes, 2 * lanes), range(PEERS)).astype(BF16)
-        for peer in range(PEERS):
-            out[peer * rows : (peer + 1) * rows, :] = hot
+        total[...] = peer_sum(got, range(PEERS))
+        held[: 2 * whole, :] = total[: 2 * whole, :]
+        row[: 2 * near, :] = total[2 * whole : 2 * whole + 2 * near, :]
 
     @pl.when(core_of() == 1)
     def _():
         for side, peers in enumerate(SIDES):
-            part = chunk_sum(got, slice(0, lanes), peers).astype(BF16)
+            total[...] = peer_sum(got, peers)
             for core in range(2):
-                at = core * lanes + side * half
-                held[:, at : at + half] = part[:, core * half : (core + 1) * half]
-        out[...] = jnp.zeros(out.shape, BF16)
-
-
-def second_kernel(got, held, out):
-    rows = got.shape[0] // PEERS
-    lanes = got.shape[1]
+                at = (2 * core + side) * whole
+                held[at : at + whole, :] = total[core * whole : (core + 1) * whole, :]
+            at = side * 2 * last
+            row[at : at + 2 * last, :] = total[2 * whole : 2 * whole + 2 * last, :]
+
+    value = row[...].astype(BF16)
+    for peer in range(PEERS):
+        out[peer] = value
+
+
+def second_kernel(width, got, held, out, total, row):
+    whole, near, last = cuts(width)
+    row[...] = jnp.zeros(row.shape, F32)
 
     @pl.when(core_of() == 0)
     def _():
-        parts = [held[:, :lanes]]
-        parts += [chunk_sum(got, slice(0, lanes), peers).astype(BF16) for peers in SIDES]
-        for peer in range(PEERS):
-            for at, part in enumerate(parts):
-                out[peer * rows : (peer + 1) * rows, at * lanes : (at + 1) * lanes] = part
+        row[: 2 * whole, :] = held[: 2 * whole, :]
+        for side, peers in enumerate(SIDES):
+            total[...] = peer_sum(got, peers)
+            at = 2 * whole + side * 2 * near
+            row[at : at + 2 * near, :] = total[: 2 * near, :]
 
     @pl.when(core_of() == 1)
     def _():
-        for peer in range(PEERS):
-            out[peer * rows : (peer + 1) * rows, : 2 * lanes] = held[...]
-            out[peer * rows : (peer + 1) * rows, 2 * lanes :] = jnp.zeros((rows, lanes), BF16)
+        total[...] = peer_sum(got, range(PEERS))
+        row[: 4 * whole, :] = held[: 4 * whole, :]
+        row[4 * whole : 4 * whole + 4 * last, :] = total[: 4 * last, :]
+
+    value = row[...].astype(BF16)
+    for peer in range(PEERS):
+        out[peer] = value
 
 
 def update_kernel(mine, other, states, block, hot, rel, *refs):
-    outs, state_outs, helds, state_held, sems = refs[:3], refs[3:6], refs[6:9], refs[9], refs[10]
+    outs, state_outs, helds, state_held = refs[:3], refs[3:6], refs[6:9], refs[9]
+    near_f, far_f, grads, sems = refs[10:]
     width, rows = block.shape
+    whole, near, last = cuts(width)
+    split = PEERS * near
     first = core_of() == 0
     copies = []
     state_held[...] = states[...]
+    near_f[...] = jnp.where(first, mine[...], other[...]).astype(F32)
+    far_f[...] = jnp.where(first, other[...], mine[...]).astype(F32)
     for table, weights in enumerate((block, hot, rel)):
-        for low in range(0, weights.shape[1], rows):
-            at = slice(low, low + rows)
-            if table < 2:
-                lanes = slice(table * rows + low, (table + 1) * rows + low)
-                grads = jnp.where(first, mine[:width, lanes], other[:width, lanes])
-            else:
-                grads = jnp.where(first, other[:width, :rows], mine[:width, rows : 2 * rows])
-            grads = grads.astype(F32)
-            total = states[table : table + 1, at] + jnp.sum(grads * grads, axis=0, keepdims=True) / width
+        for column in range(weights.shape[1] // LANES):
+            for peer in range(PEERS):
+                at = slice(peer * whole, (peer + 1) * whole)
+                low = column * whole
+                if table == 0:
+                    grads[at, :] = near_f[peer, low : low + whole, :]
+                elif table == 2:
+                    high = low + 2 * whole
+                    grads[at, :] = jnp.where(
+                        first, far_f[peer, low : low + whole, :], far_f[peer, high : high + whole, :]
+                    )
+                else:
+                    low = 2 * whole + column * near
+                    grads[peer * near : (peer + 1) * near, :] = near_f[peer, low : low + near, :]
+                    low, start = 4 * whole + column * last, split + peer * last
+                    grads[start : start + last, :] = far_f[peer, low : low + last, :]
+            value = grads[...]
+            at = slice(column * LANES, (column + 1) * LANES)
+            total = states[table : table + 1, at] + jnp.sum(value * value, axis=0, keepdims=True) / width
             state_held[table : table + 1, at] = total
-            helds[table][:, at] = weights[:, at] - grads * (STEP / (jnp.sqrt(total) + EPS))
+            helds[table][:, at] = weights[:, at] - value * (STEP / (jnp.sqrt(total) + EPS))
         state = state_held.at[table : table + 1, : weights.shape[1]]
         copies.append(pltpu.make_async_copy(helds[table], outs[table], sems.at[2 * table]))
         copies.append(pltpu.make_async_copy(state, state_outs[table], sems.at[2 * table + 1]))
@@ -313,8 +381,6 @@
     rows, width = entity_block.shape
     hot_rows = hot_entities.shape[0]
     edges = source_ids.shape[1]
-    padded = -(-width // 256) * 256
-    slot = padded // PEERS
     block_t, hot_t, rel_t = entity_block.T, hot_entities.T, relations.T
     negatives = negative_ids.shape[-1]
     ids = (source_ids, target_ids, relation_ids, negative_ids.reshape(1, -1))
@@ -345,15 +411,30 @@
         1 << 31,
     )
     both = edge_groups(0) + bucket_groups(1)
+    sizes = slot_rows(width)
+    whole = width // PEERS
+    slots = [((PEERS, size, LANES), BF16) for size in sizes]
+    rows_f = [pltpu.VMEM((size, LANES), F32) for size in sizes]
     (mixed,) = call(
-        merge_kernel, [((padded, 2 * rows), BF16)], (keep, flipped(send, "edge", 1))
+        merge_kernel,
+        [slots[0]],
+        (keep, flipped(send, "edge", 1)),
+        scratch=[pltpu.VMEM((4, width, LANES), F32), pltpu.VMEM((PEERS, sizes[0], LANES), F32)],
     )
     mixed = exchanged(mixed, both)
     hot_part, held = call(
-        first_kernel, [((padded, rows), BF16), ((slot, 2 * rows), BF16)], (mixed,)
+        functools.partial(first_kernel, width),
+        [slots[1], ((-(-4 * whole // 8) * 8, LANES), F32)],
+        (mixed,),
+        scratch=[rows_f[0], rows_f[1]],
     )
     hot_part = exchanged(hot_part, bucket_groups(0) + edge_groups(1))
-    (totals,) = call(second_kernel, [((padded, 3 * rows), BF16)], (hot_part, held))
+    (totals,) = call(
+        functools.partial(second_kernel, width),
+        [slots[2]],
+        (hot_part, held),
+        scratch=[rows_f[1], rows_f[2]],
+    )
     mine = exchanged(totals, both)
     other = flipped(mine, "edge", 1)
     tables = (block_t, hot_t, rel_t)
@@ -362,8 +443,8 @@
         [(part.shape, F32) for part in (*tables, *state_rows)],
         (mine, other, states, *tables),
         out_specs=[HBM] * 6,
-        scratch=[pltpu.VMEM(part.shape, F32) for part in (*tables, states)]
-        + [pltpu.SemaphoreType.DMA((6,))],
+        scratch=[pltpu.VMEM(part.shape, F32) for part in (*tables, states, mine, mine)]
+        + [pltpu.VMEM((width, LANES), F32), pltpu.SemaphoreType.DMA((6,))],
     )
     new_block_state, new_hot_state, new_relation_state = [part.reshape(-1) for part in new_states]
     return (

time: 90.1 us -> 85.4 us (0.948)
  blocking collectives: 53.6 us -> 48.1 us
    all_to_all x3, blocking collectives: 53.6 us -> 48.1 us  [exchanged(): lax.all_to_all(x, ('bucket', 'edge'), 0, 0, tiled=True, axis_index_groups...]
where the time goes in v5:
time: 85.4 us; the launch traced here: 85 us
  blocking collectives  48.1 us (56%)
  starting transfers between devices  20.4 us (24%)
  Pallas kernels  10.1 us (12%)
  waiting for transfers between devices  2.87 us (3%)
  local copies, waits for them, and re-layouts  2.78 us (3%)
    all_to_all x3, blocking collectives, exchanged(): lax.all_to_all(x, ('bucket', 'edge'), 0, 0, tiled=True, axis_index_groups...  48.1 us
    ppermute x3, starting transfers between devices, flipped(): lax.ppermute(x, axis, [(i, i ^ bit) for i in range(lax.axis_size(axis))])  20.4 us
    pallas_call x7, Pallas kernels, call(): pl.pallas_call(body, out_shape=[jax.ShapeDtypeStruct(shape, dtype) for sh...  10.1 us
    ppermute x3, waiting for transfers between devices, flipped(): lax.ppermute(x, axis, [(i, i ^ bit) for i in range(lax.axis_size(axis))])  2.87 us
    unnamed x18, local copies, waits for them, and re-layouts  2.78 us
  transfers between devices with their start and end apart: 3, of which 2 were waited for; matrix products, arithmetic and copies ran while one was open for 0% of the time, Pallas kernels for 1%

profile of v5, /device:TPU:1, one launch (start us, length us, event | category | flops | bytes accessed | tf_op | source)
XLA Modules:
  0.0 85.0 jit_solution(8940517817476982330)
XLA Ops:
  0.6 1.8 %shard_map.145.own = bf16[432,256]{1,0:T(8,128)(2,1)} custom-call(f32[400,256]{1,0:T(8,128)} %bitcast.13, s32[1,640]{1,0:T(1,128)} %src_ids.1, s32[1,640]{1,0:T(1,128)} %dst_ids.1, s32[1,640]{1,0:T(1,128)} %rel_ids.1, s32[1,1000]{1,0:T(1,128)} %bitcast.22), custom_call_target="tpu_custom_call" | custom-call | flops 4194304 | bytes 421280 | tf_op jit(solution)/shard_map/pallas_call | solution.py:22
  2.5 3.9 %collective-permute-start = (bf16[432,256]{1,0:T(8,128)(2,1)}, bf16[432,256]{1,0:T(8,128)(2,1)S(1)}, u32[]{:S(2)}, u32[]{:S(2)}) collective-permute-start(bf16[432,256]{1,0:T(8,128)(2,1)} %shard_map.145.own), channel_id=1, source_target_pairs={{0,256},{32,288},{64,320},{96,352},{128,384},{160,416},{192,448},{... | collective-permute-start | bytes 663560 | tf_op jit(solution)/shard_map/ppermute | solution.py:352
  6.4 0.0 copy-start.8
  6.4 0.0 copy-start.6
  6.4 0.0 copy-start.7
  6.5 0.6 copy-done.8
  7.1 0.0 copy-done.6
  7.1 0.0 copy-done.7
  7.1 1.1 %copy-done.1 = f32[512,400]{0,1:T(8,128)S(1)} copy-done((f32[512,400]{0,1:T(8,128)S(1)}, f32[512,400]{0,1:T(8,128)}, u32[]{:S(2)}) %copy-start.1) | copy-done | bytes 819224
  8.3 0.9 %copy-done.4 = bf16[432,256]{1,0:T(8,128)(2,1)S(1)} copy-done((bf16[432,256]{1,0:T(8,128)(2,1)S(1)}, bf16[432,256]{1,0:T(8,128)(2,1)}, u32[]{:S(2)}) %copy-start.4) | copy-done | bytes 221208
  9.2 1.2 %shard_map.146 = (bf16[400,640]{1,0:T(8,128)(2,1)S(1)}, bf16[400,640]{1,0:T(8,128)(2,1)S(1)}, bf16[400,640]{1,0:T(8,128)(2,1)S(1)}, bf16[400,512]{1,0:T(8,128)(2...) custom-call(bf16[432,256]{1,0:T(8,128)(2,1)S(1)} %copy-done.4, f32[400,512]{1,0:T(8,128)S(1)} %bitcast.15, ...), custom_call_target="tpu_custom_call" | custom-call | flops 1073741824 | bytes 1454080 | tf_op jit(solution)/shard_map/pallas_call | solution.py:22
  10.4 4.8 %shard_map.147 = (f32[400,512]{1,0:T(8,128)S(1)}, bf16[400,512]{1,0:T(8,128)(2,1)S(1)}) custom-call(bf16[432,256]{1,0:T(8,128)(2,1)S(1)} %copy-done.5, bf16[432,256]{1,0:T(8,128)(2,1)S(1)} %collective-permute-done.partner, bf16[400,512]{1,0:T(8,128)(2,1)S(1)} %get-tuple-element.22.hot, bf16[400,256]{1,0:T(8,128)(2,1)S(1)} %get-tuple-element.23.rel, ...), custom_call_target="tpu_custom_call" | custom-call | flops 2147483648 | bytes 2592768 | tf_op jit(solution)/shard_map/pallas_call | solution.py:22
  15.3 8.8 %collective-permute-start.1 = (bf16[400,512]{1,0:T(8,128)(2,1)S(1)}, bf16[400,512]{1,0:T(8,128)(2,1)S(1)}, u32[]{:S(2)}, u32[]{:S(2)}) collective-permute-start(bf16[400,512]{1,0:T(8,128)(2,1)S(1)} %get-tuple-element.28), channel_id=1, source_target_pairs={{0,1},{1,0},{2,3},{3,2},{4,5},{5,4},{6,7},{7,6},{8,9},{9,8},{10,11... | collective-permute-start | bytes 1228808 | tf_op jit(solution)/shard_map/ppermute | solution.py:352
  24.1 1.4 %collective-permute-done.1.got = bf16[400,512]{1,0:T(8,128)(2,1)S(1)} collective-permute-done((bf16[400,512]{1,0:T(8,128)(2,1)S(1)}, bf16[400,512]{1,0:T(8,128)(2,1)S(1)}, u32[]{:S(2)}, u32[]{:S(2)}) %collective-permute-start.1) | collective-permute-done | bytes 409632 | tf_op jit(solution)/shard_map/ppermute | solution.py:352
  25.5 0.2 shard_map.148
  25.6 11.7 %all_to_all.15.got = bf16[16,88,128]{2,1,0:T(8,128)(2,1)S(1)} all-to-all(bf16[16,88,128]{2,1,0:T(8,128)(2,1)S(1)} %shard_map.148), channel_id=1, replica_groups={{0,2,4,6,8,10,12,14,16,18,20,22,24,26,28,30},{32,34,36,38,40,42,44,46,4..., dimensions={0} | all-to-all | bytes 720896 | tf_op jit(solution)/shard_map/all_to_all | solution.py:356
  37.4 0.1 shard_map.149
  37.4 21.4 %all_to_all.16.got = bf16[16,40,128]{2,1,0:T(8,128)(2,1)S(1)} all-to-all(bf16[16,40,128]{2,1,0:T(8,128)(2,1)S(1)} %get-tuple-element.29), channel_id=1, replica_groups={{0,32,64,96,128,160,192,224,256,288,320,352,384,416,448,480},{2,34,66,9..., dimensions={0} | all-to-all | bytes 327680 | tf_op jit(solution)/shard_map/all_to_all | solution.py:356
  58.8 0.1 shard_map.150
  58.9 0.0 copy-start
  58.9 15.0 %all_to_all.17.mine = bf16[16,128,128]{2,1,0:T(8,128)(2,1)S(1)} all-to-all(bf16[16,128,128]{2,1,0:T(8,128)(2,1)S(1)} %shard_map.150), channel_id=1, replica_groups={{0,2,4,6,8,10,12,14,16,18,20,22,24,26,28,30},{32,34,36,38,40,42,44,46,4..., dimensions={0} | all-to-all | bytes 1048576 | tf_op jit(solution)/shard_map/all_to_all | solution.py:356
  73.9 7.6 %collective-permute-start.2 = (bf16[16,128,128]{2,1,0:T(8,128)(2,1)S(1)}, bf16[16,128,128]{2,1,0:T(8,128)(2,1)S(1)}, u32[]{:S(2)}, u32[]{:S(2)}) collective-permute-start(bf16[16,128,128]{2,1,0:T(8,128)(2,1)S(1)} %all_to_all.17.mine), channel_id=1, source_target_pairs={{0,1},{1,0},{2,3},{3,2},{4,5},{5,4},{6,7},{7,6},{8,9},{9,8},{10,11... | collective-permute-start | bytes 1572872 | tf_op jit(solution)/shard_map/ppermute | solution.py:352
  81.5 1.5 %collective-permute-done.2.other = bf16[16,128,128]{2,1,0:T(8,128)(2,1)S(1)} collective-permute-done((bf16[16,128,128]{2,1,0:T(8,128)(2,1)S(1)}, bf16[16,128,128]{2,1,0:T(8,128)(2,1)S(1)}, u32[]{:S(2)}, u32[]{:S(2)}) %collective-permute-start.2) | collective-permute-done | bytes 524320 | tf_op jit(solution)/shard_map/ppermute | solution.py:352
  83.1 2.0 %shard_map.151 = (f32[400,256]{1,0:T(8,128)}, f32[400,512]{1,0:T(8,128)}, f32[400,256]{1,0:T(8,128)}, f32[1,256]{1,0:T(1,128)}, f32[1,512]{1,0:T(1,128)}, /*index=5*/f32[1,256]{1,0:T(1,128)}) custom-call(bf16[16,128,128]{2,1,0:T(8,128)(2,1)S(1)} %all_to_all.17.mine, bf16[16,128,128]{2,1,0:T(8,128)(2,1)S(1)} %collective-permute-done.2.other, ...), custom_call_target="tpu_custom_call" | custom-call | flops 4194304 | bytes 2703360 | tf_op jit(solution)/shard_map/pallas_call | solution.py:22
  (10 shorter events, 0.0 us)
Async XLA Ops:
  0.6 5.8 %copy-start.3 = (f32[256,400]{0,1:T(8,128)S(1)}, f32[256,400]{0,1:T(8,128)}, u32[]{:S(2)}) copy-start(f32[256,400]{0,1:T(8,128)} %param.14) | copy-start | bytes 1228804
  2.5 8.0 %collective-permute-start = (bf16[432,256]{1,0:T(8,128)(2,1)}, bf16[432,256]{1,0:T(8,128)(2,1)S(1)}, u32[]{:S(2)}, u32[]{:S(2)}) collective-permute-start(bf16[432,256]{1,0:T(8,128)(2,1)} %shard_map.145.own), channel_id=1, source_target_pairs={{0,256},{32,288},{64,320},{96,352},{128,384},{160,416},{192,448},{... | collective-permute-start | bytes 663560 | tf_op jit(solution)/shard_map/ppermute | solution.py:352
  6.4 0.7 copy-start.8
  6.4 0.7 copy-start.6
  6.4 0.7 copy-start.7
  7.1 1.1 %copy-start.1 = (f32[512,400]{0,1:T(8,128)S(1)}, f32[512,400]{0,1:T(8,128)}, u32[]{:S(2)}) copy-start(f32[512,400]{0,1:T(8,128)} %param.12) | copy-start | bytes 2457604
  8.3 0.9 %copy-start.4 = (bf16[432,256]{1,0:T(8,128)(2,1)S(1)}, bf16[432,256]{1,0:T(8,128)(2,1)}, u32[]{:S(2)}) copy-start(bf16[432,256]{1,0:T(8,128)(2,1)} %shard_map.145.own) | copy-start | bytes 663556
  9.2 1.2 %copy-start.5 = (bf16[432,256]{1,0:T(8,128)(2,1)S(1)}, bf16[432,256]{1,0:T(8,128)(2,1)}, u32[]{:S(2)}) copy-start(bf16[432,256]{1,0:T(8,128)(2,1)} %shard_map.145.own) | copy-start | bytes 663556
  15.3 10.2 %collective-permute-start.1 = (bf16[400,512]{1,0:T(8,128)(2,1)S(1)}, bf16[400,512]{1,0:T(8,128)(2,1)S(1)}, u32[]{:S(2)}, u32[]{:S(2)}) collective-permute-start(bf16[400,512]{1,0:T(8,128)(2,1)S(1)} %get-tuple-element.28), channel_id=1, source_target_pairs={{0,1},{1,0},{2,3},{3,2},{4,5},{5,4},{6,7},{7,6},{8,9},{9,8},{10,11... | collective-permute-start | bytes 1228808 | tf_op jit(solution)/shard_map/ppermute | solution.py:352
  58.8 24.2 %copy-start.2 = (f32[512,400]{0,1:T(8,128)S(1)}, f32[512,400]{0,1:T(8,128)}, u32[]{:S(2)}) copy-start(f32[512,400]{0,1:T(8,128)} %param.12) | copy-start | bytes 2457604
  58.9 24.2 %copy-start = (f32[256,400]{0,1:T(8,128)S(1)}, f32[256,400]{0,1:T(8,128)}, u32[]{:S(2)}) copy-start(f32[256,400]{0,1:T(8,128)} %param.10) | copy-start | bytes 1228804
  73.9 9.2 %collective-permute-start.2 = (bf16[16,128,128]{2,1,0:T(8,128)(2,1)S(1)}, bf16[16,128,128]{2,1,0:T(8,128)(2,1)S(1)}, u32[]{:S(2)}, u32[]{:S(2)}) collective-permute-start(bf16[16,128,128]{2,1,0:T(8,128)(2,1)S(1)} %all_to_all.17.mine), channel_id=1, source_target_pairs={{0,1},{1,0},{2,3},{3,2},{4,5},{5,4},{6,7},{7,6},{8,9},{9,8},{10,11... | collective-permute-start | bytes 1572872 | tf_op jit(solution)/shard_map/ppermute | solution.py:352

commit v6 on v5

--- a/solution.py
+++ b/solution.py
@@ -17,7 +17,7 @@
 HBM = pl.BlockSpec(memory_space=pltpu.HBM)
 
 
-def call(body, outs, args, flops=1 << 22, specs=None, out_specs=None, scratch=(), room=32):
+def call(body, outs, args, flops=1 << 22, specs=None, out_specs=None, scratch=(), room=32, aliases=None):
     moved = sum(a.size * a.dtype.itemsize for a in args)
     return pl.pallas_call(
         body,
@@ -25,14 +25,15 @@
         in_specs=specs or [VMEM] * len(args),
         out_specs=out_specs or [VMEM] * len(outs),
         scratch_shapes=scratch,
+        input_output_aliases=aliases or {},
         compiler_params=pltpu.CompilerParams(vmem_limit_bytes=room << 20),
         cost_estimate=pl.CostEstimate(flops=flops, bytes_accessed=moved, transcendentals=0),
     )(*args)
 
 
 def one_hot(ids, rows):
-    grid = lax.broadcasted_iota(jnp.int32, (rows, ids.shape[1]), 0)
-    return jnp.where(grid == ids, 1.0, 0.0).astype(BF16)
+    grid = lax.broadcasted_iota(jnp.int16, (rows, ids.shape[1]), 0)
+    return jnp.where(grid == ids.astype(jnp.int16), jnp.ones((), BF16), jnp.zeros((), BF16))
 
 
 def mm(a, b):
@@ -97,15 +98,34 @@
     return out
 
 
+def counts(neg_at, rows):
+    ones = jnp.ones((8, neg_at.shape[1]), BF16)
+    return mm_t(ones, one_hot(neg_at, rows))[:1, :]
+
+
 def gather_kernel(
-    negatives, own, hot, rel, block_s, hot_s, rel_s, src_out, rel_out, dst_out, hot_bf, rel_bf, states
+    negatives,
+    own,
+    hot,
+    rel,
+    block_s,
+    hot_s,
+    rel_s,
+    src_out,
+    rel_out,
+    dst_out,
+    query_out,
+    hot_bf,
+    rel_bf,
+    states,
 ):
     width, rows = hot.shape[0], own.shape[1]
     states[...] = jnp.zeros(states.shape, F32)
+    src_at, dst_at, rel_at, neg_at = unpack(own, width, src_out.shape[1], negatives)
+    states[4:5, :rows] = counts(neg_at, rows)
     for at, state in enumerate((block_s, hot_s, rel_s)):
         states[at : at + 1, : state.shape[1]] = state[...]
     hot_rows = hot.shape[1]
-    src_at, dst_at, rel_at, _ = unpack(own, width, src_out.shape[1], negatives)
     hot_bf[...] = hot[...].astype(BF16)
     rel_bf[...] = rel[...].astype(BF16)
     src_out[...] = (
@@ -113,29 +133,27 @@
         + mm(hot_bf[...], one_hot(src_at - rows, hot_rows))
     ).astype(BF16)
     rel_out[...] = mm(rel_bf[...], one_hot(rel_at, rel.shape[1])).astype(BF16)
+    query_out[...] = (src_out[...].astype(F32) * rel_out[...].astype(F32)).astype(BF16)
     dst_out[...] = mm(hot_bf[...], one_hot(dst_at - rows, hot_rows)).astype(BF16)
 
 
-def edge_grads(partner, src, rel, dst, neg_at):
-    query = (src * rel).astype(BF16)
+def edge_grads(partner, src, rel, dst, query, count):
     query_f = query.astype(F32)
     positive = jnp.sum(query_f * dst, axis=0, keepdims=True)
     pos_grad = -1.0 / (1.0 + jnp.exp(positive))
     scores = mm(partner.T, query)
     sig = (1.0 / (1.0 + jnp.exp(-scores))).astype(BF16)
-    named = one_hot(neg_at, partner.shape[1])
-    count = mm_t(jnp.ones((8, neg_at.shape[1]), BF16), named)[:1, :]
-    scaled = partner.astype(F32) * count
-    high = scaled.astype(BF16)
-    low = (scaled - high.astype(F32)).astype(BF16)
-    query_grad = pos_grad * dst + mm(high, sig) + mm(low, sig)
+    weighed = (partner.astype(F32) * count).astype(BF16)
+    query_grad = pos_grad * dst + mm(weighed, sig)
     src_grad = (query_grad * rel).astype(BF16)
     kind_grad = (query_grad * src).astype(BF16)
     dst_grad = (pos_grad * query_f).astype(BF16)
-    return query, sig, count, src_grad, kind_grad, dst_grad
-
-
-def grad_kernel(negatives, own, partner, hot, rel, src, rel_rows, dst_hot, keep, send):
+    return sig, src_grad, kind_grad, dst_grad
+
+
+def grad_kernel(
+    negatives, own, partner, hot, rel, src, rel_rows, dst_hot, near_query, states, keep, send
+):
     width, edges = src.shape
     rows, hot_rows = own.shape[1], hot.shape[1]
     half = rows // 2
@@ -145,10 +163,15 @@
     def hot_hits(at):
         return one_hot(at - rows - side * rows, rows)
 
-    near_src, near_dst, near_rel, near_neg = unpack(own, width, edges, negatives)
+    near_src, near_dst, near_rel, _ = unpack(own, width, edges, negatives)
     dst = mm(partner_table, one_hot(near_dst, rows)) + dst_hot[...].astype(F32)
-    _, _, _, near_src_grad, near_kind_grad, near_dst_grad = edge_grads(
-        partner_table, src[...].astype(F32), rel_rows[...].astype(F32), dst, near_neg
+    _, near_src_grad, near_kind_grad, near_dst_grad = edge_grads(
+        partner_table,
+        src[...].astype(F32),
+        rel_rows[...].astype(F32),
+        dst,
+        near_query[...],
+        states[4:5, :rows],
     )
     far_src, far_dst, far_rel, far_neg = unpack(partner, width, edges, negatives)
     ends = jnp.concatenate([far_src, far_dst], axis=1)
@@ -156,8 +179,10 @@
     src_rows = mm(partner_table, one_hot(far_src, rows)) + from_hot[:, :edges]
     dst_rows = mm(own_table, one_hot(far_dst, rows)) + from_hot[:, edges:]
     kind_rows = mm(rel[...], one_hot(far_rel, rel.shape[1]))
-    query, sig, count, far_src_grad, far_kind_grad, far_dst_grad = edge_grads(
-        own_table, src_rows, kind_rows, dst_rows, far_neg
+    query = (src_rows * kind_rows).astype(BF16)
+    count = counts(far_neg, rows)
+    sig, far_src_grad, far_kind_grad, far_dst_grad = edge_grads(
+        own_table, src_rows, kind_rows, dst_rows, query, count
     )
     cold = jnp.concatenate([near_src_grad, far_dst_grad], axis=1)
     cold_at = jnp.concatenate([near_src, far_dst], axis=1)
@@ -306,46 +331,108 @@
         out[peer] = value
 
 
-def update_kernel(mine, other, states, block, hot, rel, *refs):
-    outs, state_outs, helds, state_held = refs[:3], refs[3:6], refs[6:9], refs[9]
-    near_f, far_f, grads, sems = refs[10:]
-    width, rows = block.shape
+def stepped(table, column, grads, weights, states, held, state_held):
+    at = slice(column * LANES, (column + 1) * LANES)
+    total = jnp.sum(grads * grads, axis=0, keepdims=True) / grads.shape[0]
+    total = states[table : table + 1, at] + total
+    state_held[table : table + 1, at] = total
+    held[:, at] = weights[:, at] - grads * (STEP / (jnp.sqrt(total) + EPS))
+
+
+def written(table, held, state_held, out, state_out, sems):
+    state = state_held.at[table : table + 1, : held.shape[1]]
+    copies = [
+        pltpu.make_async_copy(held, out, sems.at[2 * table]),
+        pltpu.make_async_copy(state, state_out, sems.at[2 * table + 1]),
+    ]
+    for copy in copies:
+        copy.start()
+    return copies
+
+
+def near_hot(rows_f, hot_rows, whole, near):
+    for column in range(hot_rows.shape[0]):
+        for peer in range(PEERS):
+            low = 2 * whole + column * near
+            hot_rows[column, peer * near : (peer + 1) * near, :] = rows_f[peer, low : low + near, :]
+
+
+def last_hot(rows_f, hot_rows, whole, near, last):
+    for column in range(hot_rows.shape[0]):
+        for peer in range(PEERS):
+            low, start = 4 * whole + column * last, PEERS * near + peer * last
+            hot_rows[column, start : start + last, :] = rows_f[peer, low : low + last, :]
+
+
+def whole_rows(rows_f, grads, whole, low):
+    for peer in range(PEERS):
+        grads[peer * whole : (peer + 1) * whole, :] = rows_f[peer, low : low + whole, :]
+    return grads[...]
+
+
+def early_kernel(
+    mine, states, block, rel, new_b, new_bs, new_r, new_rs, hot_rows, rows_f, held, state_held, grads, sems
+):
+    whole, near, last = cuts(block.shape[0])
+    rows_f[...] = mine[...].astype(F32)
+
+    @pl.when(core_of() == 0)
+    def _():
+        for column in range(2):
+            value = whole_rows(rows_f, grads, whole, column * whole)
+            stepped(0, column, value, block, states, held, state_held)
+        copies = written(0, held, state_held, new_b, new_bs, sems)
+        near_hot(rows_f, hot_rows, whole, near)
+        for copy in copies:
+            copy.wait()
+
+    @pl.when(core_of() == 1)
+    def _():
+        for column in range(2):
+            value = whole_rows(rows_f, grads, whole, (2 + column) * whole)
+            stepped(2, column, value, rel, states, held, state_held)
+        copies = written(2, held, state_held, new_r, new_rs, sems)
+        last_hot(rows_f, hot_rows, whole, near, last)
+        for copy in copies:
+            copy.wait()
+
+
+def late_kernel(
+    other, states, block, hot, rel, part, in_b, in_bs, in_r, in_rs, new_b, new_bs, new_r, new_rs, new_h, new_hs, *refs
+):
+    del in_b, in_bs, in_r, in_rs
+    rows_f, hot_rows, held_hot, held, state_held, grads, sems = refs
+    width = block.shape[0]
     whole, near, last = cuts(width)
     split = PEERS * near
-    first = core_of() == 0
-    copies = []
-    state_held[...] = states[...]
-    near_f[...] = jnp.where(first, mine[...], other[...]).astype(F32)
-    far_f[...] = jnp.where(first, other[...], mine[...]).astype(F32)
-    for table, weights in enumerate((block, hot, rel)):
-        for column in range(weights.shape[1] // LANES):
-            for peer in range(PEERS):
-                at = slice(peer * whole, (peer + 1) * whole)
-                low = column * whole
-                if table == 0:
-                    grads[at, :] = near_f[peer, low : low + whole, :]
-                elif table == 2:
-                    high = low + 2 * whole
-                    grads[at, :] = jnp.where(
-                        first, far_f[peer, low : low + whole, :], far_f[peer, high : high + whole, :]
-                    )
-                else:
-                    low = 2 * whole + column * near
-                    grads[peer * near : (peer + 1) * near, :] = near_f[peer, low : low + near, :]
-                    low, start = 4 * whole + column * last, split + peer * last
-                    grads[start : start + last, :] = far_f[peer, low : low + last, :]
-            value = grads[...]
-            at = slice(column * LANES, (column + 1) * LANES)
-            total = states[table : table + 1, at] + jnp.sum(value * value, axis=0, keepdims=True) / width
-            state_held[table : table + 1, at] = total
-            helds[table][:, at] = weights[:, at] - value * (STEP / (jnp.sqrt(total) + EPS))
-        state = state_held.at[table : table + 1, : weights.shape[1]]
-        copies.append(pltpu.make_async_copy(helds[table], outs[table], sems.at[2 * table]))
-        copies.append(pltpu.make_async_copy(state, state_outs[table], sems.at[2 * table + 1]))
-        copies[-2].start()
-        copies[-1].start()
-    for copy in copies:
-        copy.wait()
+    rows_f[...] = other[...].astype(F32)
+
+    def hot_steps():
+        for column in range(hot_rows.shape[0]):
+            stepped(1, column, hot_rows[column], hot, states, held_hot, state_held)
+        return written(1, held_hot, state_held, new_h, new_hs, sems)
+
+    @pl.when(core_of() == 0)
+    def _():
+        hot_rows[:, :split, :] = part[:, :split, :]
+        last_hot(rows_f, hot_rows, whole, near, last)
+        copies = hot_steps()
+        for column in range(2):
+            value = whole_rows(rows_f, grads, whole, column * whole)
+            stepped(2, column, value, rel, states, held, state_held)
+        for copy in copies + written(2, held, state_held, new_r, new_rs, sems):
+            copy.wait()
+
+    @pl.when(core_of() == 1)
+    def _():
+        hot_rows[:, split:, :] = part[:, split:, :]
+        near_hot(rows_f, hot_rows, whole, near)
+        copies = hot_steps()
+        for column in range(2):
+            value = whole_rows(rows_f, grads, whole, column * whole)
+            stepped(0, column, value, block, states, held, state_held)
+        for copy in copies + written(0, held, state_held, new_b, new_bs, sems):
+            copy.wait()
 
 
 def flipped(x, axis, bit):
@@ -397,9 +484,9 @@
     )
     partner = flipped(own, "bucket", lax.axis_size("bucket") // 2)
     state_rows = [state.reshape(1, -1) for state in (block_state, hot_state, relation_state)]
-    src, rel_rows, dst_hot, hot_bf, rel_bf, states = call(
+    src, rel_rows, dst_hot, near_query, hot_bf, rel_bf, states = call(
         functools.partial(gather_kernel, negatives),
-        [((width, edges), BF16)] * 3
+        [((width, edges), BF16)] * 4
         + [((width, hot_rows), BF16), ((width, rows), BF16), ((8, hot_rows), F32)],
         (own, hot_t, rel_t, *state_rows),
         1 << 30,
@@ -407,7 +494,7 @@
     keep, send = call(
         functools.partial(grad_kernel, negatives),
         [((width, 2 * rows), F32), ((width, 2 * rows), BF16)],
-        (own, partner, hot_bf, rel_bf, src, rel_rows, dst_hot),
+        (own, partner, hot_bf, rel_bf, src, rel_rows, dst_hot, near_query, states),
         1 << 31,
     )
     both = edge_groups(0) + bucket_groups(1)
@@ -437,16 +524,30 @@
     )
     mine = exchanged(totals, both)
     other = flipped(mine, "edge", 1)
-    tables = (block_t, hot_t, rel_t)
-    new_block, new_hot, new_relations, *new_states = call(
-        update_kernel,
-        [(part.shape, F32) for part in (*tables, *state_rows)],
-        (mine, other, states, *tables),
+    block_s, hot_s, rel_s = [(part.shape, F32) for part in state_rows]
+    block_like, hot_like = (block_t.shape, F32), (hot_t.shape, F32)
+    columns = ((hot_rows // LANES, width, LANES), F32)
+    held = [pltpu.VMEM(block_t.shape, F32), pltpu.VMEM(states.shape, F32)]
+    held += [pltpu.VMEM((width, LANES), F32), pltpu.SemaphoreType.DMA((6,))]
+    *done, part = call(
+        early_kernel,
+        [block_like, block_s, block_like, rel_s, columns],
+        (mine, states, block_t, rel_t),
+        out_specs=[HBM] * 4 + [VMEM],
+        scratch=[pltpu.VMEM(mine.shape, F32)] + held,
+    )
+    new_block, new_block_state, new_relations, new_relation_state, new_hot, new_hot_state = call(
+        late_kernel,
+        [block_like, block_s, block_like, rel_s, hot_like, hot_s],
+        (other, states, block_t, hot_t, rel_t, part, *done),
+        specs=[VMEM] * 6 + [HBM] * 4,
         out_specs=[HBM] * 6,
-        scratch=[pltpu.VMEM(part.shape, F32) for part in (*tables, states, mine, mine)]
-        + [pltpu.VMEM((width, LANES), F32), pltpu.SemaphoreType.DMA((6,))],
-    )
-    new_block_state, new_hot_state, new_relation_state = [part.reshape(-1) for part in new_states]
+        scratch=[pltpu.VMEM(mine.shape, F32), pltpu.VMEM(*columns), pltpu.VMEM(*hot_like)] + held,
+        aliases={6 + at: at for at in range(4)},
+    )
+    new_block_state, new_hot_state, new_relation_state = [
+        part.reshape(-1) for part in (new_block_state, new_hot_state, new_relation_state)
+    ]
     return (
         new_block.T,
         new_block_state,

time: 85.4 us -> 84.4 us (0.988)
  waiting for transfers between devices: 2.87 us -> 1.8 us
    ppermute x3, waiting for transfers between devices: 2.87 us -> 1.8 us  [flipped(): lax.ppermute(x, axis, [(i, i ^ bit) for i in range(lax.axis_size(axis))])]
    pallas_call x7 -> x8, Pallas kernels: 10.1 us -> 10 us  [call(): pl.pallas_call(body, out_shape=[jax.ShapeDtypeStruct(shape, dtype) for sh...]
  transfers between devices with their start and end apart: 3 -> 3, of which waited for: 2 -> 2; matrix products, arithmetic and copies ran while one was open for 0% -> 0% of each run, Pallas kernels for 1% -> 3%
where the time goes in v6:
time: 84.4 us; the launch traced here: 84 us
  blocking collectives  48.1 us (57%)
  starting transfers between devices  20.4 us (24%)
  Pallas kernels  10 us (12%)
  local copies, waits for them, and re-layouts  2.78 us (3%)
  waiting for transfers between devices  1.8 us (2%)
    all_to_all x3, blocking collectives, exchanged(): lax.all_to_all(x, ('bucket', 'edge'), 0, 0, tiled=True, axis_index_groups...  48.1 us
    ppermute x3, starting transfers between devices, flipped(): lax.ppermute(x, axis, [(i, i ^ bit) for i in range(lax.axis_size(axis))])  20.4 us
    pallas_call x8, Pallas kernels, call(): pl.pallas_call(body, out_shape=[jax.ShapeDtypeStruct(shape, dtype) for sh...  10 us
    unnamed x18, local copies, waits for them, and re-layouts  2.78 us
    ppermute x3, waiting for transfers between devices, flipped(): lax.ppermute(x, axis, [(i, i ^ bit) for i in range(lax.axis_size(axis))])  1.8 us
  transfers between devices with their start and end apart: 3, of which 2 were waited for; matrix products, arithmetic and copies ran while one was open for 0% of the time, Pallas kernels for 3%

profile of v6, /device:TPU:1, one launch (start us, length us, event | category | flops | bytes accessed | tf_op | source)
XLA Modules:
  0.0 84.0 jit_solution(11562662920717110772)
XLA Ops:
  0.6 1.8 %shard_map.145.own = bf16[432,256]{1,0:T(8,128)(2,1)} custom-call(f32[400,256]{1,0:T(8,128)} %bitcast.13, s32[1,640]{1,0:T(1,128)} %src_ids.1, s32[1,640]{1,0:T(1,128)} %dst_ids.1, s32[1,640]{1,0:T(1,128)} %rel_ids.1, s32[1,1000]{1,0:T(1,128)} %bitcast.26), custom_call_target="tpu_custom_call" | custom-call | flops 4194304 | bytes 421280 | tf_op jit(solution)/shard_map/pallas_call | solution.py:22
  2.5 3.9 %collective-permute-start = (bf16[432,256]{1,0:T(8,128)(2,1)}, bf16[432,256]{1,0:T(8,128)(2,1)S(1)}, u32[]{:S(2)}, u32[]{:S(2)}) collective-permute-start(bf16[432,256]{1,0:T(8,128)(2,1)} %shard_map.145.own), channel_id=1, source_target_pairs={{0,256},{32,288},{64,320},{96,352},{128,384},{160,416},{192,448},{... | collective-permute-start | bytes 663560 | tf_op jit(solution)/shard_map/ppermute | solution.py:439
  6.4 0.0 copy-start.8
  6.4 0.0 copy-start.7
  6.5 0.6 copy-done.8
  7.1 0.0 copy-done.6
  7.1 0.0 copy-done.7
  7.1 1.1 %copy-done.2 = f32[512,400]{0,1:T(8,128)S(1)} copy-done((f32[512,400]{0,1:T(8,128)S(1)}, f32[512,400]{0,1:T(8,128)}, u32[]{:S(2)}) %copy-start.2) | copy-done | bytes 819224
  8.3 0.9 %copy-done.4 = bf16[432,256]{1,0:T(8,128)(2,1)S(1)} copy-done((bf16[432,256]{1,0:T(8,128)(2,1)S(1)}, bf16[432,256]{1,0:T(8,128)(2,1)}, u32[]{:S(2)}) %copy-start.4) | copy-done | bytes 221208
  9.2 1.3 %shard_map.146 = (bf16[400,640]{1,0:T(8,128)(2,1)S(1)}, bf16[400,640]{1,0:T(8,128)(2,1)S(1)}, bf16[400,640]{1,0:T(8,128)(2,1)S(1)}, bf16[400,640]{1,0:T(8,128)(2...) custom-call(bf16[432,256]{1,0:T(8,128)(2,1)S(1)} %copy-done.4, ...), custom_call_target="tpu_custom_call" | custom-call | flops 1073741824 | bytes 1454080 | tf_op jit(solution)/shard_map/pallas_call | solution.py:22
  10.5 4.1 %shard_map.147 = (f32[400,512]{1,0:T(8,128)S(1)}, bf16[400,512]{1,0:T(8,128)(2,1)S(1)}) custom-call(bf16[432,256]{1,0:T(8,128)(2,1)S(1)} %copy-done.5, bf16[432,256]{1,0:T(8,128)(2,1)S(1)} %collective-permute-done.partner, bf16[400,512]{1,0:T(8,128)(2,1)S(1)} %get-tuple-element.28.hot, bf16[400,256]{1,0:T(8,128)(2,1)S(1)} %get-tuple-element.29.rel, ...), custom_call_target="tpu_custom_call" | custom-call | flops 2147483648 | bytes 3121152 | tf_op jit(solution)/shard_map/pallas_call | solution.py:22
  14.6 8.7 %collective-permute-start.1 = (bf16[400,512]{1,0:T(8,128)(2,1)S(1)}, bf16[400,512]{1,0:T(8,128)(2,1)S(1)}, u32[]{:S(2)}, u32[]{:S(2)}) collective-permute-start(bf16[400,512]{1,0:T(8,128)(2,1)S(1)} %get-tuple-element.36), channel_id=1, source_target_pairs={{0,1},{1,0},{2,3},{3,2},{4,5},{5,4},{6,7},{7,6},{8,9},{9,8},{10,11... | collective-permute-start | bytes 1228808 | tf_op jit(solution)/shard_map/ppermute | solution.py:439
  23.3 1.4 %collective-permute-done.1.got = bf16[400,512]{1,0:T(8,128)(2,1)S(1)} collective-permute-done((bf16[400,512]{1,0:T(8,128)(2,1)S(1)}, bf16[400,512]{1,0:T(8,128)(2,1)S(1)}, u32[]{:S(2)}, u32[]{:S(2)}) %collective-permute-start.1) | collective-permute-done | bytes 409632 | tf_op jit(solution)/shard_map/ppermute | solution.py:439
  24.7 0.2 shard_map.148
  24.9 11.8 %all_to_all.15.got = bf16[16,88,128]{2,1,0:T(8,128)(2,1)S(1)} all-to-all(bf16[16,88,128]{2,1,0:T(8,128)(2,1)S(1)} %shard_map.148), channel_id=1, replica_groups={{0,2,4,6,8,10,12,14,16,18,20,22,24,26,28,30},{32,34,36,38,40,42,44,46,4..., dimensions={0} | all-to-all | bytes 720896 | tf_op jit(solution)/shard_map/all_to_all | solution.py:443
  36.6 0.1 shard_map.149
  36.7 21.4 %all_to_all.16.got = bf16[16,40,128]{2,1,0:T(8,128)(2,1)S(1)} all-to-all(bf16[16,40,128]{2,1,0:T(8,128)(2,1)S(1)} %get-tuple-element.37), channel_id=1, replica_groups={{0,32,64,96,128,160,192,224,256,288,320,352,384,416,448,480},{2,34,66,9..., dimensions={0} | all-to-all | bytes 327680 | tf_op jit(solution)/shard_map/all_to_all | solution.py:443
  58.1 0.1 shard_map.150
  58.2 0.0 copy-start
  58.2 15.0 %all_to_all.17.mine = bf16[16,128,128]{2,1,0:T(8,128)(2,1)S(1)} all-to-all(bf16[16,128,128]{2,1,0:T(8,128)(2,1)S(1)} %shard_map.150), channel_id=1, replica_groups={{0,2,4,6,8,10,12,14,16,18,20,22,24,26,28,30},{32,34,36,38,40,42,44,46,4..., dimensions={0} | all-to-all | bytes 1048576 | tf_op jit(solution)/shard_map/all_to_all | solution.py:443
  73.2 7.8 %collective-permute-start.2 = (bf16[16,128,128]{2,1,0:T(8,128)(2,1)S(1)}, bf16[16,128,128]{2,1,0:T(8,128)(2,1)S(1)}, u32[]{:S(2)}, u32[]{:S(2)}) collective-permute-start(bf16[16,128,128]{2,1,0:T(8,128)(2,1)S(1)} %all_to_all.17.mine), channel_id=1, source_target_pairs={{0,1},{1,0},{2,3},{3,2},{4,5},{5,4},{6,7},{7,6},{8,9},{9,8},{10,11... | collective-permute-start | bytes 1572872 | tf_op jit(solution)/shard_map/ppermute | solution.py:439
  80.9 1.1 %shard_map.151 = (f32[400,256]{1,0:T(8,128)}, f32[1,256]{1,0:T(1,128)}, f32[400,256]{1,0:T(8,128)}, f32[1,256]{1,0:T(1,128)}, f32[4,400,128]{2,1,0:T(8,128)S(1)}) custom-call(bf16[16,128,128]{2,1,0:T(8,128)(2,1)S(1)} %all_to_all.17.mine, f32[8,512]{1,0:T(8,128)S(1)} %get-tuple-element.34.states, f32[400,256]{1,0:T(8,128)S(1)} %bitcast.14, ...), custom_call_target="tpu_custom_call" | custom-call | flops 4194304 | bytes 1359872 | tf_op jit(solution)/shard_map/pallas_call | solution.py:22
  82.0 0.4 collective-permute-done.2.other
  82.4 1.5 %shard_map.152 = (f32[400,256]{1,0:T(8,128)}, f32[1,256]{1,0:T(1,128)}, f32[400,256]{1,0:T(8,128)}, f32[1,256]{1,0:T(1,128)}, f32[400,512]{1,0:T(8,128)}, /*index=5*/f32[1,512]{1,0:T(1,128)}) custom-call(bf16[16,128,128]{2,1,0:T(8,128)(2,1)S(1)} %collective-permute-done.2.other, ...), custom_call_target="tpu_custom_call", output_to_operand_aliasing={{0}: (6, {}), {1}: (7, {}), {2}: (8, {}), {3}: (9, {})} | custom-call | flops 4194304 | bytes 3819520 | tf_op jit(solution)/shard_map/pallas_call | solution.py:22
  (11 shorter events, 0.0 us)
Async XLA Ops:
  0.6 5.8 %copy-start.1 = (f32[256,400]{0,1:T(8,128)S(1)}, f32[256,400]{0,1:T(8,128)}, u32[]{:S(2)}) copy-start(f32[256,400]{0,1:T(8,128)} %param.14) | copy-start | bytes 1228804
  2.5 8.1 %collective-permute-start = (bf16[432,256]{1,0:T(8,128)(2,1)}, bf16[432,256]{1,0:T(8,128)(2,1)S(1)}, u32[]{:S(2)}, u32[]{:S(2)}) collective-permute-start(bf16[432,256]{1,0:T(8,128)(2,1)} %shard_map.145.own), channel_id=1, source_target_pairs={{0,256},{32,288},{64,320},{96,352},{128,384},{160,416},{192,448},{... | collective-permute-start | bytes 663560 | tf_op jit(solution)/shard_map/ppermute | solution.py:439
  6.4 0.7 copy-start.8
  6.4 0.7 copy-start.6
  6.4 0.7 copy-start.7
  7.1 1.1 %copy-start.2 = (f32[512,400]{0,1:T(8,128)S(1)}, f32[512,400]{0,1:T(8,128)}, u32[]{:S(2)}) copy-start(f32[512,400]{0,1:T(8,128)} %param.12) | copy-start | bytes 2457604
  8.3 0.9 %copy-start.4 = (bf16[432,256]{1,0:T(8,128)(2,1)S(1)}, bf16[432,256]{1,0:T(8,128)(2,1)}, u32[]{:S(2)}) copy-start(bf16[432,256]{1,0:T(8,128)(2,1)} %shard_map.145.own) | copy-start | bytes 663556
  9.2 1.3 %copy-start.5 = (bf16[432,256]{1,0:T(8,128)(2,1)S(1)}, bf16[432,256]{1,0:T(8,128)(2,1)}, u32[]{:S(2)}) copy-start(bf16[432,256]{1,0:T(8,128)(2,1)} %shard_map.145.own) | copy-start | bytes 663556
  14.6 10.1 %collective-permute-start.1 = (bf16[400,512]{1,0:T(8,128)(2,1)S(1)}, bf16[400,512]{1,0:T(8,128)(2,1)S(1)}, u32[]{:S(2)}, u32[]{:S(2)}) collective-permute-start(bf16[400,512]{1,0:T(8,128)(2,1)S(1)} %get-tuple-element.36), channel_id=1, source_target_pairs={{0,1},{1,0},{2,3},{3,2},{4,5},{5,4},{6,7},{7,6},{8,9},{9,8},{10,11... | collective-permute-start | bytes 1228808 | tf_op jit(solution)/shard_map/ppermute | solution.py:439
  58.2 22.8 %copy-start = (f32[256,400]{0,1:T(8,128)S(1)}, f32[256,400]{0,1:T(8,128)}, u32[]{:S(2)}) copy-start(f32[256,400]{0,1:T(8,128)} %param.10) | copy-start | bytes 1228804
  73.2 9.3 %copy-start.3 = (f32[512,400]{0,1:T(8,128)S(1)}, f32[512,400]{0,1:T(8,128)}, u32[]{:S(2)}) copy-start(f32[512,400]{0,1:T(8,128)} %param.12) | copy-start | bytes 2457604
  73.2 9.3 %collective-permute-start.2 = (bf16[16,128,128]{2,1,0:T(8,128)(2,1)S(1)}, bf16[16,128,128]{2,1,0:T(8,128)(2,1)S(1)}, u32[]{:S(2)}, u32[]{:S(2)}) collective-permute-start(bf16[16,128,128]{2,1,0:T(8,128)(2,1)S(1)} %all_to_all.17.mine), channel_id=1, source_target_pairs={{0,1},{1,0},{2,3},{3,2},{4,5},{5,4},{6,7},{7,6},{8,9},{9,8},{10,11... | collective-permute-start | bytes 1572872 | tf_op jit(solution)/shard_map/ppermute | solution.py:439

commit v7 on v6

--- a/solution.py
+++ b/solution.py
@@ -17,7 +17,7 @@
 HBM = pl.BlockSpec(memory_space=pltpu.HBM)
 
 
-def call(body, outs, args, flops=1 << 22, specs=None, out_specs=None, scratch=(), room=32, aliases=None):
+def call(body, outs, args, flops=1 << 22, specs=None, out_specs=None, scratch=(), aliases=None):
     moved = sum(a.size * a.dtype.itemsize for a in args)
     return pl.pallas_call(
         body,
@@ -26,7 +26,7 @@
         out_specs=out_specs or [VMEM] * len(outs),
         scratch_shapes=scratch,
         input_output_aliases=aliases or {},
-        compiler_params=pltpu.CompilerParams(vmem_limit_bytes=room << 20),
+        compiler_params=pltpu.CompilerParams(vmem_limit_bytes=32 << 20),
         cost_estimate=pl.CostEstimate(flops=flops, bytes_accessed=moved, transcendentals=0),
     )(*args)
 
@@ -475,9 +475,8 @@
     (own,) = call(
         pack_kernel,
         [((width + id_height, rows), BF16)],
-        (block_t, *ids),
+        [pltpu.with_memory_space_constraint(part, pltpu.HBM) for part in (block_t, *ids)],
         specs=[HBM] * 5,
-        room=63,
         scratch=[pltpu.VMEM((width, rows), F32)]
         + [pltpu.VMEM(part.shape, jnp.int32) for part in ids]
         + [pltpu.SemaphoreType.DMA((5,)), pltpu.VMEM((id_height, rows), F32)],

time: 84.4 us -> 83.5 us (0.989)
  local copies, waits for them, and re-layouts: 2.78 us -> 1.84 us
    unnamed x18 -> x14, local copies, waits for them, and re-layouts: 2.78 us -> 1.84 us
  transfers between devices with their start and end apart: 3 -> 3, of which waited for: 2 -> 3; matrix products, arithmetic and copies ran while one was open for 0% -> 0% of each run, Pallas kernels for 3% -> 3%
where the time goes in v7:
time: 83.5 us; the launch traced here: 83.1 us
  blocking collectives  48.1 us (58%)
  starting transfers between devices  21.1 us (25%)
  Pallas kernels  9.38 us (11%)
  waiting for transfers between devices  1.93 us (2%)
  local copies, waits for them, and re-layouts  1.84 us (2%)
    all_to_all x3, blocking collectives, exchanged(): lax.all_to_all(x, ('bucket', 'edge'), 0, 0, tiled=True, axis_index_groups...  48.1 us
    ppermute x3, starting transfers between devices, flipped(): lax.ppermute(x, axis, [(i, i ^ bit) for i in range(lax.axis_size(axis))])  21.1 us
    pallas_call x8, Pallas kernels, call(): pl.pallas_call(body, out_shape=[jax.ShapeDtypeStruct(shape, dtype) for sh...  9.38 us
    ppermute x3, waiting for transfers between devices, flipped(): lax.ppermute(x, axis, [(i, i ^ bit) for i in range(lax.axis_size(axis))])  1.93 us
    unnamed x14, local copies, waits for them, and re-layouts  1.84 us
  transfers between devices with their start and end apart: 3, of which 3 were waited for; matrix products, arithmetic and copies ran while one was open for 0% of the time, Pallas kernels for 3%

profile of v7, /device:TPU:1, one launch (start us, length us, event | category | flops | bytes accessed | tf_op | source)
XLA Modules:
  0.0 83.1 jit_solution(12022377527228727693)
XLA Ops:
  0.6 1.1 %shard_map.145.own = bf16[432,256]{1,0:T(8,128)(2,1)S(1)} custom-call(f32[400,256]{1,0:T(8,128)} %bitcast.13, s32[1,640]{1,0:T(1,128)} %src_ids.1, s32[1,640]{1,0:T(1,128)} %dst_ids.1, s32[1,640]{1,0:T(1,128)} %rel_ids.1, s32[1,1000]{1,0:T(1,128)} %bitcast.26), custom_call_target="tpu_custom_call" | custom-call | flops 4194304 | bytes 421280 | tf_op jit(solution)/shard_map/pallas_call | solution.py:22
  1.8 3.9 %collective-permute-start = (bf16[432,256]{1,0:T(8,128)(2,1)S(1)}, bf16[432,256]{1,0:T(8,128)(2,1)S(1)}, u32[]{:S(2)}, u32[]{:S(2)}) collective-permute-start(bf16[432,256]{1,0:T(8,128)(2,1)S(1)} %shard_map.145.own), channel_id=1, source_target_pairs={{0,256},{32,288},{64,320},{96,352},{128,384},{160,416},{192,448},{... | collective-permute-start | bytes 663560 | tf_op jit(solution)/shard_map/ppermute | solution.py:439
  5.7 0.0 copy-start.6
  5.7 0.0 copy-start.4
  5.8 0.0 copy-start.5
  5.8 0.6 copy-done.6
  6.4 0.0 copy-done.4
  6.4 0.0 copy-done.5
  6.4 1.1 %copy-done.2 = f32[512,400]{0,1:T(8,128)S(1)} copy-done((f32[512,400]{0,1:T(8,128)S(1)}, f32[512,400]{0,1:T(8,128)}, u32[]{:S(2)}) %copy-start.2) | copy-done | bytes 819224
  7.6 1.3 %shard_map.146 = (bf16[400,640]{1,0:T(8,128)(2,1)S(1)}, bf16[400,640]{1,0:T(8,128)(2,1)S(1)}, bf16[400,640]{1,0:T(8,128)(2,1)S(1)}, bf16[400,640]{1,0:T(8,128)(2...) custom-call(bf16[432,256]{1,0:T(8,128)(2,1)S(1)} %shard_map.145.own, ...), custom_call_target="tpu_custom_call" | custom-call | flops 1073741824 | bytes 1454080 | tf_op jit(solution)/shard_map/pallas_call | solution.py:22
  8.9 0.1 collective-permute-done.partner
  9.0 4.1 %shard_map.147 = (f32[400,512]{1,0:T(8,128)S(1)}, bf16[400,512]{1,0:T(8,128)(2,1)S(1)}) custom-call(bf16[432,256]{1,0:T(8,128)(2,1)S(1)} %shard_map.145.own, bf16[432,256]{1,0:T(8,128)(2,1)S(1)} %collective-permute-done.partner, bf16[400,512]{1,0:T(8,128)(2,1)S(1)} %get-tuple-element.28.hot, bf16[400,256]{1,0:T(8,128)(2,1)S(1)} %get-tuple-element.29.rel, ...), custom_call_target="tpu_custom_call" | custom-call | flops 2147483648 | bytes 3121152 | tf_op jit(solution)/shard_map/pallas_call | solution.py:22
  13.1 9.3 %collective-permute-start.1 = (bf16[400,512]{1,0:T(8,128)(2,1)S(1)}, bf16[400,512]{1,0:T(8,128)(2,1)S(1)}, u32[]{:S(2)}, u32[]{:S(2)}) collective-permute-start(bf16[400,512]{1,0:T(8,128)(2,1)S(1)} %get-tuple-element.36), channel_id=1, source_target_pairs={{0,1},{1,0},{2,3},{3,2},{4,5},{5,4},{6,7},{7,6},{8,9},{9,8},{10,11... | collective-permute-start | bytes 1228808 | tf_op jit(solution)/shard_map/ppermute | solution.py:439
  22.5 1.4 %collective-permute-done.1.got = bf16[400,512]{1,0:T(8,128)(2,1)S(1)} collective-permute-done((bf16[400,512]{1,0:T(8,128)(2,1)S(1)}, bf16[400,512]{1,0:T(8,128)(2,1)S(1)}, u32[]{:S(2)}, u32[]{:S(2)}) %collective-permute-start.1) | collective-permute-done | bytes 409632 | tf_op jit(solution)/shard_map/ppermute | solution.py:439
  23.8 0.2 shard_map.148
  24.0 11.7 %all_to_all.15.got = bf16[16,88,128]{2,1,0:T(8,128)(2,1)S(1)} all-to-all(bf16[16,88,128]{2,1,0:T(8,128)(2,1)S(1)} %shard_map.148), channel_id=1, replica_groups={{0,2,4,6,8,10,12,14,16,18,20,22,24,26,28,30},{32,34,36,38,40,42,44,46,4..., dimensions={0} | all-to-all | bytes 720896 | tf_op jit(solution)/shard_map/all_to_all | solution.py:443
  35.7 0.1 shard_map.149
  35.8 21.4 %all_to_all.16.got = bf16[16,40,128]{2,1,0:T(8,128)(2,1)S(1)} all-to-all(bf16[16,40,128]{2,1,0:T(8,128)(2,1)S(1)} %get-tuple-element.37), channel_id=1, replica_groups={{0,32,64,96,128,160,192,224,256,288,320,352,384,416,448,480},{2,34,66,9..., dimensions={0} | all-to-all | bytes 327680 | tf_op jit(solution)/shard_map/all_to_all | solution.py:443
  57.2 0.1 shard_map.150
  57.3 15.0 %all_to_all.17.mine = bf16[16,128,128]{2,1,0:T(8,128)(2,1)S(1)} all-to-all(bf16[16,128,128]{2,1,0:T(8,128)(2,1)S(1)} %shard_map.150), channel_id=1, replica_groups={{0,2,4,6,8,10,12,14,16,18,20,22,24,26,28,30},{32,34,36,38,40,42,44,46,4..., dimensions={0} | all-to-all | bytes 1048576 | tf_op jit(solution)/shard_map/all_to_all | solution.py:443
  72.3 7.8 %collective-permute-start.2 = (bf16[16,128,128]{2,1,0:T(8,128)(2,1)S(1)}, bf16[16,128,128]{2,1,0:T(8,128)(2,1)S(1)}, u32[]{:S(2)}, u32[]{:S(2)}) collective-permute-start(bf16[16,128,128]{2,1,0:T(8,128)(2,1)S(1)} %all_to_all.17.mine), channel_id=1, source_target_pairs={{0,1},{1,0},{2,3},{3,2},{4,5},{5,4},{6,7},{7,6},{8,9},{9,8},{10,11... | collective-permute-start | bytes 1572872 | tf_op jit(solution)/shard_map/ppermute | solution.py:439
  80.1 1.1 %shard_map.151 = (f32[400,256]{1,0:T(8,128)}, f32[1,256]{1,0:T(1,128)}, f32[400,256]{1,0:T(8,128)}, f32[1,256]{1,0:T(1,128)}, f32[4,400,128]{2,1,0:T(8,128)S(1)}) custom-call(bf16[16,128,128]{2,1,0:T(8,128)(2,1)S(1)} %all_to_all.17.mine, f32[8,512]{1,0:T(8,128)S(1)} %get-tuple-element.34.states, f32[400,256]{1,0:T(8,128)S(1)} %bitcast.14, ...), custom_call_target="tpu_custom_call" | custom-call | flops 4194304 | bytes 1359872 | tf_op jit(solution)/shard_map/pallas_call | solution.py:22
  81.1 0.4 collective-permute-done.2.other
  81.6 1.5 %shard_map.152 = (f32[400,256]{1,0:T(8,128)}, f32[1,256]{1,0:T(1,128)}, f32[400,256]{1,0:T(8,128)}, f32[1,256]{1,0:T(1,128)}, f32[400,512]{1,0:T(8,128)}, /*index=5*/f32[1,512]{1,0:T(1,128)}) custom-call(bf16[16,128,128]{2,1,0:T(8,128)(2,1)S(1)} %collective-permute-done.2.other, ...), custom_call_target="tpu_custom_call", output_to_operand_aliasing={{0}: (6, {}), {1}: (7, {}), {2}: (8, {}), {3}: (9, {})} | custom-call | flops 4194304 | bytes 3819520 | tf_op jit(solution)/shard_map/pallas_call | solution.py:22
  (7 shorter events, 0.0 us)
Async XLA Ops:
  0.6 5.1 %copy-start.1 = (f32[256,400]{0,1:T(8,128)S(1)}, f32[256,400]{0,1:T(8,128)}, u32[]{:S(2)}) copy-start(f32[256,400]{0,1:T(8,128)} %param.14) | copy-start | bytes 1228804
  1.8 7.3 %collective-permute-start = (bf16[432,256]{1,0:T(8,128)(2,1)S(1)}, bf16[432,256]{1,0:T(8,128)(2,1)S(1)}, u32[]{:S(2)}, u32[]{:S(2)}) collective-permute-start(bf16[432,256]{1,0:T(8,128)(2,1)S(1)} %shard_map.145.own), channel_id=1, source_target_pairs={{0,256},{32,288},{64,320},{96,352},{128,384},{160,416},{192,448},{... | collective-permute-start | bytes 663560 | tf_op jit(solution)/shard_map/ppermute | solution.py:439
  5.7 0.7 copy-start.6
  5.7 0.7 copy-start.4
  5.8 0.7 copy-start.5
  6.4 1.1 %copy-start.2 = (f32[512,400]{0,1:T(8,128)S(1)}, f32[512,400]{0,1:T(8,128)}, u32[]{:S(2)}) copy-start(f32[512,400]{0,1:T(8,128)} %param.12) | copy-start | bytes 2457604
  13.1 10.7 %collective-permute-start.1 = (bf16[400,512]{1,0:T(8,128)(2,1)S(1)}, bf16[400,512]{1,0:T(8,128)(2,1)S(1)}, u32[]{:S(2)}, u32[]{:S(2)}) collective-permute-start(bf16[400,512]{1,0:T(8,128)(2,1)S(1)} %get-tuple-element.36), channel_id=1, source_target_pairs={{0,1},{1,0},{2,3},{3,2},{4,5},{5,4},{6,7},{7,6},{8,9},{9,8},{10,11... | collective-permute-start | bytes 1228808 | tf_op jit(solution)/shard_map/ppermute | solution.py:439
  57.3 22.8 %copy-start = (f32[256,400]{0,1:T(8,128)S(1)}, f32[256,400]{0,1:T(8,128)}, u32[]{:S(2)}) copy-start(f32[256,400]{0,1:T(8,128)} %param.10) | copy-start | bytes 1228804
  72.3 9.3 %copy-start.3 = (f32[512,400]{0,1:T(8,128)S(1)}, f32[512,400]{0,1:T(8,128)}, u32[]{:S(2)}) copy-start(f32[512,400]{0,1:T(8,128)} %param.12) | copy-start | bytes 2457604
  72.3 9.3 %collective-permute-start.2 = (bf16[16,128,128]{2,1,0:T(8,128)(2,1)S(1)}, bf16[16,128,128]{2,1,0:T(8,128)(2,1)S(1)}, u32[]{:S(2)}, u32[]{:S(2)}) collective-permute-start(bf16[16,128,128]{2,1,0:T(8,128)(2,1)S(1)} %all_to_all.17.mine), channel_id=1, source_target_pairs={{0,1},{1,0},{2,3},{3,2},{4,5},{5,4},{6,7},{7,6},{8,9},{9,8},{10,11... | collective-permute-start | bytes 1572872 | tf_op jit(solution)/shard_map/ppermute | solution.py:439

commit v8 on v7

--- a/solution.py
+++ b/solution.py
@@ -61,7 +61,7 @@
     return plan, -(-row // 32) * 32
 
 
-def pack_kernel(block, src_ids, dst_ids, rel_ids, neg_ids, table, in_block, *scratch):
+def pack_kernel(block, src_ids, dst_ids, rel_ids, neg_ids, table, id_table, in_block, *scratch):
     held, sems, rows_f = scratch[:4], scratch[4], scratch[5]
     sources = (src_ids, dst_ids, rel_ids, neg_ids)
     copies = [pltpu.make_async_copy(block, in_block, sems.at[4])]
@@ -80,6 +80,7 @@
         for step, (at, size) in enumerate(pieces(length)):
             rows_f[row + step : row + step + 1, :size] = ids[:, at : at + size].astype(F32)
     table[width:, :] = rows_f[...].astype(BF16)
+    id_table[...] = rows_f[...].astype(BF16)
     copies[0].wait()
     table[:width, :] = in_block[...].astype(BF16)
 
@@ -137,6 +138,19 @@
     dst_out[...] = mm(hot_bf[...], one_hot(dst_at - rows, hot_rows)).astype(BF16)
 
 
+def far_kernel(negatives, ids, own, hot, rel, src_out, dst_out, rel_out, count_out):
+    width, hot_rows = hot.shape
+    rows = own.shape[1]
+    src_at, dst_at, rel_at, neg_at = unpack(ids, 0, src_out.shape[1], negatives)
+    ends = jnp.concatenate([src_at, dst_at], axis=1)
+    from_hot = mm(hot[...], one_hot(ends - rows, hot_rows))
+    edges = src_out.shape[1]
+    src_out[...] = from_hot[:, :edges].astype(BF16)
+    dst_out[...] = (mm(own[:width, :], one_hot(dst_at, rows)) + from_hot[:, edges:]).astype(BF16)
+    rel_out[...] = mm(rel[...], one_hot(rel_at, rel.shape[1])).astype(BF16)
+    count_out[...] = jnp.broadcast_to(counts(neg_at, rows), count_out.shape)
+
+
 def edge_grads(partner, src, rel, dst, query, count):
     query_f = query.astype(F32)
     positive = jnp.sum(query_f * dst, axis=0, keepdims=True)
@@ -152,10 +166,24 @@
 
 
 def grad_kernel(
-    negatives, own, partner, hot, rel, src, rel_rows, dst_hot, near_query, states, keep, send
+    negatives,
+    own,
+    partner,
+    far_ids,
+    far_src_hot,
+    far_dst_rows,
+    far_rel_rows,
+    far_count,
+    src,
+    rel_rows,
+    dst_hot,
+    near_query,
+    states,
+    keep,
+    send,
 ):
     width, edges = src.shape
-    rows, hot_rows = own.shape[1], hot.shape[1]
+    rows = own.shape[1]
     half = rows // 2
     side = lax.axis_index("bucket") // (lax.axis_size("bucket") // 2)
     own_table, partner_table = own[:width, :], partner[:width, :]
@@ -173,14 +201,12 @@
         near_query[...],
         states[4:5, :rows],
     )
-    far_src, far_dst, far_rel, far_neg = unpack(partner, width, edges, negatives)
-    ends = jnp.concatenate([far_src, far_dst], axis=1)
-    from_hot = mm(hot[...], one_hot(ends - rows, hot_rows))
-    src_rows = mm(partner_table, one_hot(far_src, rows)) + from_hot[:, :edges]
-    dst_rows = mm(own_table, one_hot(far_dst, rows)) + from_hot[:, edges:]
-    kind_rows = mm(rel[...], one_hot(far_rel, rel.shape[1]))
+    far_src, far_dst, far_rel, _ = unpack(far_ids, 0, edges, negatives)
+    src_rows = mm(partner_table, one_hot(far_src, rows)) + far_src_hot[...].astype(F32)
+    dst_rows = far_dst_rows[...].astype(F32)
+    kind_rows = far_rel_rows[...].astype(F32)
     query = (src_rows * kind_rows).astype(BF16)
-    count = counts(far_neg, rows)
+    count = far_count[:1, :]
     sig, far_src_grad, far_kind_grad, far_dst_grad = edge_grads(
         own_table, src_rows, kind_rows, dst_rows, query, count
     )
@@ -472,9 +498,9 @@
     negatives = negative_ids.shape[-1]
     ids = (source_ids, target_ids, relation_ids, negative_ids.reshape(1, -1))
     _, id_height = id_plan(edges, negatives)
-    (own,) = call(
+    own, id_table = call(
         pack_kernel,
-        [((width + id_height, rows), BF16)],
+        [((width + id_height, rows), BF16), ((id_height, rows), BF16)],
         [pltpu.with_memory_space_constraint(part, pltpu.HBM) for part in (block_t, *ids)],
         specs=[HBM] * 5,
         scratch=[pltpu.VMEM((width, rows), F32)]
@@ -482,6 +508,7 @@
         + [pltpu.SemaphoreType.DMA((5,)), pltpu.VMEM((id_height, rows), F32)],
     )
     partner = flipped(own, "bucket", lax.axis_size("bucket") // 2)
+    far_ids = flipped(id_table, "bucket", lax.axis_size("bucket") // 2)
     state_rows = [state.reshape(1, -1) for state in (block_state, hot_state, relation_state)]
     src, rel_rows, dst_hot, near_query, hot_bf, rel_bf, states = call(
         functools.partial(gather_kernel, negatives),
@@ -490,10 +517,16 @@
         (own, hot_t, rel_t, *state_rows),
         1 << 30,
     )
+    far = call(
+        functools.partial(far_kernel, negatives),
+        [((width, edges), BF16)] * 3 + [((8, rows), F32)],
+        (far_ids, own, hot_bf, rel_bf),
+        1 << 30,
+    )
     keep, send = call(
         functools.partial(grad_kernel, negatives),
         [((width, 2 * rows), F32), ((width, 2 * rows), BF16)],
-        (own, partner, hot_bf, rel_bf, src, rel_rows, dst_hot, near_query, states),
+        (own, partner, far_ids, *far, src, rel_rows, dst_hot, near_query, states),
         1 << 31,
     )
     both = edge_groups(0) + bucket_groups(1)

time: 83.5 us -> 84.3 us (level)
  starting transfers between devices: 21.1 us -> 22.4 us
    ppermute x3 -> x4, starting transfers between devices: 21.1 us -> 22.4 us  [flipped(): lax.ppermute(x, axis, [(i, i ^ bit) for i in range(lax.axis_size(axis))])]
    all_to_all x3, blocking collectives: 48.1 us -> 47.3 us  [exchanged(): lax.all_to_all(x, ('bucket', 'edge'), 0, 0, tiled=True, axis_index_groups...]
    pallas_call x8 -> x9, Pallas kernels: 9.38 us -> 9.8 us  [call(): pl.pallas_call(body, out_shape=[jax.ShapeDtypeStruct(shape, dtype) for sh...]
    ppermute x3 -> x4, waiting for transfers between devices: 1.93 us -> 1.8 us  [flipped(): lax.ppermute(x, axis, [(i, i ^ bit) for i in range(lax.axis_size(axis))])]
  transfers between devices with their start and end apart: 3 -> 4, of which waited for: 3 -> 2; matrix products, arithmetic and copies ran while one was open for 0% -> 0% of each run, Pallas kernels for 3% -> 4%
where the time goes in v8:
time: 84.3 us; the launch traced here: 83.9 us
  blocking collectives  47.3 us (56%)
  starting transfers between devices  22.4 us (27%)
  Pallas kernels  9.8 us (12%)
  local copies, waits for them, and re-layouts  1.84 us (2%)
  waiting for transfers between devices  1.8 us (2%)
    all_to_all x3, blocking collectives, exchanged(): lax.all_to_all(x, ('bucket', 'edge'), 0, 0, tiled=True, axis_index_groups...  47.3 us
    ppermute x4, starting transfers between devices, flipped(): lax.ppermute(x, axis, [(i, i ^ bit) for i in range(lax.axis_size(axis))])  22.4 us
    pallas_call x9, Pallas kernels, call(): pl.pallas_call(body, out_shape=[jax.ShapeDtypeStruct(shape, dtype) for sh...  9.8 us
    unnamed x14, local copies, waits for them, and re-layouts  1.84 us
    ppermute x4, waiting for transfers between devices, flipped(): lax.ppermute(x, axis, [(i, i ^ bit) for i in range(lax.axis_size(axis))])  1.8 us
  transfers between devices with their start and end apart: 4, of which 2 were waited for; matrix products, arithmetic and copies ran while one was open for 0% of the time, Pallas kernels for 4%

profile of v8, /device:TPU:1, one launch (start us, length us, event | category | flops | bytes accessed | tf_op | source)
XLA Modules:
  0.0 83.9 jit_solution(13747580310331362259)
XLA Ops:
  0.6 1.1 %shard_map.145 = (bf16[432,256]{1,0:T(8,128)(2,1)S(1)}, bf16[32,256]{1,0:T(8,128)(2,1)S(1)}) custom-call(f32[400,256]{1,0:T(8,128)} %bitcast.13, s32[1,640]{1,0:T(1,128)} %src_ids.1, s32[1,640]{1,0:T(1,128)} %dst_ids.1, s32[1,640]{1,0:T(1,128)} %rel_ids.1, s32[1,1000]{1,0:T(1,128)} %bitcast.26), custom_call_target="tpu_custom_call" | custom-call | flops 4194304 | bytes 421280 | tf_op jit(solution)/shard_map/pallas_call | solution.py:22
  1.8 3.9 %collective-permute-start = (bf16[432,256]{1,0:T(8,128)(2,1)S(1)}, bf16[432,256]{1,0:T(8,128)(2,1)S(1)}, u32[]{:S(2)}, u32[]{:S(2)}) collective-permute-start(bf16[432,256]{1,0:T(8,128)(2,1)S(1)} %get-tuple-element.34.own), channel_id=1, source_target_pairs={{0,256},{32,288},{64,320},{96,352},{128,384},{160,416},{192,448},{... | collective-permute-start | bytes 663560 | tf_op jit(solution)/shard_map/ppermute | solution.py:465
  5.7 1.9 %collective-permute-start.1 = (bf16[32,256]{1,0:T(8,128)(2,1)S(1)}, bf16[32,256]{1,0:T(8,128)(2,1)S(1)}, u32[]{:S(2)}, u32[]{:S(2)}) collective-permute-start(bf16[32,256]{1,0:T(8,128)(2,1)S(1)} %get-tuple-element.35), channel_id=1, source_target_pairs={{0,256},{32,288},{64,320},{96,352},{128,384},{160,416},{192,448},{... | collective-permute-start | bytes 49160 | tf_op jit(solution)/shard_map/ppermute | solution.py:465
  7.7 0.0 copy-start.4
  7.7 0.0 copy-start.5
  7.7 0.6 copy-done.6
  8.3 0.0 copy-done.4
  8.4 0.0 copy-done.5
  8.4 1.1 %copy-done.2 = f32[512,400]{0,1:T(8,128)S(1)} copy-done((f32[512,400]{0,1:T(8,128)S(1)}, f32[512,400]{0,1:T(8,128)}, u32[]{:S(2)}) %copy-start.2) | copy-done | bytes 819224
  9.5 1.3 %shard_map.146 = (bf16[400,640]{1,0:T(8,128)(2,1)S(1)}, bf16[400,640]{1,0:T(8,128)(2,1)S(1)}, bf16[400,640]{1,0:T(8,128)(2,1)S(1)}, bf16[400,640]{1,0:T(8,128)(2...) custom-call(bf16[432,256]{1,0:T(8,128)(2,1)S(1)} %get-tuple-element.34.own, ...), custom_call_target="tpu_custom_call" | custom-call | flops 1073741824 | bytes 1454080 | tf_op jit(solution)/shard_map/pallas_call | solution.py:22
  10.8 1.1 %shard_map.147 = (bf16[400,640]{1,0:T(8,128)(2,1)S(1)}, bf16[400,640]{1,0:T(8,128)(2,1)S(1)}, bf16[400,640]{1,0:T(8,128)(2,1)S(1)}, f32[8,256]{1,0:T(8,128)S(1)}) custom-call(bf16[32,256]{1,0:T(8,128)(2,1)S(1)} %collective-permute-done.1.ids.far_ids, bf16[432,256]{1,0:T(8,128)(2,1)S(1)} %get-tuple-element.34.own, ...), custom_call_target="tpu_custom_call" | custom-call | flops 1073741824 | bytes 851968 | tf_op jit(solution)/shard_map/pallas_call | solution.py:22
  12.0 3.4 %shard_map.148 = (f32[400,512]{1,0:T(8,128)S(1)}, bf16[400,512]{1,0:T(8,128)(2,1)S(1)}) custom-call(bf16[432,256]{1,0:T(8,128)(2,1)S(1)} %get-tuple-element.34.own, bf16[432,256]{1,0:T(8,128)(2,1)S(1)} %collective-permute-done.partner, bf16[32,256]{1,0:T(8,128)(2,1)S(1)} %collective-permute-done.1.ids.far_ids, ...), custom_call_target="tpu_custom_call" | custom-call | flops 2147483648 | bytes 4067328 | tf_op jit(solution)/shard_map/pallas_call | solution.py:22
  15.4 8.7 %collective-permute-start.2 = (bf16[400,512]{1,0:T(8,128)(2,1)S(1)}, bf16[400,512]{1,0:T(8,128)(2,1)S(1)}, u32[]{:S(2)}, u32[]{:S(2)}) collective-permute-start(bf16[400,512]{1,0:T(8,128)(2,1)S(1)} %get-tuple-element.48), channel_id=1, source_target_pairs={{0,1},{1,0},{2,3},{3,2},{4,5},{5,4},{6,7},{7,6},{8,9},{9,8},{10,11... | collective-permute-start | bytes 1228808 | tf_op jit(solution)/shard_map/ppermute | solution.py:465
  24.1 1.4 %collective-permute-done.2.got = bf16[400,512]{1,0:T(8,128)(2,1)S(1)} collective-permute-done((bf16[400,512]{1,0:T(8,128)(2,1)S(1)}, bf16[400,512]{1,0:T(8,128)(2,1)S(1)}, u32[]{:S(2)}, u32[]{:S(2)}) %collective-permute-start.2) | collective-permute-done | bytes 409632 | tf_op jit(solution)/shard_map/ppermute | solution.py:465
  25.5 0.2 shard_map.149
  25.6 10.9 %all_to_all.15.got = bf16[16,88,128]{2,1,0:T(8,128)(2,1)S(1)} all-to-all(bf16[16,88,128]{2,1,0:T(8,128)(2,1)S(1)} %shard_map.149), channel_id=1, replica_groups={{0,2,4,6,8,10,12,14,16,18,20,22,24,26,28,30},{32,34,36,38,40,42,44,46,4..., dimensions={0} | all-to-all | bytes 720896 | tf_op jit(solution)/shard_map/all_to_all | solution.py:469
  36.5 0.1 shard_map.150
  36.6 21.4 %all_to_all.16.got = bf16[16,40,128]{2,1,0:T(8,128)(2,1)S(1)} all-to-all(bf16[16,40,128]{2,1,0:T(8,128)(2,1)S(1)} %get-tuple-element.49), channel_id=1, replica_groups={{0,32,64,96,128,160,192,224,256,288,320,352,384,416,448,480},{2,34,66,9..., dimensions={0} | all-to-all | bytes 327680 | tf_op jit(solution)/shard_map/all_to_all | solution.py:469
  58.0 0.1 shard_map.151
  58.1 15.0 %all_to_all.17.mine = bf16[16,128,128]{2,1,0:T(8,128)(2,1)S(1)} all-to-all(bf16[16,128,128]{2,1,0:T(8,128)(2,1)S(1)} %shard_map.151), channel_id=1, replica_groups={{0,2,4,6,8,10,12,14,16,18,20,22,24,26,28,30},{32,34,36,38,40,42,44,46,4..., dimensions={0} | all-to-all | bytes 1048576 | tf_op jit(solution)/shard_map/all_to_all | solution.py:469
  73.1 7.8 %collective-permute-start.3 = (bf16[16,128,128]{2,1,0:T(8,128)(2,1)S(1)}, bf16[16,128,128]{2,1,0:T(8,128)(2,1)S(1)}, u32[]{:S(2)}, u32[]{:S(2)}) collective-permute-start(bf16[16,128,128]{2,1,0:T(8,128)(2,1)S(1)} %all_to_all.17.mine), channel_id=1, source_target_pairs={{0,1},{1,0},{2,3},{3,2},{4,5},{5,4},{6,7},{7,6},{8,9},{9,8},{10,11... | collective-permute-start | bytes 1572872 | tf_op jit(solution)/shard_map/ppermute | solution.py:465
  80.8 1.1 %shard_map.152 = (f32[400,256]{1,0:T(8,128)}, f32[1,256]{1,0:T(1,128)}, f32[400,256]{1,0:T(8,128)}, f32[1,256]{1,0:T(1,128)}, f32[4,400,128]{2,1,0:T(8,128)S(1)}) custom-call(bf16[16,128,128]{2,1,0:T(8,128)(2,1)S(1)} %all_to_all.17.mine, f32[8,512]{1,0:T(8,128)S(1)} %get-tuple-element.46.states, f32[400,256]{1,0:T(8,128)S(1)} %bitcast.14, ...), custom_call_target="tpu_custom_call" | custom-call | flops 4194304 | bytes 1359872 | tf_op jit(solution)/shard_map/pallas_call | solution.py:22
  81.9 0.4 collective-permute-done.3.other
  82.4 1.5 %shard_map.153 = (f32[400,256]{1,0:T(8,128)}, f32[1,256]{1,0:T(1,128)}, f32[400,256]{1,0:T(8,128)}, f32[1,256]{1,0:T(1,128)}, f32[400,512]{1,0:T(8,128)}, /*index=5*/f32[1,512]{1,0:T(1,128)}) custom-call(bf16[16,128,128]{2,1,0:T(8,128)(2,1)S(1)} %collective-permute-done.3.other, ...), custom_call_target="tpu_custom_call", output_to_operand_aliasing={{0}: (6, {}), {1}: (7, {}), {2}: (8, {}), {3}: (9, {})} | custom-call | flops 4194304 | bytes 3819520 | tf_op jit(solution)/shard_map/pallas_call | solution.py:22
  (10 shorter events, 0.0 us)
Async XLA Ops:
  0.6 7.1 %copy-start.1 = (f32[256,400]{0,1:T(8,128)S(1)}, f32[256,400]{0,1:T(8,128)}, u32[]{:S(2)}) copy-start(f32[256,400]{0,1:T(8,128)} %param.14) | copy-start | bytes 1228804
  1.8 10.2 %collective-permute-start = (bf16[432,256]{1,0:T(8,128)(2,1)S(1)}, bf16[432,256]{1,0:T(8,128)(2,1)S(1)}, u32[]{:S(2)}, u32[]{:S(2)}) collective-permute-start(bf16[432,256]{1,0:T(8,128)(2,1)S(1)} %get-tuple-element.34.own), channel_id=1, source_target_pairs={{0,256},{32,288},{64,320},{96,352},{128,384},{160,416},{192,448},{... | collective-permute-start | bytes 663560 | tf_op jit(solution)/shard_map/ppermute | solution.py:465
  5.7 5.1 %collective-permute-start.1 = (bf16[32,256]{1,0:T(8,128)(2,1)S(1)}, bf16[32,256]{1,0:T(8,128)(2,1)S(1)}, u32[]{:S(2)}, u32[]{:S(2)}) collective-permute-start(bf16[32,256]{1,0:T(8,128)(2,1)S(1)} %get-tuple-element.35), channel_id=1, source_target_pairs={{0,256},{32,288},{64,320},{96,352},{128,384},{160,416},{192,448},{... | collective-permute-start | bytes 49160 | tf_op jit(solution)/shard_map/ppermute | solution.py:465
  7.7 0.7 copy-start.6
  7.7 0.7 copy-start.4
  7.7 0.7 copy-start.5
  8.4 1.1 %copy-start.2 = (f32[512,400]{0,1:T(8,128)S(1)}, f32[512,400]{0,1:T(8,128)}, u32[]{:S(2)}) copy-start(f32[512,400]{0,1:T(8,128)} %param.12) | copy-start | bytes 2457604
  15.4 10.1 %collective-permute-start.2 = (bf16[400,512]{1,0:T(8,128)(2,1)S(1)}, bf16[400,512]{1,0:T(8,128)(2,1)S(1)}, u32[]{:S(2)}, u32[]{:S(2)}) collective-permute-start(bf16[400,512]{1,0:T(8,128)(2,1)S(1)} %get-tuple-element.48), channel_id=1, source_target_pairs={{0,1},{1,0},{2,3},{3,2},{4,5},{5,4},{6,7},{7,6},{8,9},{9,8},{10,11... | collective-permute-start | bytes 1228808 | tf_op jit(solution)/shard_map/ppermute | solution.py:465
  58.0 22.8 %copy-start = (f32[256,400]{0,1:T(8,128)S(1)}, f32[256,400]{0,1:T(8,128)}, u32[]{:S(2)}) copy-start(f32[256,400]{0,1:T(8,128)} %param.10) | copy-start | bytes 1228804
  73.0 9.3 %copy-start.3 = (f32[512,400]{0,1:T(8,128)S(1)}, f32[512,400]{0,1:T(8,128)}, u32[]{:S(2)}) copy-start(f32[512,400]{0,1:T(8,128)} %param.12) | copy-start | bytes 2457604
  73.1 9.3 %collective-permute-start.3 = (bf16[16,128,128]{2,1,0:T(8,128)(2,1)S(1)}, bf16[16,128,128]{2,1,0:T(8,128)(2,1)S(1)}, u32[]{:S(2)}, u32[]{:S(2)}) collective-permute-start(bf16[16,128,128]{2,1,0:T(8,128)(2,1)S(1)} %all_to_all.17.mine), channel_id=1, source_target_pairs={{0,1},{1,0},{2,3},{3,2},{4,5},{5,4},{6,7},{7,6},{8,9},{9,8},{10,11... | collective-permute-start | bytes 1572872 | tf_op jit(solution)/shard_map/ppermute | solution.py:465

commit v9 on v7

--- a/solution.py
+++ b/solution.py
@@ -194,21 +194,24 @@
     kind_at = jnp.concatenate([near_rel, far_rel], axis=1)
     kind_sum = mm_t(kind_grad, one_hot(kind_at - side * half, half))
 
+    split = PEERS * cuts(width)[1]
+
     @pl.when(core_of() == 0)
     def _():
         keep[:, :rows] = block_sum
         keep[:, rows:] = hot_sum
-        send[:, :half] = kind_sum.astype(BF16)
-        send[:, half:rows] = jnp.zeros((width, half), BF16)
-        send[:, rows:] = hot_sum.astype(BF16)
+        send[:width, :half] = kind_sum.astype(BF16)
+        send[:width, half:] = jnp.zeros((width, half), BF16)
+        send[width : 2 * width - split, :] = hot_sum[split:, :].astype(BF16)
+        send[2 * width - split :, :] = jnp.zeros((2 * split - width, rows), BF16)
 
     @pl.when(core_of() == 1)
     def _():
         keep[:, :half] = kind_sum
         keep[:, half:rows] = jnp.zeros((width, half), F32)
         keep[:, rows:] = hot_sum
-        send[:, :rows] = block_sum.astype(BF16)
-        send[:, rows:] = hot_sum.astype(BF16)
+        send[:width, :] = block_sum.astype(BF16)
+        send[width:, :] = hot_sum[:split, :].astype(BF16)
 
 
 SIDES = (range(PEERS // 2), range(PEERS // 2, PEERS))
@@ -244,15 +247,18 @@
         if end < packed.shape[1]:
             packed[:, end:, :] = jnp.zeros((PEERS, packed.shape[1] - end, LANES), F32)
 
-    for block in range(2):
-        at = slice(hot.start + block * LANES, hot.start + (block + 1) * LANES)
-        put(2 + block, keep[:, at] + got[:, at].astype(F32))
+    def put_hot(low, high):
+        for block in range(2):
+            at = slice(hot.start + block * LANES, hot.start + (block + 1) * LANES)
+            came = got[width : width + high - low, block * LANES : (block + 1) * LANES]
+            sums[2 + block, low:high, :] = keep[low:high, at] + came.astype(F32)
 
     @pl.when(core_of() == 0)
     def _():
+        put_hot(0, split)
         for block in range(2):
             at = slice(block * LANES, (block + 1) * LANES)
-            put(block, keep[:, at] + got[:, at].astype(F32))
+            put(block, keep[:, at] + got[:width, at].astype(F32))
             for peer in range(PEERS):
                 low = 2 * whole + block * near
                 packed[peer, low : low + near, :] = sums[2 + block, peer * near : (peer + 1) * near, :]
@@ -260,7 +266,8 @@
 
     @pl.when(core_of() == 1)
     def _():
-        put(0, got[:, :LANES].astype(F32))
+        put_hot(split, width)
+        put(0, got[:width, :LANES].astype(F32))
         put(1, keep[:, :LANES])
         for block in range(2):
             for peer in range(PEERS):
@@ -492,7 +499,7 @@
     )
     keep, send = call(
         functools.partial(grad_kernel, negatives),
-        [((width, 2 * rows), F32), ((width, 2 * rows), BF16)],
+        [((width, 2 * rows), F32), ((width + PEERS * cuts(width)[1], rows), BF16)],
         (own, partner, hot_bf, rel_bf, src, rel_rows, dst_hot, near_query, states),
         1 << 31,
     )

time: 83.5 us -> 83.4 us (level)
  no operation moved by 1% of the time
where the time goes in v9:
time: 83.4 us; the launch traced here: 83 us
  blocking collectives  48.1 us (58%)
  starting transfers between devices  21.1 us (25%)
  Pallas kernels  9.35 us (11%)
  waiting for transfers between devices  1.86 us (2%)
  local copies, waits for them, and re-layouts  1.84 us (2%)
    all_to_all x3, blocking collectives, exchanged(): lax.all_to_all(x, ('bucket', 'edge'), 0, 0, tiled=True, axis_index_groups...  48.1 us
    ppermute x3, starting transfers between devices, flipped(): lax.ppermute(x, axis, [(i, i ^ bit) for i in range(lax.axis_size(axis))])  21.1 us
    pallas_call x8, Pallas kernels, call(): pl.pallas_call(body, out_shape=[jax.ShapeDtypeStruct(shape, dtype) for sh...  9.35 us
    ppermute x3, waiting for transfers between devices, flipped(): lax.ppermute(x, axis, [(i, i ^ bit) for i in range(lax.axis_size(axis))])  1.86 us
    unnamed x14, local copies, waits for them, and re-layouts  1.84 us
  transfers between devices with their start and end apart: 3, of which 3 were waited for; matrix products, arithmetic and copies ran while one was open for 0% of the time, Pallas kernels for 3%

profile of v9, /device:TPU:1, one launch (start us, length us, event | category | flops | bytes accessed | tf_op | source)
XLA Modules:
  0.0 83.0 jit_solution(17768197863733874512)
XLA Ops:
  0.6 1.1 %shard_map.145.own = bf16[432,256]{1,0:T(8,128)(2,1)S(1)} custom-call(f32[400,256]{1,0:T(8,128)} %bitcast.13, s32[1,640]{1,0:T(1,128)} %src_ids.1, s32[1,640]{1,0:T(1,128)} %dst_ids.1, s32[1,640]{1,0:T(1,128)} %rel_ids.1, s32[1,1000]{1,0:T(1,128)} %bitcast.26), custom_call_target="tpu_custom_call" | custom-call | flops 4194304 | bytes 421280 | tf_op jit(solution)/shard_map/pallas_call | solution.py:22
  1.8 3.9 %collective-permute-start = (bf16[432,256]{1,0:T(8,128)(2,1)S(1)}, bf16[432,256]{1,0:T(8,128)(2,1)S(1)}, u32[]{:S(2)}, u32[]{:S(2)}) collective-permute-start(bf16[432,256]{1,0:T(8,128)(2,1)S(1)} %shard_map.145.own), channel_id=1, source_target_pairs={{0,256},{32,288},{64,320},{96,352},{128,384},{160,416},{192,448},{... | collective-permute-start | bytes 663560 | tf_op jit(solution)/shard_map/ppermute | solution.py:446
  5.7 0.0 copy-start.4
  5.8 0.0 copy-start.5
  5.8 0.6 copy-done.6
  6.4 0.0 copy-done.4
  6.4 0.0 copy-done.5
  6.4 1.1 %copy-done.2 = f32[512,400]{0,1:T(8,128)S(1)} copy-done((f32[512,400]{0,1:T(8,128)S(1)}, f32[512,400]{0,1:T(8,128)}, u32[]{:S(2)}) %copy-start.2) | copy-done | bytes 819224
  7.6 1.3 %shard_map.146 = (bf16[400,640]{1,0:T(8,128)(2,1)S(1)}, bf16[400,640]{1,0:T(8,128)(2,1)S(1)}, bf16[400,640]{1,0:T(8,128)(2,1)S(1)}, bf16[400,640]{1,0:T(8,128)(2...) custom-call(bf16[432,256]{1,0:T(8,128)(2,1)S(1)} %shard_map.145.own, ...), custom_call_target="tpu_custom_call" | custom-call | flops 1073741824 | bytes 1454080 | tf_op jit(solution)/shard_map/pallas_call | solution.py:22
  8.9 0.1 collective-permute-done.partner
  9.0 4.1 %shard_map.147 = (f32[400,512]{1,0:T(8,128)S(1)}, bf16[704,256]{1,0:T(8,128)(2,1)S(1)}) custom-call(bf16[432,256]{1,0:T(8,128)(2,1)S(1)} %shard_map.145.own, bf16[432,256]{1,0:T(8,128)(2,1)S(1)} %collective-permute-done.partner, bf16[400,512]{1,0:T(8,128)(2,1)S(1)} %get-tuple-element.28.hot, bf16[400,256]{1,0:T(8,128)(2,1)S(1)} %get-tuple-element.29.rel, ...), custom_call_target="tpu_custom_call" | custom-call | flops 2147483648 | bytes 3121152 | tf_op jit(solution)/shard_map/pallas_call | solution.py:22
  13.1 9.3 %collective-permute-start.1 = (bf16[704,256]{1,0:T(8,128)(2,1)S(1)}, bf16[704,256]{1,0:T(8,128)(2,1)S(1)}, u32[]{:S(2)}, u32[]{:S(2)}) collective-permute-start(bf16[704,256]{1,0:T(8,128)(2,1)S(1)} %get-tuple-element.36), channel_id=1, source_target_pairs={{0,1},{1,0},{2,3},{3,2},{4,5},{5,4},{6,7},{7,6},{8,9},{9,8},{10,11... | collective-permute-start | bytes 1081352 | tf_op jit(solution)/shard_map/ppermute | solution.py:446
  22.4 1.3 %collective-permute-done.1.got = bf16[704,256]{1,0:T(8,128)(2,1)S(1)} collective-permute-done((bf16[704,256]{1,0:T(8,128)(2,1)S(1)}, bf16[704,256]{1,0:T(8,128)(2,1)S(1)}, u32[]{:S(2)}, u32[]{:S(2)}) %collective-permute-start.1) | collective-permute-done | bytes 360480 | tf_op jit(solution)/shard_map/ppermute | solution.py:446
  23.7 0.1 shard_map.148
  23.8 11.8 %all_to_all.15.got = bf16[16,88,128]{2,1,0:T(8,128)(2,1)S(1)} all-to-all(bf16[16,88,128]{2,1,0:T(8,128)(2,1)S(1)} %shard_map.148), channel_id=1, replica_groups={{0,2,4,6,8,10,12,14,16,18,20,22,24,26,28,30},{32,34,36,38,40,42,44,46,4..., dimensions={0} | all-to-all | bytes 720896 | tf_op jit(solution)/shard_map/all_to_all | solution.py:450
  35.6 0.1 shard_map.149
  35.7 21.4 %all_to_all.16.got = bf16[16,40,128]{2,1,0:T(8,128)(2,1)S(1)} all-to-all(bf16[16,40,128]{2,1,0:T(8,128)(2,1)S(1)} %get-tuple-element.37), channel_id=1, replica_groups={{0,32,64,96,128,160,192,224,256,288,320,352,384,416,448,480},{2,34,66,9..., dimensions={0} | all-to-all | bytes 327680 | tf_op jit(solution)/shard_map/all_to_all | solution.py:450
  57.0 0.1 shard_map.150
  57.1 0.0 copy-start
  57.1 14.9 %all_to_all.17.mine = bf16[16,128,128]{2,1,0:T(8,128)(2,1)S(1)} all-to-all(bf16[16,128,128]{2,1,0:T(8,128)(2,1)S(1)} %shard_map.150), channel_id=1, replica_groups={{0,2,4,6,8,10,12,14,16,18,20,22,24,26,28,30},{32,34,36,38,40,42,44,46,4..., dimensions={0} | all-to-all | bytes 1048576 | tf_op jit(solution)/shard_map/all_to_all | solution.py:450
  72.1 7.9 %collective-permute-start.2 = (bf16[16,128,128]{2,1,0:T(8,128)(2,1)S(1)}, bf16[16,128,128]{2,1,0:T(8,128)(2,1)S(1)}, u32[]{:S(2)}, u32[]{:S(2)}) collective-permute-start(bf16[16,128,128]{2,1,0:T(8,128)(2,1)S(1)} %all_to_all.17.mine), channel_id=1, source_target_pairs={{0,1},{1,0},{2,3},{3,2},{4,5},{5,4},{6,7},{7,6},{8,9},{9,8},{10,11... | collective-permute-start | bytes 1572872 | tf_op jit(solution)/shard_map/ppermute | solution.py:446
  80.0 1.1 %shard_map.151 = (f32[400,256]{1,0:T(8,128)}, f32[1,256]{1,0:T(1,128)}, f32[400,256]{1,0:T(8,128)}, f32[1,256]{1,0:T(1,128)}, f32[4,400,128]{2,1,0:T(8,128)S(1)}) custom-call(bf16[16,128,128]{2,1,0:T(8,128)(2,1)S(1)} %all_to_all.17.mine, f32[8,512]{1,0:T(8,128)S(1)} %get-tuple-element.34.states, f32[400,256]{1,0:T(8,128)S(1)} %bitcast.14, ...), custom_call_target="tpu_custom_call" | custom-call | flops 4194304 | bytes 1359872 | tf_op jit(solution)/shard_map/pallas_call | solution.py:22
  81.0 0.4 collective-permute-done.2.other
  81.5 1.5 %shard_map.152 = (f32[400,256]{1,0:T(8,128)}, f32[1,256]{1,0:T(1,128)}, f32[400,256]{1,0:T(8,128)}, f32[1,256]{1,0:T(1,128)}, f32[400,512]{1,0:T(8,128)}, /*index=5*/f32[1,512]{1,0:T(1,128)}) custom-call(bf16[16,128,128]{2,1,0:T(8,128)(2,1)S(1)} %collective-permute-done.2.other, ...), custom_call_target="tpu_custom_call", output_to_operand_aliasing={{0}: (6, {}), {1}: (7, {}), {2}: (8, {}), {3}: (9, {})} | custom-call | flops 4194304 | bytes 3819520 | tf_op jit(solution)/shard_map/pallas_call | solution.py:22
  (7 shorter events, 0.0 us)
Async XLA Ops:
  0.6 5.1 %copy-start.1 = (f32[256,400]{0,1:T(8,128)S(1)}, f32[256,400]{0,1:T(8,128)}, u32[]{:S(2)}) copy-start(f32[256,400]{0,1:T(8,128)} %param.14) | copy-start | bytes 1228804
  1.8 7.3 %collective-permute-start = (bf16[432,256]{1,0:T(8,128)(2,1)S(1)}, bf16[432,256]{1,0:T(8,128)(2,1)S(1)}, u32[]{:S(2)}, u32[]{:S(2)}) collective-permute-start(bf16[432,256]{1,0:T(8,128)(2,1)S(1)} %shard_map.145.own), channel_id=1, source_target_pairs={{0,256},{32,288},{64,320},{96,352},{128,384},{160,416},{192,448},{... | collective-permute-start | bytes 663560 | tf_op jit(solution)/shard_map/ppermute | solution.py:446
  5.7 0.7 copy-start.6
  5.7 0.7 copy-start.4
  5.8 0.7 copy-start.5
  6.4 1.1 %copy-start.2 = (f32[512,400]{0,1:T(8,128)S(1)}, f32[512,400]{0,1:T(8,128)}, u32[]{:S(2)}) copy-start(f32[512,400]{0,1:T(8,128)} %param.12) | copy-start | bytes 2457604
  13.1 10.6 %collective-permute-start.1 = (bf16[704,256]{1,0:T(8,128)(2,1)S(1)}, bf16[704,256]{1,0:T(8,128)(2,1)S(1)}, u32[]{:S(2)}, u32[]{:S(2)}) collective-permute-start(bf16[704,256]{1,0:T(8,128)(2,1)S(1)} %get-tuple-element.36), channel_id=1, source_target_pairs={{0,1},{1,0},{2,3},{3,2},{4,5},{5,4},{6,7},{7,6},{8,9},{9,8},{10,11... | collective-permute-start | bytes 1081352 | tf_op jit(solution)/shard_map/ppermute | solution.py:446
  57.1 22.8 %copy-start = (f32[256,400]{0,1:T(8,128)S(1)}, f32[256,400]{0,1:T(8,128)}, u32[]{:S(2)}) copy-start(f32[256,400]{0,1:T(8,128)} %param.10) | copy-start | bytes 1228804
  72.1 9.4 %copy-start.3 = (f32[512,400]{0,1:T(8,128)S(1)}, f32[512,400]{0,1:T(8,128)}, u32[]{:S(2)}) copy-start(f32[512,400]{0,1:T(8,128)} %param.12) | copy-start | bytes 2457604
  72.1 9.4 %collective-permute-start.2 = (bf16[16,128,128]{2,1,0:T(8,128)(2,1)S(1)}, bf16[16,128,128]{2,1,0:T(8,128)(2,1)S(1)}, u32[]{:S(2)}, u32[]{:S(2)}) collective-permute-start(bf16[16,128,128]{2,1,0:T(8,128)(2,1)S(1)} %all_to_all.17.mine), channel_id=1, source_target_pairs={{0,1},{1,0},{2,3},{3,2},{4,5},{5,4},{6,7},{7,6},{8,9},{9,8},{10,11... | collective-permute-start | bytes 1572872 | tf_op jit(solution)/shard_map/ppermute | solution.py:446
